TPU v7x, 32 devices: a whole 2x2x4 slice. The times are simulated.
32 devices in a mesh: seq: 8 (over y, x, core), tp: 4 (over z).
Axes of the slice: x: 2, y: 2, z: 4, core: 2. Of those that a mesh axis runs over, the one named last changes fastest.
Arguments:
- tokens: bfloat16 [8192, 2048], P('seq'), may hold values from -6 to 6
- doc_start: int32 [8192], P('seq'), may hold values from 0 to 1, as said below
- norm_first: bfloat16 [2048], replicated, may hold values from 0.099609375 to 1.8984375
- in_weight: bfloat16 [2048, 3, 2048], P('seq', None, 'tp'), may hold values from -0.125 to 0.125
- conv_weight: bfloat16 [3, 2048], P(None, 'tp'), may hold values from -3.5 to 3.5
- out_weight: bfloat16 [2048, 2048], P('tp', 'seq'), may hold values from -0.125 to 0.125
- norm_second: bfloat16 [2048], replicated, may hold values from 0.099609375 to 1.8984375
- gate_weight: bfloat16 [2048, 8192], P('seq', 'tp'), may hold values from -0.125 to 0.125
- up_weight: bfloat16 [2048, 8192], P('seq', 'tp'), may hold values from -0.125 to 0.125
- down_weight: bfloat16 [8192, 2048], P('tp', 'seq'), may hold values from -0.125 to 0.125
- out_grad: bfloat16 [8192, 2048], P('seq'), may hold values from -6 to 6
Outputs:
- block_out: bfloat16 [8192, 2048], P('seq')
- tokens_grad: float32 [8192, 2048], P('seq')
- in_grad: float32 [2048, 3, 2048], P('seq', None, 'tp')
- conv_grad: float32 [3, 2048], P(None, 'tp')
- out_proj_grad: float32 [2048, 2048], P('tp', 'seq')
- gate_grad: float32 [2048, 8192], P('seq', 'tp')
- up_grad: float32 [2048, 8192], P('seq', 'tp')
- down_grad: float32 [8192, 2048], P('tp', 'seq')
- norm_first_grad: float32 [2048], replicated
- norm_second_grad: float32 [2048], replicated
Inputs may be any that keep to these rules, and one draw needn't show every extreme that they name: doc_start is 1 at row 0 and wherever a document begins.
All inputs are finite; a program needn't handle non-finite values.
Results may differ from a plain program's by a relative error of at most 0.012.
The roundings to bfloat16 on the way count: a program that leaves them out, or rounds other values in their place, can miss the bound.
Values may be sent and summed in bfloat16 or wider, within the bound.
No kernel may reach another device: no remote copies, remote signals or barrier semaphores. Data moves between devices by JAX's collectives and lax.ppermute only.
A program may use at most 256 MiB of HBM per device.

v0:
```python
import functools

import jax
import jax.numpy as jnp
from jax import lax
from jax.experimental import pallas as pl
from jax.experimental.pallas import tpu as pltpu
from jax.sharding import PartitionSpec as P

epsilon = 1e-05
bf16 = jnp.bfloat16
f32 = jnp.float32
halo = 16
chunks = 4


def dot_plain(left, right):
    return lax.dot_general(left, right, (((1,), (0,)), ((), ())), preferred_element_type=f32)


def dot_right(left, right):
    return lax.dot_general(left, right, (((1,), (1,)), ((), ())), preferred_element_type=f32)


def dot_left(left, right):
    return lax.dot_general(left, right, (((0,), (0,)), ((), ())), preferred_element_type=f32)


def rms_scale(value):
    return lax.rsqrt(jnp.mean(value * value, axis=1, keepdims=True) + epsilon)


def norm_back(grad_normed, scaled, inverse, gain):
    weighted = grad_normed * gain
    return inverse * (weighted - scaled * jnp.mean(weighted * scaled, axis=1, keepdims=True))


def from_before(block, axis):
    devices = lax.axis_size(axis)
    return lax.ppermute(block, axis, [(i, i + 1) for i in range(devices - 1)])


def from_after(block, axis):
    devices = lax.axis_size(axis)
    return lax.ppermute(block, axis, [(i + 1, i) for i in range(devices - 1)])


def bits_of(axis):
    devices = lax.axis_size(axis)
    return [1 << i for i in range(devices.bit_length() - 1)]


def paired(value, axis, bit):
    return lax.ppermute(value, axis, [(i, i ^ bit) for i in range(lax.axis_size(axis))])


def place_kernel(moves, here_ref, *refs):
    pieces, out, sems = refs[:-2], refs[-2], refs[-1]
    here = here_ref[0]
    copies = []
    for number, (piece, first, size, mask, offset, dim) in enumerate(moves):
        target = pl.ds(pl.multiple_of((here ^ mask) * size, size), size)
        other = pl.ds(offset, pieces[piece].shape[1 - dim])
        if dim == 0:
            source, place = pieces[piece].at[pl.ds(first, size), :], out.at[target, other]
        else:
            source, place = pieces[piece].at[:, pl.ds(first, size)], out.at[other, target]
        copies.append(pltpu.make_async_copy(source, place, sems.at[number]))
    for copy in copies:
        copy.start()
    for copy in copies:
        copy.wait()


def placed(pieces, shape, size, dim, here):
    moves = []
    for number, (_, masks, offset) in enumerate(pieces):
        moves += [(number, size * i, size, mask, offset, dim) for i, mask in enumerate(masks)]
    anywhere = pl.BlockSpec(memory_space=pl.ANY)
    return pl.pallas_call(
        functools.partial(place_kernel, moves),
        in_specs=[pl.BlockSpec(memory_space=pltpu.SMEM)] + [anywhere] * len(pieces),
        out_specs=pl.BlockSpec(memory_space=pltpu.VMEM),
        out_shape=jax.ShapeDtypeStruct(shape, bf16),
        scratch_shapes=[pltpu.SemaphoreType.DMA((len(moves),))],
        compiler_params=pltpu.CompilerParams(vmem_limit_bytes=2 * 2**20),
        cost_estimate=pl.CostEstimate(
            flops=0, bytes_accessed=4 * shape[0] * shape[1], transcendentals=0
        ),
    )(here.reshape(1), *[piece for piece, _, _ in pieces])


class Gather:
    def __init__(self, shards, axis):
        self.shards, self.axis = shards, axis
        self.devices = lax.axis_size(axis)
        self.outer = [1 << i for i in range(1, self.devices.bit_length() - 1)]
        self.plain = self.devices & (self.devices - 1) or len(self.outer) < 2
        self.turns = 0 if self.plain else len(self.outer) + 1
        self.turn, self.held, self.pieces, self.fresh = 0, {}, {}, []
        for number, (block, dim) in enumerate(shards):
            middle = block.shape[1 - dim] // 2
            for side in range(2):
                half = lax.slice_in_dim(block, side * middle, (side + 1) * middle, axis=1 - dim)
                self.held[number, side] = [(half, [0])]
            self.pieces[number] = [(block, [0], 0)]
            self.fresh.append((number, block, [0], 0))

    def sends(self):
        values = []
        self.bits, self.notes = [], []
        if self.turn < len(self.outer):
            for (number, side), parts in self.held.items():
                block, dim = self.shards[number]
                bit = (self.outer, self.outer[::-1])[side][self.turn]
                masks = [m ^ bit for _, ms in parts for m in ms]
                blocks = [part for part, _ in parts]
                values.append(jnp.concatenate(blocks, axis=dim) if self.turn else blocks[0])
                self.bits.append(bit)
                self.notes.append((number, side, masks, side * (block.shape[1 - dim] // 2)))
        for number, value, masks, offset in self.fresh:
            values.append(value)
            self.bits.append(1)
            self.notes.append((number, None, [m ^ 1 for m in masks], offset))
        return values

    def swap(self, values):
        got = []
        for value, bit in zip(values, self.bits):
            pairs = [(i, i ^ bit) for i in range(self.devices)]
            got.append(lax.ppermute(value, self.axis, pairs))
        return got

    def take(self, got):
        self.turn += 1
        self.fresh = []
        for value, (number, side, masks, offset) in zip(got, self.notes):
            self.pieces[number].append((value, masks, offset))
            if side is not None:
                self.held[number, side].append((value, masks))
                self.fresh.append((number, value, masks, offset))

    def whole(self):
        if self.plain:
            return [lax.all_gather(b, self.axis, axis=d, tiled=True) for b, d in self.shards]
        here = lax.axis_index(self.axis)
        results = []
        for number, (block, dim) in enumerate(self.shards):
            shape = list(block.shape)
            shape[dim] *= self.devices
            results.append(placed(self.pieces[number], shape, block.shape[dim], dim, here))
        return results


def together(gathers, run=None):
    live = [gather for gather in gathers if gather.turn < gather.turns]
    sends = lax.optimization_barrier([gather.sends() for gather in live])
    got = [gather.swap(values) for gather, values in zip(live, sends)]
    extra = run() if run else ()
    got, extra = lax.optimization_barrier((got, extra))
    for gather, values in zip(live, got):
        gather.take(values)
    return extra


def feed_kernel(
    normed, grads, weights, act, grad_both, out, grad_normed, out_sum, grad_sum
):
    tile = pl.program_id(0)
    size = weights.shape[3]
    gate_w, up_w, down_w = (weights[:, i].reshape(-1, size) for i in range(3))
    gate = dot_plain(normed[...], gate_w)
    up = dot_plain(normed[...], up_w)
    grad_act = dot_plain(grads[...], down_w)
    sig = jax.nn.sigmoid(gate)
    swish = gate * sig
    act_here = (swish * up).astype(bf16)
    gate_here = (grad_act * up * sig * (1.0 + gate * (1.0 - sig))).astype(bf16)
    up_here = (grad_act * swish).astype(bf16)
    act[...] = act_here
    grad_both[0] = gate_here
    grad_both[1] = up_here
    out_here = dot_right(act_here, down_w)
    grad_here = dot_right(gate_here, gate_w) + dot_right(up_here, up_w)

    @pl.when(tile == 0)
    def _():
        out_sum[...] = out_here
        grad_sum[...] = grad_here

    @pl.when(tile > 0)
    def _():
        out_sum[...] += out_here
        grad_sum[...] += grad_here

    @pl.when(tile == pl.num_programs(0) - 1)
    def _():
        out[...] = out_sum[...].astype(bf16)
        grad_normed[...] = grad_sum[...].astype(bf16)


def feed_forward(normed, grads, weights):
    rows, width = normed.shape
    devices, _, each, hidden = weights.shape
    tile = 512 if hidden % 512 == 0 else 256
    whole = pl.BlockSpec((rows, width), lambda j: (0, 0))
    block = pl.BlockSpec((devices, 3, each, tile), lambda j: (0, 0, 0, j))
    part = pl.BlockSpec((rows, tile), lambda j: (0, j))
    both = pl.BlockSpec((2, rows, tile), lambda j: (0, 0, j))
    narrow = jax.ShapeDtypeStruct((rows, width), bf16)
    return pl.pallas_call(
        feed_kernel,
        grid=(hidden // tile,),
        in_specs=[whole, whole, block],
        out_specs=[part, both, whole, whole],
        out_shape=[
            jax.ShapeDtypeStruct((rows, hidden), bf16),
            jax.ShapeDtypeStruct((2, rows, hidden), bf16),
            narrow,
            narrow,
        ],
        scratch_shapes=[pltpu.VMEM((rows, width), f32)] * 2,
        compiler_params=pltpu.CompilerParams(vmem_limit_bytes=40 * 2**20),
        cost_estimate=pl.CostEstimate(
            flops=12 * rows * width * hidden,
            bytes_accessed=6 * width * hidden + 10 * rows * hidden,
            transcendentals=rows * hidden,
        ),
    )(normed, grads, weights)


class Step:
    def __init__(self, name, needs, gives, run, cost, rank, lasts):
        self.name, self.needs, self.gives = name, needs, gives
        self.run, self.cost, self.rank, self.lasts = run, cost, rank, lasts
        self.alone = name.startswith("small")


class Sum:
    def __init__(self, name, part, finish, own, joined, rank):
        self.name, self.part, self.finish = name, part, finish
        self.own, self.joined, self.rank = own, joined, rank
        self.start = None


def plan(steps, sums, line, budget):
    slot_of = {}
    todo = list(steps)
    waiting = list(sums)
    taken = set()
    finishing = {}
    arriving = {}
    slots = []
    slot = 0
    while todo or waiting or any(s >= slot for s in arriving):
        for one in sorted(waiting, key=lambda q: q.rank):
            if one.part in slot_of and slot_of[one.part] < slot:
                if slot not in taken and slot + line not in taken:
                    taken.update((slot, slot + line))
                    one.start = slot
                    waiting.remove(one)
                    finishing.setdefault(slot + line - 1, []).append(one)
                    arriving.setdefault(slot + 2 * line - 1, []).append(one)
                    break
        here = []
        spent = 0.0
        for one in finishing.get(slot, []):
            slot_of[one.name + "_sum"] = slot - 1
            step = next(s for s in todo if s.name == one.finish)
            here.append(step)
            todo.remove(step)
            spent += step.cost
            slot_of.update({name: slot for name in step.gives})
        for one in arriving.get(slot, []):
            slot_of[one.joined] = slot - 1
        again = True
        while again:
            again = False
            for step in sorted(todo, key=lambda s: s.rank):
                ready = all(name in slot_of for name in step.needs)
                if step.alone:
                    ready = ready and all(slot_of[name] < slot for name in step.needs)
                if not taken:
                    fits = spent + step.cost <= 7.0
                elif step.rank[0] >= 5:
                    fits = spent <= 6.0
                else:
                    fits = spent + step.cost <= budget
                if ready and (spent == 0.0 or fits):
                    here.append(step)
                    todo.remove(step)
                    spent += step.cost
                    slot_of.update({name: slot for name in step.gives})
                    again = True
                    break
        slots.append(here)
        slot += 1
    return slots


def local(
    tokens,
    doc_start,
    norm_first,
    in_weight,
    conv_weight,
    out_weight,
    norm_second,
    gate_weight,
    up_weight,
    down_weight,
    out_grad,
):
    line = lax.axis_size("tp")
    place = lax.axis_index("tp")
    count, width = tokens.shape
    rows = count // chunks
    half = rows // 2
    inner = conv_weight.shape[1]

    def tokens_of(c):
        return tokens[c * rows : (c + 1) * rows]

    def own_half(block):
        return jnp.where(place == line - 1, block[:half], block[half:])

    gain_one = norm_first.astype(f32)
    gain_two = norm_second.astype(f32)
    taps = conv_weight.astype(f32)
    kept_one = (1 - doc_start).astype(f32)[:, None]

    def normed(block):
        value = block.astype(f32)
        return (value * rms_scale(value) * gain_one).astype(bf16)

    before_tokens = from_before(tokens[count - halo :], "seq")
    before_kept = from_before(kept_one[count - 1 :], "seq")

    def norms():
        return normed(tokens), normed(before_tokens)

    def norms():
        return normed(tokens), normed(before_tokens)

    def held_back():
        return jnp.stack([gate_weight, up_weight, down_weight.T])

    in_full = lax.all_gather(
        in_weight.reshape(in_weight.shape[0], 3 * inner), "seq", axis=0, tiled=True
    )
    out_gather = Gather([(out_weight, 1)], "seq")
    feed_held = together([out_gather], held_back)
    normed_one, normed_before = together([out_gather], norms)
    while out_gather.turn < out_gather.turns:
        together([out_gather])
    (out_full,) = out_gather.whole()
    feed_full = lax.all_gather(feed_held, "seq")
    env = {}
    kept_back = jnp.concatenate([before_kept, kept_one[:-1]], axis=0)
    both_kept = kept_one * kept_back

    def kept_of(c):
        return kept_one[c * rows : (c + 1) * rows]

    def both_of(c):
        return both_kept[c * rows : (c + 1) * rows]

    steps = []
    sums = []

    def add(name, needs, gives, cost, rank, lasts=0):
        def keep(run):
            steps.append(Step(name, needs, gives, run, cost, rank, lasts))
            return run

        return keep

    def mix(c):
        def run_a(e):
            block = normed_one[c * rows : (c + 1) * rows]
            if c == 0:
                block = jnp.concatenate([normed_before, block], axis=0)
            projected = dot_plain(block, in_full).astype(bf16)
            left = projected[:, :inner].astype(f32)
            right = projected[:, 2 * inner :].astype(f32)
            product = left * right
            if c == 0:
                earlier = product[halo - 2 : halo]
                product = product[halo:]
                projected = projected[halo:]
            else:
                earlier = e[f"tail{c - 1}"]
            longer = jnp.concatenate([earlier, product], axis=0)
            convolved = (
                taps[0] * product
                + taps[1] * kept_of(c) * longer[1:-1]
                + taps[2] * both_of(c) * longer[:-2]
            )
            gated = (projected[:, inner : 2 * inner].astype(f32) * convolved).astype(bf16)
            return projected, longer, product[-2:], convolved, gated

        def run_b(e):
            return (dot_plain(e[f"gated{c}"], out_full).astype(bf16),)

        gives = [f"{n}{c}" for n in ("proj", "longer", "tail", "conv", "gated")]
        needs = [] if c == 0 else [f"tail{c - 1}"]
        add(f"mixA{c}", needs, gives, 5.0, (0, c))(run_a)
        add(f"mixB{c}", [f"gated{c}"], [f"mixed{c}"], 2.0, (0, c))(run_b)

    def first(c):
        def run(e):
            hidden = own_half(tokens_of(c)).astype(f32) + e[f"one{c}_sum"]
            inverse = rms_scale(hidden)
            return hidden, inverse, (hidden * inverse * gain_two).astype(bf16)

        add(f"first{c}", [f"one{c}_sum"], [f"hid{c}", f"inv{c}", f"n2own{c}"], 2.0, (1, c))(run)
        sums.append(Sum(f"one{c}", f"mixed{c}", f"first{c}", f"n2own{c}", f"n2{c}", (0, c)))

    def feed(c):
        def run(e):
            grads = out_grad[c * rows : (c + 1) * rows]
            return feed_forward(e[f"n2{c}"], grads, feed_full)

        gives = [f"act{c}", f"gb{c}", f"fo{c}", f"gn2{c}"]
        add(f"feed{c}", [f"n2{c}"], gives, 22.0, (2, c))(run)

    def second(c):
        def run(e):
            hidden, inverse = e[f"hid{c}"], e[f"inv{c}"]
            scaled = hidden * inverse
            grad_normed = e[f"two{c}_sum"]
            grad_hidden = own_half(out_grad[c * rows : (c + 1) * rows]).astype(f32) + norm_back(
                grad_normed, scaled, inverse, gain_two
            )
            return grad_hidden, grad_hidden.astype(bf16), jnp.sum(grad_normed * scaled, axis=0)

        gives = [f"gh{c}", f"gmown{c}", f"g2{c}"]
        add(f"second{c}", [f"two{c}_sum", f"hid{c}", f"inv{c}"], gives, 3.0, (1, c))(run)
        sums.append(Sum(f"two{c}", f"gn2{c}", f"second{c}", f"gmown{c}", f"gm{c}", (1, c)))

    def third(first, last):
        def run(e):
            blocks = []
            for c in range(first, last):
                part = e[f"fo{c}"].astype(f32)
                top = jnp.where(place == line - 1, e[f"hid{c}"], 0.0)
                bottom = jnp.where(place == 0, e[f"hid{c}"], 0.0)
                blocks += [part[:half] + top, part[half:] + bottom]
            return (lax.psum(jnp.concatenate(blocks, axis=0).astype(bf16), "tp"),)

        needs = [f"{n}{c}" for n in ("fo", "hid") for c in range(first, last)]
        add(f"third{first}", needs, [f"out{first}"], 3.0, (2.5, first), 6)(run)

    def third_line(c):
        def run(e):
            return ((e[f"hid{c}"] + e[f"three{c}_sum"]).astype(bf16),)

        add(f"third{c}", [f"three{c}_sum", f"hid{c}"], [f"outown{c}"], 1.0, (1, c))(run)
        sums.append(Sum(f"three{c}", f"fo{c}", f"third{c}", f"outown{c}", f"out{c}", (3, c)))

    def back(c):
        def run_a(e):
            grad_gated = dot_right(e[f"gm{c}"], out_full).astype(bf16).astype(f32)
            grad_conv = grad_gated * e[f"proj{c}"][:, inner : 2 * inner].astype(f32)
            grad_out = (grad_gated * e[f"conv{c}"]).astype(bf16)
            longer = e[f"longer{c}"]
            near = grad_conv * kept_of(c)
            far = grad_conv * both_of(c)
            tap_sums = jnp.stack(
                [
                    jnp.sum(grad_conv * longer[2:], axis=0),
                    jnp.sum(near * longer[1:-1], axis=0),
                    jnp.sum(far * longer[:-2], axis=0),
                ]
            )
            head = jnp.concatenate([near[:1], far[:2]], axis=0)
            passed = (from_after(head, "seq"),) if c == 0 else ()
            return (grad_conv, grad_out, tap_sums, head) + passed

        def run_b(e):
            grad_conv = e[f"gc{c}"]
            head = e[f"head{c + 1}"]
            near = jnp.concatenate([(grad_conv * kept_of(c))[1:], head[:1]], axis=0)
            far = jnp.concatenate([(grad_conv * both_of(c))[2:], head[1:]], axis=0)
            grad_product = taps[0] * grad_conv + taps[1] * near + taps[2] * far
            left = e[f"proj{c}"][:, :inner].astype(f32)
            right = e[f"proj{c}"][:, 2 * inner :].astype(f32)
            grad_projected = jnp.concatenate(
                [
                    (grad_product * right).astype(bf16),
                    e[f"go{c}"],
                    (grad_product * left).astype(bf16),
                ],
                axis=1,
            )
            grad_normed = dot_right(grad_projected, in_full).astype(bf16)
            value = tokens_of(c).astype(f32)
            gain_sum = jnp.sum(grad_normed.astype(f32) * (value * rms_scale(value)), axis=0)
            return grad_projected, grad_normed, gain_sum

        needs = [f"gm{c}", f"proj{c}", f"longer{c}", f"conv{c}"]
        gives = [f"gc{c}", f"go{c}", f"tap{c}", f"head{c}"]
        gives += [f"head{chunks}"] if c == 0 else []
        add(f"backA{c}", needs, gives, 5.0, (2, c))(run_a)
        needs = [f"gc{c}", f"go{c}", f"proj{c}", f"head{c + 1}"]
        add(f"backB{c}", needs, [f"gp{c}", f"gn1{c}", f"g1{c}"], 9.0, (3, c))(run_b)

    def fourth(c):
        def run(e):
            value = own_half(tokens_of(c)).astype(f32)
            inverse = rms_scale(value)
            scaled = value * inverse
            grad_normed = e[f"four{c}_sum"]
            grad_tokens = e[f"gh{c}"] + norm_back(grad_normed, scaled, inverse, gain_one)
            return (grad_tokens.astype(bf16),)

        add(f"fourth{c}", [f"four{c}_sum", f"gh{c}"], [f"gtown{c}"], 3.0, (1, c))(run)
        sums.append(Sum(f"four{c}", f"gn1{c}", f"fourth{c}", f"gtown{c}", f"gt{c}", (2, c)))

    for c in range(chunks):
        mix(c)
    for c in range(chunks):
        first(c)
        feed(c)
        second(c)
        back(c)
        fourth(c)

    third(0, chunks // 2)
    for c in range(chunks // 2, chunks):
        third_line(c)

    def joined(e, name):
        return jnp.concatenate([e[f"{name}{c}"] for c in range(chunks)], axis=0)

    def scattered(part, dim):
        return lax.psum_scatter(part.astype(bf16), "seq", scatter_dimension=dim, tiled=True)

    def names(*kinds):
        return [f"{kind}{c}" for kind in kinds for c in range(chunks)]

    add("down_grad", names("act"), ["down_grad"], 12.0, (5, 0), 5)(
        lambda e: (scattered(dot_left(joined(e, "act"), out_grad), 1),)
    )
    def feed_grad(e):
        both = jnp.concatenate([e[f"gb{c}"] for c in range(chunks)], axis=1)
        part = jnp.einsum("td,ktf->kdf", joined(e, "n2"), both, preferred_element_type=f32)
        return (scattered(part, 1),)

    add("feed_grad", names("n2", "gb"), ["feed_grad"], 22.0, (5, 1), 9)(feed_grad)
    add("out_grad", names("gated", "gm"), ["out_proj_grad"], 5.0, (5, 3), 3)(
        lambda e: (scattered(dot_left(joined(e, "gated"), joined(e, "gm")), 1),)
    )
    add("in_grad", names("gp"), ["in_grad"], 10.0, (5, 4), 4)(
        lambda e: (scattered(dot_left(normed_one, joined(e, "gp")), 0),)
    )

    def total(e, kind):
        return sum(e[f"{kind}{c}"] for c in range(chunks))

    def small(e):
        owner = (place == 0) | (place == line - 1)
        gains = jnp.stack([total(e, "g1"), jnp.where(owner, total(e, "g2"), 0.0)])
        return (jnp.concatenate([gains.reshape(-1, inner), total(e, "tap")], axis=0),)

    add("small", names("g1", "g2", "tap"), ["small0"], 2.0, (4, 9))(small)
    turn = 0
    for axis in ("seq", "tp"):
        for bit in bits_of(axis):

            def run(e, axis=axis, bit=bit, turn=turn):
                value = e[f"small{turn}"]
                if axis == "seq":
                    return (value + paired(value, axis, bit),)
                gains = value[:-3] + paired(value[:-3], axis, bit)
                return (jnp.concatenate([gains, value[-3:]], axis=0),)

            add(f"small{turn + 1}", [f"small{turn}"], [f"small{turn + 1}"], 2.0, (4, 10))(run)
            turn += 1

    slots = plan(steps, sums, line, 30.0)
    run_slots(slots, sums, env, line, place, half)

    in_grad = env["in_grad"].astype(f32).reshape(in_weight.shape)
    out_proj_grad = env["out_proj_grad"].astype(f32)
    gate_grad, up_grad = env["feed_grad"].astype(f32)
    down_grad = env["down_grad"].astype(f32)

    gains = env[f"small{turn}"][:-3].reshape(2, width)
    return (
        jnp.concatenate([env["out0"]] + [env[f"out{c}"] for c in range(chunks // 2, chunks)], axis=0),
        jnp.concatenate([env[f"gt{c}"].astype(f32) for c in range(chunks)], axis=0),
        in_grad,
        env[f"small{turn}"][-3:],
        out_proj_grad,
        gate_grad,
        up_grad,
        down_grad,
        gains[0],
        gains[1],
    )


def run_slots(slots, sums, env, line, place, half):
    up, down = {}, {}
    last = line - 1
    fresh, later, busy_until = [], {}, 0
    awaited = f"head{chunks}"

    def chosen(options):
        value = None
        for position, option in sorted(options.items(), reverse=True):
            if value is None or option is value:
                value = option
            else:
                value = jnp.where(place == position, option, value)
        return value

    def local_parts(slot):
        up_options, down_options = {}, {}
        for one in sums:
            if one.start is None:
                continue
            hop = slot - one.start
            if 0 <= hop < last:
                part = env[one.part]
                up_options[hop] = part[:half]
                down_options[last - hop] = part[half:]
            hop = slot - one.start - line
            if 0 <= hop < last:
                value = env[one.own] if hop == 0 else None
                up_options[hop] = down_options[last - hop] = value
        return up_options, down_options

    def mixed(options):
        if all(value is None for value in options.values()):
            return None
        return chosen({p: 0.0 if value is None else value for p, value in options.items()})

    ready = None
    for slot, steps in enumerate(slots):
        up_options, down_options = local_parts(slot)
        sending = len(up_options) > 0
        if sending:
            send_up, send_down = ready if ready is not None else (None, None)
            if ready is None:
                send_up, send_down = mixed(up_options), mixed(down_options)
            if slot - 1 in up:
                send_up = up[slot - 1] if send_up is None else send_up + up[slot - 1]
                send_down = down[slot - 1] if send_down is None else send_down + down[slot - 1]
        for one in sums:
            if one.start is not None and slot == one.start + last:
                part = env[one.part]
                above = part[:half].astype(f32) + up[slot - 1].astype(f32)
                below = part[half:].astype(f32) + down[slot - 1].astype(f32)
                env[one.name + "_sum"] = jnp.where(place == last, above, below)
            if one.start is not None and slot == one.start + line + last:
                own, begin = env[one.own], one.start + line
                top = {last: own} | {last - 1 - j: down[begin + j] for j in range(last)}
                bottom = {0: own} | {1 + j: up[begin + j] for j in range(last)}
                env[one.joined] = jnp.concatenate([chosen(top), chosen(bottom)], axis=0)
        keys = list(fresh) + later.get(slot, [])
        for step in steps:
            keys += [name for name in step.needs if name in env and name not in keys]
        tied = [env[name] for name in keys]
        if sending:
            send_up, send_down, tied = lax.optimization_barrier((send_up, send_down, tied))
            up[slot] = lax.ppermute(send_up, "tp", [(p, p + 1) for p in up_options])
            down[slot] = lax.ppermute(send_down, "tp", [(p, p - 1) for p in down_options])
        elif tied:
            tied = lax.optimization_barrier(tied)
        env.update(zip(keys, tied))
        fresh = []
        for step in steps:
            env.update(zip(step.gives, step.run(env)))
            if step.lasts:
                busy_until = max(busy_until, slot + 1) + step.lasts
                later.setdefault(busy_until, []).extend(step.gives)
            else:
                fresh += [name for name in step.gives if name != awaited]
        ready = tuple(mixed(options) for options in local_parts(slot + 1))


def solution(mesh):
    in_specs = (
        P("seq", None),
        P("seq"),
        P(),
        P("seq", None, "tp"),
        P(None, "tp"),
        P("tp", "seq"),
        P(),
        P("seq", "tp"),
        P("seq", "tp"),
        P("tp", "seq"),
        P("seq", None),
    )
    out_specs = (
        P("seq", None),
        P("seq", None),
        P("seq", None, "tp"),
        P(None, "tp"),
        P("tp", "seq"),
        P("seq", "tp"),
        P("seq", "tp"),
        P("tp", "seq"),
        P(),
        P(),
    )
    return jax.shard_map(local, mesh=mesh, in_specs=in_specs, out_specs=out_specs, check_vma=False)
```

profile of v0, /device:TPU:0, one launch (start us, length us, event | category | flops | bytes accessed | tf_op | source)
XLA Modules:
  0.0 776.6 jit_solution(13920723965609443792)
XLA Ops:
  15.9 3.5 pad_maximum_fusion
  36.2 5.3 collective-permute-done.3.refs_4_
  48.2 12.3 %all-gather.4.cloned.1.call-done = bf16[2048,1536]{0,1:T(8,128)(2,1)} async-done(((bf16[256,1536]{0,1:T(8,128)(2,1)}), bf16[2048,1536]{0,1:T(8,128)(2,1)}) %all-gather.4.cloned.1.call-update) | async-done | bytes 6291472 | tf_op jit(solution)/shard_map/all_gather | solution.py:348
  60.5 5.2 convolution_convert_fusion.2
  90.0 5.3 collective-permute-start.13
  96.8 8.9 %collective-permute-done.13 = bf16[128,2048]{1,0:T(8,128)(2,1)} collective-permute-done((bf16[128,2048]{1,0:T(8,128)(2,1)}, bf16[128,2048]{1,0:T(8,128)(2,1)}, u32[]{:S(2)}, u32[]{:S(2)}) %collective-permute-start.13) | collective-permute-done | bytes 524320 | tf_op jit(solution)/shard_map/ppermute | solution.py:668
  109.0 9.1 %collective-permute-start.15 = (bf16[128,2048]{1,0:T(8,128)(2,1)}, bf16[128,2048]{1,0:T(8,128)(2,1)}, u32[]{:S(2)}, u32[]{:S(2)}) collective-permute-start(bf16[128,2048]{1,0:T(8,128)(2,1)} %get-tuple-element.323), channel_id=1, source_target_pairs={{2,3},{1,2},{0,1},{6,7},{5,6},{4,5},{10,11},{9,10},{8,9},{14,15},{... | collective-permute-start | bytes 1572872 | tf_op jit(solution)/shard_map/ppermute | solution.py:668
  119.4 7.9 %collective-permute-done.15 = bf16[128,2048]{1,0:T(8,128)(2,1)} collective-permute-done((bf16[128,2048]{1,0:T(8,128)(2,1)}, bf16[128,2048]{1,0:T(8,128)(2,1)}, u32[]{:S(2)}, u32[]{:S(2)}) %collective-permute-start.15) | collective-permute-done | bytes 524320 | tf_op jit(solution)/shard_map/ppermute | solution.py:668
  127.3 4.9 collective-permute-done.16
  139.8 5.8 collective-permute-done.17
  145.6 4.1 collective-permute-done.18
  151.8 4.6 collective-permute-start.19
  156.7 6.0 collective-permute-done.20
  165.6 5.0 collective-permute-start.21
  170.9 5.1 collective-permute-done.22
  180.9 4.9 collective-permute-start.23
  194.0 5.2 collective-permute-start.25
  202.0 19.1 %shard_map.187 = (bf16[256,2048]{1,0:T(8,128)(2,1)S(1)}, bf16[2,256,2048]{2,1,0:T(8,128)(2,1)S(1)}, bf16[256,2048]{1,0:T(8,128)(2,1)S(1)}, bf16[256,2048]{1,0:T(8,128)(2,1)S(1)}) custom-call(bf16[256,2048]{1,0:T(8,128)(2,1)S(1)} %pad_maximum_fusion.2.normed, bf16[256,2048]{1,0:T(8,128)(2,1)S(1)} %copy-done.20, bf16[8,3,256,2048]{3,2,1,0:T(8,128)(2,1)} %bitcast.127), custom_call_target="tpu_custom_call" | custom-call | flops 12884901888 | bytes 30408704 | tf_op jit(solution)/shard_map/pallas_call | solution.py:211
  224.5 5.3 collective-permute-start.27
  231.4 18.9 %shard_map.188 = (bf16[256,2048]{1,0:T(8,128)(2,1)S(1)}, bf16[2,256,2048]{2,1,0:T(8,128)(2,1)S(1)}, bf16[256,2048]{1,0:T(8,128)(2,1)S(1)}, bf16[256,2048]{1,0:T(8,128)(2,1)S(1)}) custom-call(bf16[256,2048]{1,0:T(8,128)(2,1)S(1)} %pad_maximum_fusion.3.normed, bf16[256,2048]{1,0:T(8,128)(2,1)S(1)} %get-tuple-element.714.grads, bf16[8,3,256,2048]{3,2,1,0:T(8,128)(2,1)} %bitcast.128), custom_call_target="tpu_custom_call" | custom-call | flops 12884901888 | bytes 30408704 | tf_op jit(solution)/shard_map/pallas_call | solution.py:211
  256.8 4.7 collective-permute-start.29
  262.9 19.5 %shard_map.189 = (bf16[256,2048]{1,0:T(8,128)(2,1)S(1)}, bf16[2,256,2048]{2,1,0:T(8,128)(2,1)S(1)}, bf16[256,2048]{1,0:T(8,128)(2,1)S(1)}, bf16[256,2048]{1,0:T(8,128)(2,1)S(1)}) custom-call(bf16[256,2048]{1,0:T(8,128)(2,1)S(1)} %pad_maximum_fusion.4.normed, bf16[256,2048]{1,0:T(8,128)(2,1)S(1)} %copy-done.19, bf16[8,3,256,2048]{3,2,1,0:T(8,128)(2,1)} %bitcast.129), custom_call_target="tpu_custom_call" | custom-call | flops 12884901888 | bytes 30408704 | tf_op jit(solution)/shard_map/pallas_call | solution.py:211
  282.5 15.7 %collective-permute-done.30 = bf16[128,2048]{1,0:T(8,128)(2,1)S(1)} collective-permute-done((bf16[128,2048]{1,0:T(8,128)(2,1)S(1)}, bf16[128,2048]{1,0:T(8,128)(2,1)S(1)}, u32[]{:S(2)}, u32[]{:S(2)}) %collective-permute-start.30) | collective-permute-done | bytes 524320 | tf_op jit(solution)/shard_map/ppermute | solution.py:669
  303.0 19.0 %shard_map.190 = (bf16[256,2048]{1,0:T(8,128)(2,1)S(1)}, bf16[2,256,2048]{2,1,0:T(8,128)(2,1)S(1)}, bf16[256,2048]{1,0:T(8,128)(2,1)S(1)}, bf16[256,2048]{1,0:T(8,128)(2,1)S(1)}) custom-call(bf16[256,2048]{1,0:T(8,128)(2,1)S(1)} %pad_maximum_fusion.5.normed, bf16[256,2048]{1,0:T(8,128)(2,1)S(1)} %copy-done.18, bf16[8,3,256,2048]{3,2,1,0:T(8,128)(2,1)} %bitcast.130), custom_call_target="tpu_custom_call" | custom-call | flops 12884901888 | bytes 30408704 | tf_op jit(solution)/shard_map/pallas_call | solution.py:211
  327.1 11.4 %convolution_convert_fusion.1 = bf16[2048,2048]{1,0:T(8,128)(2,1)} fusion(bf16[1024,2048]{1,0:T(8,128)(2,1)S(1)} %copy-done.55, bf16[256,2048]{1,0:T(8,128)(2,1)S(1)} %get-tuple-element.499, bf16[256,2048]{1,0:T(8,128)(2,1)S(1)} %get-tuple-element.498, bf16[256,2048]{1,0:T(8,128)(2,1)S(1)} %copy-done.31, bf16[256,2048]{1,0:T(8,128)(2,1)S(1)} %copy-done.29), kind=kOutput, calls=%fused_computation.14 | convolution fusion | flops 8610906112 | bytes 16777216 | tf_op jit(solution)/shard_map/dot_general | solution.py:26
  341.9 4.7 collective-permute-start.33
  348.7 17.2 %collective-permute-done.33 = bf16[128,2048]{1,0:T(8,128)(2,1)S(1)} collective-permute-done((bf16[128,2048]{1,0:T(8,128)(2,1)S(1)}, bf16[128,2048]{1,0:T(8,128)(2,1)S(1)}, u32[]{:S(2)}, u32[]{:S(2)}) %collective-permute-start.33) | collective-permute-done | bytes 524320 | tf_op jit(solution)/shard_map/ppermute | solution.py:668
  374.6 22.4 %convert_bitcast_fusion = bf16[2,2048,2048]{1,2,0:T(8,128)(2,1)} fusion(bf16[2,256,2048]{2,1,0:T(8,128)(2,1)} %copy-done.27, bf16[2,256,2048]{2,1,0:T(8,128)(2,1)S(1)} %copy-done.26, bf16[2,256,2048]{2,1,0:T(8,128)(2,1)S(1)} %copy-done.24, bf16[2,256,2048]{2,1,0:T(8,128)(2,1)S(1)} %copy-done.22, bf16[256,2048]{1,0:T(8,128)(2,1)S(1)} %copy-done.17, ...), kind=kOutput, calls=%fused_computation | convolution fusion | flops 17238589440 | bytes 29360128 | tf_op jit(solution)/shard_map/td,ktf->kdf/dot_general | solution.py:547
  399.0 4.6 collective-permute-start.35
  405.6 5.8 collective-permute-done.36
  411.4 3.9 select_add_fusion.22
  419.1 4.6 collective-permute-start.37
  425.7 5.1 collective-permute-done.38
  438.5 4.6 collective-permute-start.39
  443.5 5.4 collective-permute-done.40
  458.3 3.6 multiply_reduce_fusion.23
  464.0 4.3 collective-permute-done.42
  478.6 5.1 collective-permute-done.43
  483.7 4.1 collective-permute-done.44
  497.9 5.3 collective-permute-done.45
  503.2 4.1 collective-permute-done.46
  522.2 4.1 collective-permute-done.49
  528.8 3.7 collective-permute-start.50
  533.9 7.1 collective-permute-done.50
  541.0 4.9 collective-permute-done.51
  555.0 4.6 collective-permute-start.52
  561.1 5.0 collective-permute-done.53
  574.9 3.8 fusion.38
  592.9 4.8 collective-permute-start.59
  600.7 3.8 collective-permute-done.59
  609.4 9.0 %convolution_convert_fusion = bf16[2048,1536]{1,0:T(8,128)(2,1)} fusion(bf16[1024,2048]{1,0:T(8,128)(2,1)S(1)} %copy-done.85, bf16[256,1536]{1,0:T(8,128)(2,1)S(1)} %copy-done.162, bf16[256,1536]{1,0:T(8,128)(2,1)S(1)} %copy-done.163, bf16[256,1536]{1,0:T(8,128)(2,1)S(1)} %copy-done.161, bf16[256,1536]{1,0:T(8,128)(2,1)S(1)} %copy-done.160), kind=kOutput, calls=%fused_computation.13 | convolution fusion | flops 6458179584 | bytes 13631488 | tf_op jit(solution)/shard_map/dot_general | solution.py:26
  618.4 4.8 collective-permute-start.61
  625.9 4.5 collective-permute-done.61
  633.5 4.5 collective-permute-start.66
  640.4 6.8 collective-permute-done.66
  652.5 5.0 collective-permute-start.67
  657.5 6.8 collective-permute-done.68
  667.7 16.8 %collective-permute-done.70 = bf16[128,2048]{1,0:T(8,128)(2,1)S(1)} collective-permute-done((bf16[128,2048]{1,0:T(8,128)(2,1)S(1)}, bf16[128,2048]{1,0:T(8,128)(2,1)S(1)}, u32[]{:S(2)}, u32[]{:S(2)}) %collective-permute-start.70) | collective-permute-done | bytes 524320 | tf_op jit(solution)/shard_map/ppermute | solution.py:669
  687.4 8.7 %collective-permute-done.72 = bf16[128,2048]{1,0:T(8,128)(2,1)S(1)} collective-permute-done((bf16[128,2048]{1,0:T(8,128)(2,1)S(1)}, bf16[128,2048]{1,0:T(8,128)(2,1)S(1)}, u32[]{:S(2)}, u32[]{:S(2)}) %collective-permute-start.72) | collective-permute-done | bytes 524320 | tf_op jit(solution)/shard_map/ppermute | solution.py:669
  700.4 5.7 collective-permute-done.73
  707.0 4.4 collective-permute-start.75
  712.9 5.2 collective-permute-done.75
  730.9 15.3 %collective-permute-done.78 = bf16[128,2048]{1,0:T(8,128)(2,1)} collective-permute-done((bf16[128,2048]{1,0:T(8,128)(2,1)}, bf16[128,2048]{1,0:T(8,128)(2,1)}, u32[]{:S(2)}, u32[]{:S(2)}) %collective-permute-start.78) | collective-permute-done | bytes 524320 | tf_op jit(solution)/shard_map/ppermute | solution.py:669
  762.9 6.7 concatenate.177
  (764 shorter events, 291.0 us)
Async XLA Ops:
  7.2 53.3 %all-gather.4.cloned.1.call-start = ((), (), s32[]{:S(2)}) async-start(), calls=%async_computation.4 | async-start | bytes 7077888 | tf_op jit(solution)/shard_map/all_gather | solution.py:348
  9.6 191.1 %all-gather.6.cloned.1.call-start = ((), (), s32[]{:S(2)}) async-start(), calls=%async_computation.10 | async-start | bytes 28311552 | tf_op jit(solution)/shard_map/all_gather | solution.py:357
  19.5 434.8 %all-reduce.2.cloned.1.call-start = ((), (), s32[]{:S(2)}) async-start(), calls=%async_computation.5 | async-start | bytes 4194304 | tf_op jit(solution)/shard_map/psum | solution.py:449
  20.6 12.0 %collective-permute-start.7 = (bf16[16,2048]{1,0:T(8,128)(2,1)S(1)}, bf16[16,2048]{1,0:T(8,128)(2,1)S(1)}, u32[]{:S(2)}, u32[]{:S(2)}) collective-permute-start(bf16[16,2048]{1,0:T(8,128)(2,1)S(1)} %slice.687), channel_id=1, source_target_pairs={{0,4},{4,8},{8,12},{12,16},{16,20},{20,24},{24,28},{1,5},{5,9},{9,... | collective-permute-start | bytes 196616 | tf_op jit(solution)/shard_map/ppermute | solution.py:40
  23.1 21.4 %collective-permute-start.8 = (f32[1,1]{1,0:T(1,128)}, f32[1,1]{1,0:T(1,128)}, u32[]{:S(2)}, u32[]{:S(2)}) collective-permute-start(f32[1,1]{1,0:T(1,128)} %bitcast.8), channel_id=1, source_target_pairs={{0,4},{4,8},{8,12},{12,16},{16,20},{20,24},{24,28},{1,5},{5,9},{9,... | collective-permute-start | bytes 20 | tf_op jit(solution)/shard_map/ppermute | solution.py:40
  73.8 15.1 %collective-permute-start.11 = (bf16[128,2048]{1,0:T(8,128)(2,1)S(1)}, bf16[128,2048]{1,0:T(8,128)(2,1)S(1)}, u32[]{:S(2)}, u32[]{:S(2)}) collective-permute-start(bf16[128,2048]{1,0:T(8,128)(2,1)S(1)} %get-tuple-element.316), channel_id=1, source_target_pairs={{0,1},{4,5},{8,9},{12,13},{16,17},{20,21},{24,25},{28,29}} | collective-permute-start | bytes 1572872 | tf_op jit(solution)/shard_map/ppermute | solution.py:668
  77.3 11.6 %collective-permute-start.12 = (bf16[128,2048]{1,0:T(8,128)(2,1)S(1)}, bf16[128,2048]{1,0:T(8,128)(2,1)S(1)}, u32[]{:S(2)}, u32[]{:S(2)}) collective-permute-start(bf16[128,2048]{1,0:T(8,128)(2,1)S(1)} %get-tuple-element.317), channel_id=1, source_target_pairs={{3,2},{7,6},{11,10},{15,14},{19,18},{23,22},{27,26},{31,30}} | collective-permute-start | bytes 1572872 | tf_op jit(solution)/shard_map/ppermute | solution.py:669
  90.0 15.7 %collective-permute-start.13 = (bf16[128,2048]{1,0:T(8,128)(2,1)}, bf16[128,2048]{1,0:T(8,128)(2,1)}, u32[]{:S(2)}, u32[]{:S(2)}) collective-permute-start(bf16[128,2048]{1,0:T(8,128)(2,1)} %get-tuple-element.321), channel_id=1, source_target_pairs={{1,2},{0,1},{5,6},{4,5},{9,10},{8,9},{13,14},{12,13},{17,18},{16,1... | collective-permute-start | bytes 1572872 | tf_op jit(solution)/shard_map/ppermute | solution.py:668
  109.0 18.3 %collective-permute-start.15 = (bf16[128,2048]{1,0:T(8,128)(2,1)}, bf16[128,2048]{1,0:T(8,128)(2,1)}, u32[]{:S(2)}, u32[]{:S(2)}) collective-permute-start(bf16[128,2048]{1,0:T(8,128)(2,1)} %get-tuple-element.323), channel_id=1, source_target_pairs={{2,3},{1,2},{0,1},{6,7},{5,6},{4,5},{10,11},{9,10},{8,9},{14,15},{... | collective-permute-start | bytes 1572872 | tf_op jit(solution)/shard_map/ppermute | solution.py:668
  118.1 14.1 %collective-permute-start.16 = (bf16[128,2048]{1,0:T(8,128)(2,1)}, bf16[128,2048]{1,0:T(8,128)(2,1)}, u32[]{:S(2)}, u32[]{:S(2)}) collective-permute-start(bf16[128,2048]{1,0:T(8,128)(2,1)} %get-tuple-element.324), channel_id=1, source_target_pairs={{1,0},{2,1},{3,2},{5,4},{6,5},{7,6},{9,8},{10,9},{11,10},{13,12},{... | collective-permute-start | bytes 1572872 | tf_op jit(solution)/shard_map/ppermute | solution.py:669
  136.8 12.9 %collective-permute-start.18 = (bf16[128,2048]{1,0:T(8,128)(2,1)S(1)}, bf16[128,2048]{1,0:T(8,128)(2,1)S(1)}, u32[]{:S(2)}, u32[]{:S(2)}) collective-permute-start(bf16[128,2048]{1,0:T(8,128)(2,1)S(1)} %get-tuple-element.327), channel_id=1, source_target_pairs={{1,0},{2,1},{3,2},{5,4},{6,5},{7,6},{9,8},{10,9},{11,10},{13,12},{... | collective-permute-start | bytes 1572872 | tf_op jit(solution)/shard_map/ppermute | solution.py:669
  150.5 12.1 %collective-permute-start.20 = (bf16[128,2048]{1,0:T(8,128)(2,1)S(1)}, bf16[128,2048]{1,0:T(8,128)(2,1)S(1)}, u32[]{:S(2)}, u32[]{:S(2)}) collective-permute-start(bf16[128,2048]{1,0:T(8,128)(2,1)S(1)} %get-tuple-element.330), channel_id=1, source_target_pairs={{3,2},{1,0},{2,1},{7,6},{5,4},{6,5},{11,10},{9,8},{10,9},{15,14},{... | collective-permute-start | bytes 1572872 | tf_op jit(solution)/shard_map/ppermute | solution.py:669
  151.8 12.0 %collective-permute-start.19 = (bf16[128,2048]{1,0:T(8,128)(2,1)S(1)}, bf16[128,2048]{1,0:T(8,128)(2,1)S(1)}, u32[]{:S(2)}, u32[]{:S(2)}) collective-permute-start(bf16[128,2048]{1,0:T(8,128)(2,1)S(1)} %select_add_fusion.41), channel_id=1, source_target_pairs={{0,1},{2,3},{1,2},{4,5},{6,7},{5,6},{8,9},{10,11},{9,10},{12,13},{... | collective-permute-start | bytes 1572872 | tf_op jit(solution)/shard_map/ppermute | solution.py:668
  164.3 11.8 %collective-permute-start.22 = (bf16[128,2048]{1,0:T(8,128)(2,1)S(1)}, bf16[128,2048]{1,0:T(8,128)(2,1)S(1)}, u32[]{:S(2)}, u32[]{:S(2)}) collective-permute-start(bf16[128,2048]{1,0:T(8,128)(2,1)S(1)} %get-tuple-element.333), channel_id=1, source_target_pairs={{2,1},{3,2},{1,0},{6,5},{7,6},{5,4},{10,9},{11,10},{9,8},{14,13},{... | collective-permute-start | bytes 1572872 | tf_op jit(solution)/shard_map/ppermute | solution.py:669
  165.6 11.7 %collective-permute-start.21 = (bf16[128,2048]{1,0:T(8,128)(2,1)S(1)}, bf16[128,2048]{1,0:T(8,128)(2,1)S(1)}, u32[]{:S(2)}, u32[]{:S(2)}) collective-permute-start(bf16[128,2048]{1,0:T(8,128)(2,1)S(1)} %select_add_fusion.39), channel_id=1, source_target_pairs={{1,2},{0,1},{2,3},{5,6},{4,5},{6,7},{9,10},{8,9},{10,11},{13,14},{... | collective-permute-start | bytes 1572872 | tf_op jit(solution)/shard_map/ppermute | solution.py:668
  177.7 11.5 %collective-permute-start.24 = (bf16[128,2048]{1,0:T(8,128)(2,1)S(1)}, bf16[128,2048]{1,0:T(8,128)(2,1)S(1)}, u32[]{:S(2)}, u32[]{:S(2)}) collective-permute-start(bf16[128,2048]{1,0:T(8,128)(2,1)S(1)} %get-tuple-element.336), channel_id=1, source_target_pairs={{1,0},{2,1},{3,2},{5,4},{6,5},{7,6},{9,8},{10,9},{11,10},{13,12},{... | collective-permute-start | bytes 1572872 | tf_op jit(solution)/shard_map/ppermute | solution.py:669
  180.9 11.9 %collective-permute-start.23 = (bf16[128,2048]{1,0:T(8,128)(2,1)S(1)}, bf16[128,2048]{1,0:T(8,128)(2,1)S(1)}, u32[]{:S(2)}, u32[]{:S(2)}) collective-permute-start(bf16[128,2048]{1,0:T(8,128)(2,1)S(1)} %select_add_fusion.37), channel_id=1, source_target_pairs={{2,3},{1,2},{0,1},{6,7},{5,6},{4,5},{10,11},{9,10},{8,9},{14,15},{... | collective-permute-start | bytes 1572872 | tf_op jit(solution)/shard_map/ppermute | solution.py:668
  194.0 27.1 %collective-permute-start.25 = (bf16[128,2048]{1,0:T(8,128)(2,1)}, bf16[128,2048]{1,0:T(8,128)(2,1)}, u32[]{:S(2)}, u32[]{:S(2)}) collective-permute-start(bf16[128,2048]{1,0:T(8,128)(2,1)} %get-tuple-element.341), channel_id=1, source_target_pairs={{2,3},{1,2},{0,1},{6,7},{5,6},{4,5},{10,11},{9,10},{8,9},{14,15},{... | collective-permute-start | bytes 1572872 | tf_op jit(solution)/shard_map/ppermute | solution.py:668
  199.2 21.9 %collective-permute-start.26 = (bf16[128,2048]{1,0:T(8,128)(2,1)}, bf16[128,2048]{1,0:T(8,128)(2,1)}, u32[]{:S(2)}, u32[]{:S(2)}) collective-permute-start(bf16[128,2048]{1,0:T(8,128)(2,1)} %get-tuple-element.342), channel_id=1, source_target_pairs={{1,0},{2,1},{3,2},{5,4},{6,5},{7,6},{9,8},{10,9},{11,10},{13,12},{... | collective-permute-start | bytes 1572872 | tf_op jit(solution)/shard_map/ppermute | solution.py:669
  224.5 30.5 %collective-permute-start.27 = (bf16[128,2048]{1,0:T(8,128)(2,1)}, bf16[128,2048]{1,0:T(8,128)(2,1)}, u32[]{:S(2)}, u32[]{:S(2)}) collective-permute-start(bf16[128,2048]{1,0:T(8,128)(2,1)} %get-tuple-element.352), channel_id=1, source_target_pairs={{0,1},{2,3},{1,2},{4,5},{6,7},{5,6},{8,9},{10,11},{9,10},{12,13},{... | collective-permute-start | bytes 1572872 | tf_op jit(solution)/shard_map/ppermute | solution.py:668
  229.8 25.1 %collective-permute-start.28 = (bf16[128,2048]{1,0:T(8,128)(2,1)}, bf16[128,2048]{1,0:T(8,128)(2,1)}, u32[]{:S(2)}, u32[]{:S(2)}) collective-permute-start(bf16[128,2048]{1,0:T(8,128)(2,1)} %get-tuple-element.353), channel_id=1, source_target_pairs={{3,2},{1,0},{2,1},{7,6},{5,4},{6,5},{11,10},{9,8},{10,9},{15,14},{... | collective-permute-start | bytes 1572872 | tf_op jit(solution)/shard_map/ppermute | solution.py:669
  254.9 298.8 %reduce-scatter.5.cloned.1.call-start = ((), (), s32[]{:S(2)}) async-start(), calls=%async_computation.6 | async-start | bytes 9437184 | tf_op jit(solution)/shard_map/reduce_scatter | solution.py:537
  256.8 25.6 %collective-permute-start.29 = (bf16[128,2048]{1,0:T(8,128)(2,1)S(1)}, bf16[128,2048]{1,0:T(8,128)(2,1)S(1)}, u32[]{:S(2)}, u32[]{:S(2)}) collective-permute-start(bf16[128,2048]{1,0:T(8,128)(2,1)S(1)} %get-tuple-element.361), channel_id=1, source_target_pairs={{1,2},{0,1},{2,3},{5,6},{4,5},{6,7},{9,10},{8,9},{10,11},{13,14},{... | collective-permute-start | bytes 1572872 | tf_op jit(solution)/shard_map/ppermute | solution.py:668
  261.6 36.5 %collective-permute-start.30 = (bf16[128,2048]{1,0:T(8,128)(2,1)S(1)}, bf16[128,2048]{1,0:T(8,128)(2,1)S(1)}, u32[]{:S(2)}, u32[]{:S(2)}) collective-permute-start(bf16[128,2048]{1,0:T(8,128)(2,1)S(1)} %get-tuple-element.362), channel_id=1, source_target_pairs={{2,1},{3,2},{1,0},{6,5},{7,6},{5,4},{10,9},{11,10},{9,8},{14,13},{... | collective-permute-start | bytes 1572872 | tf_op jit(solution)/shard_map/ppermute | solution.py:669
  298.8 23.3 %collective-permute-start.31 = (bf16[128,2048]{1,0:T(8,128)(2,1)S(1)}, bf16[128,2048]{1,0:T(8,128)(2,1)S(1)}, u32[]{:S(2)}, u32[]{:S(2)}) collective-permute-start(bf16[128,2048]{1,0:T(8,128)(2,1)S(1)} %get-tuple-element.370), channel_id=1, source_target_pairs={{2,3},{1,2},{0,1},{6,7},{5,6},{4,5},{10,11},{9,10},{8,9},{14,15},{... | collective-permute-start | bytes 1572872 | tf_op jit(solution)/shard_map/ppermute | solution.py:668
  301.5 20.6 %collective-permute-start.32 = (bf16[128,2048]{1,0:T(8,128)(2,1)S(1)}, bf16[128,2048]{1,0:T(8,128)(2,1)S(1)}, u32[]{:S(2)}, u32[]{:S(2)}) collective-permute-start(bf16[128,2048]{1,0:T(8,128)(2,1)S(1)} %get-tuple-element.371), channel_id=1, source_target_pairs={{1,0},{2,1},{3,2},{5,4},{6,5},{7,6},{9,8},{10,9},{11,10},{13,12},{... | collective-permute-start | bytes 1572872 | tf_op jit(solution)/shard_map/ppermute | solution.py:669
  338.5 368.4 %reduce-scatter.7.cloned.1.call-start = ((), (), s32[]{:S(2)}) async-start(), calls=%async_computation.7 | async-start | bytes 18874368 | tf_op jit(solution)/shard_map/reduce_scatter | solution.py:537
  341.9 24.0 %collective-permute-start.33 = (bf16[128,2048]{1,0:T(8,128)(2,1)S(1)}, bf16[128,2048]{1,0:T(8,128)(2,1)S(1)}, u32[]{:S(2)}, u32[]{:S(2)}) collective-permute-start(bf16[128,2048]{1,0:T(8,128)(2,1)S(1)} %copy-done.167), channel_id=1, source_target_pairs={{2,3},{1,2},{0,1},{6,7},{5,6},{4,5},{10,11},{9,10},{8,9},{14,15},{... | collective-permute-start | bytes 1572872 | tf_op jit(solution)/shard_map/ppermute | solution.py:668
  346.6 22.2 %collective-permute-start.34 = (bf16[128,2048]{1,0:T(8,128)(2,1)S(1)}, bf16[128,2048]{1,0:T(8,128)(2,1)S(1)}, u32[]{:S(2)}, u32[]{:S(2)}) collective-permute-start(bf16[128,2048]{1,0:T(8,128)(2,1)S(1)} %copy-done.166), channel_id=1, source_target_pairs={{1,0},{2,1},{3,2},{5,4},{6,5},{7,6},{9,8},{10,9},{11,10},{13,12},{... | collective-permute-start | bytes 1572872 | tf_op jit(solution)/shard_map/ppermute | solution.py:669
  397.0 323.8 %reduce-scatter.11.cloned.1.call-start = ((), (), s32[]{:S(2)}) async-start(), calls=%async_computation.9 | async-start | bytes 2359296 | tf_op jit(solution)/shard_map/reduce_scatter | solution.py:537
  397.7 13.7 %collective-permute-start.36 = (bf16[128,2048]{1,0:T(8,128)(2,1)}, bf16[128,2048]{1,0:T(8,128)(2,1)S(1)}, u32[]{:S(2)}, u32[]{:S(2)}) collective-permute-start(bf16[128,2048]{1,0:T(8,128)(2,1)} %get-tuple-element.396), channel_id=1, source_target_pairs={{3,2},{1,0},{2,1},{7,6},{5,4},{6,5},{11,10},{9,8},{10,9},{15,14},{... | collective-permute-start | bytes 1572872 | tf_op jit(solution)/shard_map/ppermute | solution.py:669
  399.0 16.3 %collective-permute-start.35 = (bf16[128,2048]{1,0:T(8,128)(2,1)}, bf16[128,2048]{1,0:T(8,128)(2,1)S(1)}, u32[]{:S(2)}, u32[]{:S(2)}) collective-permute-start(bf16[128,2048]{1,0:T(8,128)(2,1)} %select_add_fusion.25), channel_id=1, source_target_pairs={{0,1},{2,3},{1,2},{4,5},{6,7},{5,6},{8,9},{10,11},{9,10},{12,13},{... | collective-permute-start | bytes 1572872 | tf_op jit(solution)/shard_map/ppermute | solution.py:668
  417.6 13.1 %collective-permute-start.38 = (bf16[128,2048]{1,0:T(8,128)(2,1)}, bf16[128,2048]{1,0:T(8,128)(2,1)S(1)}, u32[]{:S(2)}, u32[]{:S(2)}) collective-permute-start(bf16[128,2048]{1,0:T(8,128)(2,1)} %get-tuple-element.403), channel_id=1, source_target_pairs={{2,1},{3,2},{1,0},{6,5},{7,6},{5,4},{10,9},{11,10},{9,8},{14,13},{... | collective-permute-start | bytes 1572872 | tf_op jit(solution)/shard_map/ppermute | solution.py:669
  419.1 15.8 %collective-permute-start.37 = (bf16[128,2048]{1,0:T(8,128)(2,1)}, bf16[128,2048]{1,0:T(8,128)(2,1)S(1)}, u32[]{:S(2)}, u32[]{:S(2)}) collective-permute-start(bf16[128,2048]{1,0:T(8,128)(2,1)} %select_add_fusion.23), channel_id=1, source_target_pairs={{1,2},{0,1},{2,3},{5,6},{4,5},{6,7},{9,10},{8,9},{10,11},{13,14},{... | collective-permute-start | bytes 1572872 | tf_op jit(solution)/shard_map/ppermute | solution.py:668
  437.2 11.8 %collective-permute-start.40 = (bf16[128,2048]{1,0:T(8,128)(2,1)S(1)}, bf16[128,2048]{1,0:T(8,128)(2,1)S(1)}, u32[]{:S(2)}, u32[]{:S(2)}) collective-permute-start(bf16[128,2048]{1,0:T(8,128)(2,1)S(1)} %get-tuple-element.410), channel_id=1, source_target_pairs={{1,0},{2,1},{3,2},{5,4},{6,5},{7,6},{9,8},{10,9},{11,10},{13,12},{... | collective-permute-start | bytes 1572872 | tf_op jit(solution)/shard_map/ppermute | solution.py:669
  438.5 13.6 %collective-permute-start.39 = (bf16[128,2048]{1,0:T(8,128)(2,1)S(1)}, bf16[128,2048]{1,0:T(8,128)(2,1)S(1)}, u32[]{:S(2)}, u32[]{:S(2)}) collective-permute-start(bf16[128,2048]{1,0:T(8,128)(2,1)S(1)} %select_add_fusion.21), channel_id=1, source_target_pairs={{2,3},{1,2},{0,1},{6,7},{5,6},{4,5},{10,11},{9,10},{8,9},{14,15},{... | collective-permute-start | bytes 1572872 | tf_op jit(solution)/shard_map/ppermute | solution.py:668
  457.0 11.3 %collective-permute-start.42 = (bf16[128,2048]{1,0:T(8,128)(2,1)}, bf16[128,2048]{1,0:T(8,128)(2,1)S(1)}, u32[]{:S(2)}, u32[]{:S(2)}) collective-permute-start(bf16[128,2048]{1,0:T(8,128)(2,1)} %get-tuple-element.419), channel_id=1, source_target_pairs={{1,0},{2,1},{3,2},{5,4},{6,5},{7,6},{9,8},{10,9},{11,10},{13,12},{... | collective-permute-start | bytes 1572872 | tf_op jit(solution)/shard_map/ppermute | solution.py:669
  462.0 45.8 %collective-permute-start.47 = (f32[3,512]{1,0:T(4,128)S(1)}, f32[3,512]{1,0:T(4,128)S(1)}, u32[]{:S(2)}, u32[]{:S(2)}) collective-permute-start(f32[3,512]{1,0:T(4,128)S(1)} %pad_maximum_fusion.24), channel_id=1, source_target_pairs={{4,0},{8,4},{12,8},{16,12},{20,16},{24,20},{28,24},{5,1},{9,5},{13... | collective-permute-start | bytes 18440 | tf_op jit(solution)/shard_map/ppermute | solution.py:45
  469.9 13.8 %collective-permute-start.43 = (bf16[128,2048]{1,0:T(8,128)(2,1)S(1)}, bf16[128,2048]{1,0:T(8,128)(2,1)S(1)}, u32[]{:S(2)}, u32[]{:S(2)}) collective-permute-start(bf16[128,2048]{1,0:T(8,128)(2,1)S(1)} %get-tuple-element.433), channel_id=1, source_target_pairs={{2,3},{1,2},{0,1},{6,7},{5,6},{4,5},{10,11},{9,10},{8,9},{14,15},{... | collective-permute-start | bytes 1572872 | tf_op jit(solution)/shard_map/ppermute | solution.py:668
  472.5 15.3 %collective-permute-start.44 = (bf16[128,2048]{1,0:T(8,128)(2,1)S(1)}, bf16[128,2048]{1,0:T(8,128)(2,1)S(1)}, u32[]{:S(2)}, u32[]{:S(2)}) collective-permute-start(bf16[128,2048]{1,0:T(8,128)(2,1)S(1)} %get-tuple-element.434), channel_id=1, source_target_pairs={{1,0},{2,1},{3,2},{5,4},{6,5},{7,6},{9,8},{10,9},{11,10},{13,12},{... | collective-permute-start | bytes 1572872 | tf_op jit(solution)/shard_map/ppermute | solution.py:669
  490.7 12.5 %collective-permute-start.45 = (bf16[128,2048]{1,0:T(8,128)(2,1)S(1)}, bf16[128,2048]{1,0:T(8,128)(2,1)S(1)}, u32[]{:S(2)}, u32[]{:S(2)}) collective-permute-start(bf16[128,2048]{1,0:T(8,128)(2,1)S(1)} %get-tuple-element.447), channel_id=1, source_target_pairs={{0,1},{2,3},{1,2},{4,5},{6,7},{5,6},{8,9},{10,11},{9,10},{12,13},{... | collective-permute-start | bytes 1572872 | tf_op jit(solution)/shard_map/ppermute | solution.py:668
  492.9 14.5 %collective-permute-start.46 = (bf16[128,2048]{1,0:T(8,128)(2,1)S(1)}, bf16[128,2048]{1,0:T(8,128)(2,1)S(1)}, u32[]{:S(2)}, u32[]{:S(2)}) collective-permute-start(bf16[128,2048]{1,0:T(8,128)(2,1)S(1)} %get-tuple-element.448), channel_id=1, source_target_pairs={{3,2},{1,0},{2,1},{7,6},{5,4},{6,5},{11,10},{9,8},{10,9},{15,14},{... | collective-permute-start | bytes 1572872 | tf_op jit(solution)/shard_map/ppermute | solution.py:669
  510.3 11.9 %collective-permute-start.48 = (bf16[128,2048]{1,0:T(8,128)(2,1)S(1)}, bf16[128,2048]{1,0:T(8,128)(2,1)S(1)}, u32[]{:S(2)}, u32[]{:S(2)}) collective-permute-start(bf16[128,2048]{1,0:T(8,128)(2,1)S(1)} %get-tuple-element.461), channel_id=1, source_target_pairs={{1,2},{0,1},{2,3},{5,6},{4,5},{6,7},{9,10},{8,9},{10,11},{13,14},{... | collective-permute-start | bytes 1572872 | tf_op jit(solution)/shard_map/ppermute | solution.py:668
  512.9 13.4 %collective-permute-start.49 = (bf16[128,2048]{1,0:T(8,128)(2,1)S(1)}, bf16[128,2048]{1,0:T(8,128)(2,1)S(1)}, u32[]{:S(2)}, u32[]{:S(2)}) collective-permute-start(bf16[128,2048]{1,0:T(8,128)(2,1)S(1)} %get-tuple-element.462), channel_id=1, source_target_pairs={{2,1},{3,2},{1,0},{6,5},{7,6},{5,4},{10,9},{11,10},{9,8},{14,13},{... | collective-permute-start | bytes 1572872 | tf_op jit(solution)/shard_map/ppermute | solution.py:669
  528.8 12.2 %collective-permute-start.50 = (bf16[128,2048]{1,0:T(8,128)(2,1)}, bf16[128,2048]{1,0:T(8,128)(2,1)}, u32[]{:S(2)}, u32[]{:S(2)}) collective-permute-start(bf16[128,2048]{1,0:T(8,128)(2,1)} %get-tuple-element.482), channel_id=1, source_target_pairs={{2,3},{1,2},{0,1},{6,7},{5,6},{4,5},{10,11},{9,10},{8,9},{14,15},{... | collective-permute-start | bytes 1572872 | tf_op jit(solution)/shard_map/ppermute | solution.py:668
  532.5 13.5 %collective-permute-start.51 = (bf16[128,2048]{1,0:T(8,128)(2,1)}, bf16[128,2048]{1,0:T(8,128)(2,1)}, u32[]{:S(2)}, u32[]{:S(2)}) collective-permute-start(bf16[128,2048]{1,0:T(8,128)(2,1)} %get-tuple-element.483), channel_id=1, source_target_pairs={{1,0},{2,1},{3,2},{5,4},{6,5},{7,6},{9,8},{10,9},{11,10},{13,12},{... | collective-permute-start | bytes 1572872 | tf_op jit(solution)/shard_map/ppermute | solution.py:669
  553.7 12.4 %collective-permute-start.53 = (bf16[128,2048]{1,0:T(8,128)(2,1)}, bf16[128,2048]{1,0:T(8,128)(2,1)S(1)}, u32[]{:S(2)}, u32[]{:S(2)}) collective-permute-start(bf16[128,2048]{1,0:T(8,128)(2,1)} %get-tuple-element.508), channel_id=1, source_target_pairs={{1,0},{2,1},{3,2},{5,4},{6,5},{7,6},{9,8},{10,9},{11,10},{13,12},{... | collective-permute-start | bytes 1572872 | tf_op jit(solution)/shard_map/ppermute | solution.py:669
  555.0 14.1 %collective-permute-start.52 = (bf16[128,2048]{1,0:T(8,128)(2,1)}, bf16[128,2048]{1,0:T(8,128)(2,1)S(1)}, u32[]{:S(2)}, u32[]{:S(2)}) collective-permute-start(bf16[128,2048]{1,0:T(8,128)(2,1)} %select_add_fusion.15), channel_id=1, source_target_pairs={{2,3},{1,2},{0,1},{6,7},{5,6},{4,5},{10,11},{9,10},{8,9},{14,15},{... | collective-permute-start | bytes 1572872 | tf_op jit(solution)/shard_map/ppermute | solution.py:668
  570.4 12.4 %collective-permute-start.55 = (bf16[128,2048]{1,0:T(8,128)(2,1)}, bf16[128,2048]{1,0:T(8,128)(2,1)S(1)}, u32[]{:S(2)}, u32[]{:S(2)}) collective-permute-start(bf16[128,2048]{1,0:T(8,128)(2,1)} %select_add_fusion.13), channel_id=1, source_target_pairs={{0,1},{2,3},{1,2},{4,5},{6,7},{5,6},{8,9},{10,11},{9,10},{12,13},{... | collective-permute-start | bytes 1572872 | tf_op jit(solution)/shard_map/ppermute | solution.py:668
  573.1 11.4 %collective-permute-start.56 = (bf16[128,2048]{1,0:T(8,128)(2,1)}, bf16[128,2048]{1,0:T(8,128)(2,1)}, u32[]{:S(2)}, u32[]{:S(2)}) collective-permute-start(bf16[128,2048]{1,0:T(8,128)(2,1)} %get-tuple-element.514), channel_id=1, source_target_pairs={{3,2},{1,0},{2,1},{7,6},{5,4},{6,5},{11,10},{9,8},{10,9},{15,14},{... | collective-permute-start | bytes 1572872 | tf_op jit(solution)/shard_map/ppermute | solution.py:669
  578.7 147.2 %reduce-scatter.9.cloned.1.call-start = ((), (), s32[]{:S(2)}) async-start(), calls=%async_computation.8 | async-start | bytes 7077888 | tf_op jit(solution)/shard_map/reduce_scatter | solution.py:537
  592.9 11.7 %collective-permute-start.59 = (bf16[128,2048]{1,0:T(8,128)(2,1)S(1)}, bf16[128,2048]{1,0:T(8,128)(2,1)S(1)}, u32[]{:S(2)}, u32[]{:S(2)}) collective-permute-start(bf16[128,2048]{1,0:T(8,128)(2,1)S(1)} %select_add_fusion.11), channel_id=1, source_target_pairs={{1,2},{0,1},{2,3},{5,6},{4,5},{6,7},{9,10},{8,9},{10,11},{13,14},{... | collective-permute-start | bytes 1572872 | tf_op jit(solution)/shard_map/ppermute | solution.py:668
  605.5 17.7 %collective-permute-start.63 = (f32[8,512]{1,0:T(8,128)S(1)}, f32[8,512]{1,0:T(8,128)S(1)}, u32[]{:S(2)}, u32[]{:S(2)}) collective-permute-start(f32[8,512]{1,0:T(8,128)S(1)} %slice.830), channel_id=1, source_target_pairs={{0,1},{1,0},{2,3},{3,2},{4,5},{5,4},{6,7},{7,6},{8,9},{9,8},{10,11... | collective-permute-start | bytes 49160 | tf_op jit(solution)/shard_map/ppermute | solution.py:54
  608.0 15.3 %collective-permute-start.62 = (bf16[128,2048]{1,0:T(8,128)(2,1)}, bf16[128,2048]{1,0:T(8,128)(2,1)S(1)}, u32[]{:S(2)}, u32[]{:S(2)}) collective-permute-start(bf16[128,2048]{1,0:T(8,128)(2,1)} %get-tuple-element.526), channel_id=1, source_target_pairs={{1,0},{2,1},{3,2},{5,4},{6,5},{7,6},{9,8},{10,9},{11,10},{13,12},{... | collective-permute-start | bytes 1572872 | tf_op jit(solution)/shard_map/ppermute | solution.py:669
  618.4 12.0 %collective-permute-start.61 = (bf16[128,2048]{1,0:T(8,128)(2,1)}, bf16[128,2048]{1,0:T(8,128)(2,1)S(1)}, u32[]{:S(2)}, u32[]{:S(2)}) collective-permute-start(bf16[128,2048]{1,0:T(8,128)(2,1)} %select_add_fusion.6), channel_id=1, source_target_pairs={{2,3},{1,2},{0,1},{6,7},{5,6},{4,5},{10,11},{9,10},{8,9},{14,15},{... | collective-permute-start | bytes 1572872 | tf_op jit(solution)/shard_map/ppermute | solution.py:668
  632.2 15.0 %collective-permute-start.65 = (bf16[128,2048]{1,0:T(8,128)(2,1)S(1)}, bf16[128,2048]{1,0:T(8,128)(2,1)S(1)}, u32[]{:S(2)}, u32[]{:S(2)}) collective-permute-start(bf16[128,2048]{1,0:T(8,128)(2,1)S(1)} %get-tuple-element.529), channel_id=1, source_target_pairs={{1,0},{2,1},{3,2},{5,4},{6,5},{7,6},{9,8},{10,9},{11,10},{13,12},{... | collective-permute-start | bytes 1572872 | tf_op jit(solution)/shard_map/ppermute | solution.py:669
  633.5 13.7 %collective-permute-start.66 = (f32[8,512]{1,0:T(8,128)S(1)}, f32[8,512]{1,0:T(8,128)S(1)}, u32[]{:S(2)}, u32[]{:S(2)}) collective-permute-start(f32[8,512]{1,0:T(8,128)S(1)} %slice.833), channel_id=1, source_target_pairs={{0,2},{1,3},{2,0},{3,1},{4,6},{5,7},{6,4},{7,5},{8,10},{9,11},{10,... | collective-permute-start | bytes 49160 | tf_op jit(solution)/shard_map/ppermute | solution.py:54
  638.1 12.2 %collective-permute-start.64 = (bf16[128,2048]{1,0:T(8,128)(2,1)S(1)}, bf16[128,2048]{1,0:T(8,128)(2,1)S(1)}, u32[]{:S(2)}, u32[]{:S(2)}) collective-permute-start(bf16[128,2048]{1,0:T(8,128)(2,1)S(1)} %get-tuple-element.528), channel_id=1, source_target_pairs={{2,3},{1,2},{0,1},{6,7},{5,6},{4,5},{10,11},{9,10},{8,9},{14,15},{... | collective-permute-start | bytes 1572872 | tf_op jit(solution)/shard_map/ppermute | solution.py:668
  651.2 13.2 %collective-permute-start.68 = (bf16[128,2048]{1,0:T(8,128)(2,1)S(1)}, bf16[128,2048]{1,0:T(8,128)(2,1)S(1)}, u32[]{:S(2)}, u32[]{:S(2)}) collective-permute-start(bf16[128,2048]{1,0:T(8,128)(2,1)S(1)} %get-tuple-element.532), channel_id=1, source_target_pairs={{1,0},{2,1},{3,2},{5,4},{6,5},{7,6},{9,8},{10,9},{11,10},{13,12},{... | collective-permute-start | bytes 1572872 | tf_op jit(solution)/shard_map/ppermute | solution.py:669
  652.5 12.2 %collective-permute-start.67 = (bf16[128,2048]{1,0:T(8,128)(2,1)S(1)}, bf16[128,2048]{1,0:T(8,128)(2,1)S(1)}, u32[]{:S(2)}, u32[]{:S(2)}) collective-permute-start(bf16[128,2048]{1,0:T(8,128)(2,1)S(1)} %get-tuple-element.531), channel_id=1, source_target_pairs={{2,3},{1,2},{0,1},{6,7},{5,6},{4,5},{10,11},{9,10},{8,9},{14,15},{... | collective-permute-start | bytes 1572872 | tf_op jit(solution)/shard_map/ppermute | solution.py:668
  666.4 18.1 %collective-permute-start.70 = (bf16[128,2048]{1,0:T(8,128)(2,1)S(1)}, bf16[128,2048]{1,0:T(8,128)(2,1)S(1)}, u32[]{:S(2)}, u32[]{:S(2)}) collective-permute-start(bf16[128,2048]{1,0:T(8,128)(2,1)S(1)} %get-tuple-element.534), channel_id=1, source_target_pairs={{1,0},{2,1},{5,4},{6,5},{9,8},{10,9},{13,12},{14,13},{17,16},{18,1... | collective-permute-start | bytes 1572872 | tf_op jit(solution)/shard_map/ppermute | solution.py:669
  718.1 12.8 %collective-permute-start.77 = (bf16[128,2048]{1,0:T(8,128)(2,1)S(1)}, bf16[128,2048]{1,0:T(8,128)(2,1)}, u32[]{:S(2)}, u32[]{:S(2)}) collective-permute-start(bf16[128,2048]{1,0:T(8,128)(2,1)S(1)} %collective-permute-done.75), channel_id=1, source_target_pairs={{2,3},{1,2},{6,7},{5,6},{10,11},{9,10},{14,15},{13,14},{18,19},{17... | collective-permute-start | bytes 1572872 | tf_op jit(solution)/shard_map/ppermute | solution.py:668
  719.5 26.6 %collective-permute-start.78 = (bf16[128,2048]{1,0:T(8,128)(2,1)}, bf16[128,2048]{1,0:T(8,128)(2,1)}, u32[]{:S(2)}, u32[]{:S(2)}) collective-permute-start(bf16[128,2048]{1,0:T(8,128)(2,1)} %collective-permute-done.76), channel_id=1, source_target_pairs={{1,0},{2,1},{5,4},{6,5},{9,8},{10,9},{13,12},{14,13},{17,16},{18,1... | collective-permute-start | bytes 1572872 | tf_op jit(solution)/shard_map/ppermute | solution.py:669
  746.1 11.4 %collective-permute-start.79 = (bf16[128,2048]{1,0:T(8,128)(2,1)}, bf16[128,2048]{1,0:T(8,128)(2,1)}, u32[]{:S(2)}, u32[]{:S(2)}) collective-permute-start(bf16[128,2048]{1,0:T(8,128)(2,1)} %collective-permute-done.78), channel_id=1, source_target_pairs={{1,0},{5,4},{9,8},{13,12},{17,16},{21,20},{25,24},{29,28}} | collective-permute-start | bytes 1572872 | tf_op jit(solution)/shard_map/ppermute | solution.py:669
  (228 other events, 2486.5 us)
Sparse Core Ops, SparseCore 0:
  10.5 49.9 all-gather.3
  62.9 126.4 all-gather.5
  255.0 111.8 all-reduce.1
  371.2 73.2 reduce-scatter.4
  448.0 115.9 reduce-scatter.6
  578.8 40.9 reduce-scatter.10
  624.2 61.7 reduce-scatter.8
where the time goes:
time: 792 us; the launch traced here: 777 us
  waiting for transfers between devices  253 us (32%)
  starting transfers between devices  185 us (23%)
  other arithmetic  126 us (16%)
  matrix products  77.6 us (10%)
  Pallas kernels  77 us (10%)
  local copies, waits for them, and re-layouts  39.9 us (5%)
  between operations  17.9 us (2%)
    ppermute x32, waiting for transfers between devices, run_slots(): lax.ppermute(send_down, 'tp', [(p, p - 1) for p in down_options])  138 us
    ppermute x32, starting transfers between devices, run_slots(): up[slot] = lax.ppermute(send_up, 'tp', [(p, p + 1) for p in up_options])  118 us
    ppermute x32, waiting for transfers between devices, run_slots(): up[slot] = lax.ppermute(send_up, 'tp', [(p, p + 1) for p in up_options])  84.6 us
    pallas_call x4, Pallas kernels, feed_forward(): pl.pallas_call(feed_kernel, grid=(hidden // tile,), in_specs=[whole, whol...  76.5 us
    add x29, other arithmetic, run_slots(): send_down + down[slot - 1]  43.5 us
    ppermute x32, starting transfers between devices, run_slots(): lax.ppermute(send_down, 'tp', [(p, p - 1) for p in down_options])  42.9 us
    unnamed x417, local copies, waits for them, and re-layouts  27.4 us
    dot_general x3, matrix products, dot_left(): lax.dot_general(left, right, (((0,), (0,)), ((), ())), preferred_element_...  24.1 us
  transfers between devices with their start and end apart: 88, of which 48 were waited for; matrix products, arithmetic and copies ran while one was open for 27% of the time, Pallas kernels for 10%

commit v1 on v0

--- a/solution.py
+++ b/solution.py
@@ -163,8 +163,12 @@
     return extra
 
 
+def light(elements):
+    return pl.CostEstimate(flops=elements, bytes_accessed=elements, transcendentals=0)
+
+
 def feed_kernel(
-    normed, grads, weights, act, grad_both, out, grad_normed, out_sum, grad_sum
+    normed, grads, weights, act, grad_gate, grad_up, out, grad_normed, out_sum, grad_sum
 ):
     tile = pl.program_id(0)
     size = weights.shape[3]
@@ -178,8 +182,8 @@
     gate_here = (grad_act * up * sig * (1.0 + gate * (1.0 - sig))).astype(bf16)
     up_here = (grad_act * swish).astype(bf16)
     act[...] = act_here
-    grad_both[0] = gate_here
-    grad_both[1] = up_here
+    grad_gate[...] = gate_here
+    grad_up[...] = up_here
     out_here = dot_right(act_here, down_w)
     grad_here = dot_right(gate_here, gate_w) + dot_right(up_here, up_w)
 
@@ -206,21 +210,22 @@
     whole = pl.BlockSpec((rows, width), lambda j: (0, 0))
     block = pl.BlockSpec((devices, 3, each, tile), lambda j: (0, 0, 0, j))
     part = pl.BlockSpec((rows, tile), lambda j: (0, j))
-    both = pl.BlockSpec((2, rows, tile), lambda j: (0, 0, j))
+    wide = jax.ShapeDtypeStruct((rows, hidden), bf16)
     narrow = jax.ShapeDtypeStruct((rows, width), bf16)
     return pl.pallas_call(
         feed_kernel,
         grid=(hidden // tile,),
         in_specs=[whole, whole, block],
-        out_specs=[part, both, whole, whole],
+        out_specs=[part, part, part, whole, whole],
         out_shape=[
-            jax.ShapeDtypeStruct((rows, hidden), bf16),
-            jax.ShapeDtypeStruct((2, rows, hidden), bf16),
+            wide,
+            wide,
+            wide,
             narrow,
             narrow,
         ],
         scratch_shapes=[pltpu.VMEM((rows, width), f32)] * 2,
-        compiler_params=pltpu.CompilerParams(vmem_limit_bytes=40 * 2**20),
+        compiler_params=pltpu.CompilerParams(vmem_limit_bytes=36 * 2**20),
         cost_estimate=pl.CostEstimate(
             flops=12 * rows * width * hidden,
             bytes_accessed=6 * width * hidden + 10 * rows * hidden,
@@ -229,39 +234,75 @@
     )(normed, grads, weights)
 
 
+def mixer_kernel(left, right, left_last, right_last, out):
+    last = pl.num_programs(0) - 1
+
+    @pl.when(pl.program_id(0) < last)
+    def _():
+        out[...] = dot_left(left[...], right[...]).astype(bf16)
+
+    @pl.when(pl.program_id(0) == last)
+    def _():
+        out[...] = dot_left(left_last[...], right_last[...]).astype(bf16)
+
+
+def mixer_products(left, right, left_last, right_last):
+    count, width = left.shape
+    tile = right_last.shape[1]
+    tiles = right.shape[1] // tile
+    whole = pl.BlockSpec((count, width), lambda j: (0, 0), pipeline_mode=pl.Buffered(1))
+    return pl.pallas_call(
+        mixer_kernel,
+        grid=(tiles + 1,),
+        in_specs=[
+            whole,
+            pl.BlockSpec((count, tile), lambda j: (0, jnp.minimum(j, tiles - 1))),
+            whole,
+            pl.BlockSpec((count, tile), lambda j: (0, 0)),
+        ],
+        out_specs=pl.BlockSpec((width, tile), lambda j: (0, j)),
+        out_shape=jax.ShapeDtypeStruct((width, (tiles + 1) * tile), bf16),
+        compiler_params=pltpu.CompilerParams(vmem_limit_bytes=24 * 2**20),
+        cost_estimate=light(count * tile),
+    )(left, right, left_last, right_last)
+
+
 class Step:
     def __init__(self, name, needs, gives, run, cost, rank, lasts):
         self.name, self.needs, self.gives = name, needs, gives
         self.run, self.cost, self.rank, self.lasts = run, cost, rank, lasts
-        self.alone = name.startswith("small")
+        self.alone = name.startswith(("small", "call"))
 
 
 class Sum:
-    def __init__(self, name, part, finish, own, joined, rank):
+    def __init__(self, name, part, finish, own, joined, rank, back_rank):
         self.name, self.part, self.finish = name, part, finish
-        self.own, self.joined, self.rank = own, joined, rank
-        self.start = None
+        self.own, self.joined, self.rank, self.back_rank = own, joined, rank, back_rank
+        self.start = self.back = None
 
 
 def plan(steps, sums, line, budget):
     slot_of = {}
     todo = list(steps)
     waiting = list(sums)
-    taken = set()
-    finishing = {}
-    arriving = {}
+    finishing, returning, arriving = {}, [], {}
     slots = []
-    slot = 0
-    while todo or waiting or any(s >= slot for s in arriving):
-        for one in sorted(waiting, key=lambda q: q.rank):
-            if one.part in slot_of and slot_of[one.part] < slot:
-                if slot not in taken and slot + line not in taken:
-                    taken.update((slot, slot + line))
-                    one.start = slot
-                    waiting.remove(one)
-                    finishing.setdefault(slot + line - 1, []).append(one)
-                    arriving.setdefault(slot + 2 * line - 1, []).append(one)
-                    break
+    slot = busy = 0
+    while todo or waiting or returning or any(s >= slot for s in arriving):
+        ready = [one for one in waiting if slot_of.get(one.part, slot) < slot]
+        back = [one for one in returning if slot >= one.start + line]
+        turn = [(one.rank, one) for one in ready] + [(one.back_rank, one) for one in back]
+        if turn:
+            one = min(turn, key=lambda t: t[0])[1]
+            if one in ready:
+                one.start = slot
+                waiting.remove(one)
+                returning.append(one)
+                finishing.setdefault(slot + line - 1, []).append(one)
+            else:
+                one.back = slot
+                returning.remove(one)
+                arriving.setdefault(slot + line - 1, []).append(one)
         here = []
         spent = 0.0
         for one in finishing.get(slot, []):
@@ -277,20 +318,23 @@
         while again:
             again = False
             for step in sorted(todo, key=lambda s: s.rank):
-                ready = all(name in slot_of for name in step.needs)
-                if step.alone:
-                    ready = ready and all(slot_of[name] < slot for name in step.needs)
-                if not taken:
+                newest = max((slot_of.get(name, slot + 1) for name in step.needs), default=-1)
+                ready = newest < slot if step.alone else newest <= slot
+                if len(waiting) == len(sums):
                     fits = spent + step.cost <= 7.0
                 elif step.rank[0] >= 5:
-                    fits = spent <= 6.0
+                    fits = spent <= 6.0 or spent + step.cost <= budget
                 else:
-                    fits = spent + step.cost <= budget
+                    fits = spent + step.cost <= budget or step.cost <= 3.0
+                    fits = fits or (spent <= 4.0 and step.cost > budget)
                 if ready and (spent == 0.0 or fits):
                     here.append(step)
                     todo.remove(step)
                     spent += step.cost
-                    slot_of.update({name: slot for name in step.gives})
+                    if step.lasts:
+                        step.until = busy = max(busy, slot + 1) + step.lasts
+                    until = step.until if step.lasts else slot
+                    slot_of.update({name: until for name in step.gives})
                     again = True
                     break
         slots.append(here)
@@ -414,14 +458,14 @@
             return hidden, inverse, (hidden * inverse * gain_two).astype(bf16)
 
         add(f"first{c}", [f"one{c}_sum"], [f"hid{c}", f"inv{c}", f"n2own{c}"], 2.0, (1, c))(run)
-        sums.append(Sum(f"one{c}", f"mixed{c}", f"first{c}", f"n2own{c}", f"n2{c}", (0, c)))
+        sums.append(Sum(f"one{c}", f"mixed{c}", f"first{c}", f"n2own{c}", f"n2{c}", (0, c), (0.5, c)))
 
     def feed(c):
         def run(e):
             grads = out_grad[c * rows : (c + 1) * rows]
             return feed_forward(e[f"n2{c}"], grads, feed_full)
 
-        gives = [f"act{c}", f"gb{c}", f"fo{c}", f"gn2{c}"]
+        gives = [f"act{c}", f"gg{c}", f"gu{c}", f"fo{c}", f"gn2{c}"]
         add(f"feed{c}", [f"n2{c}"], gives, 22.0, (2, c))(run)
 
     def second(c):
@@ -436,27 +480,27 @@
 
         gives = [f"gh{c}", f"gmown{c}", f"g2{c}"]
         add(f"second{c}", [f"two{c}_sum", f"hid{c}", f"inv{c}"], gives, 3.0, (1, c))(run)
-        sums.append(Sum(f"two{c}", f"gn2{c}", f"second{c}", f"gmown{c}", f"gm{c}", (1, c)))
-
-    def third(first, last):
-        def run(e):
+        sums.append(Sum(f"two{c}", f"gn2{c}", f"second{c}", f"gmown{c}", f"gm{c}", (1, c), (1.5, c)))
+
+    def third(last):
+        def run_part(e):
             blocks = []
-            for c in range(first, last):
+            for c in range(last):
                 part = e[f"fo{c}"].astype(f32)
                 top = jnp.where(place == line - 1, e[f"hid{c}"], 0.0)
                 bottom = jnp.where(place == 0, e[f"hid{c}"], 0.0)
                 blocks += [part[:half] + top, part[half:] + bottom]
             return (lax.psum(jnp.concatenate(blocks, axis=0).astype(bf16), "tp"),)
 
-        needs = [f"{n}{c}" for n in ("fo", "hid") for c in range(first, last)]
-        add(f"third{first}", needs, [f"out{first}"], 3.0, (2.5, first), 6)(run)
+        needs = [f"{n}{c}" for n in ("fo", "hid") for c in range(last)]
+        add("third0", needs, ["out0"], 3.0, (2.5, 0), 5)(run_part)
 
     def third_line(c):
         def run(e):
             return ((e[f"hid{c}"] + e[f"three{c}_sum"]).astype(bf16),)
 
         add(f"third{c}", [f"three{c}_sum", f"hid{c}"], [f"outown{c}"], 1.0, (1, c))(run)
-        sums.append(Sum(f"three{c}", f"fo{c}", f"third{c}", f"outown{c}", f"out{c}", (3, c)))
+        sums.append(Sum(f"three{c}", f"fo{c}", f"third{c}", f"outown{c}", f"out{c}", (3, c), (5, c)))
 
     def back(c):
         def run_a(e):
@@ -515,7 +559,7 @@
             return (grad_tokens.astype(bf16),)
 
         add(f"fourth{c}", [f"four{c}_sum", f"gh{c}"], [f"gtown{c}"], 3.0, (1, c))(run)
-        sums.append(Sum(f"four{c}", f"gn1{c}", f"fourth{c}", f"gtown{c}", f"gt{c}", (2, c)))
+        sums.append(Sum(f"four{c}", f"gn1{c}", f"fourth{c}", f"gtown{c}", f"gt{c}", (2, c), (4, c)))
 
     for c in range(chunks):
         mix(c)
@@ -526,34 +570,40 @@
         back(c)
         fourth(c)
 
-    third(0, chunks // 2)
+    third(chunks // 2)
     for c in range(chunks // 2, chunks):
         third_line(c)
 
     def joined(e, name):
         return jnp.concatenate([e[f"{name}{c}"] for c in range(chunks)], axis=0)
 
-    def scattered(part, dim):
-        return lax.psum_scatter(part.astype(bf16), "seq", scatter_dimension=dim, tiled=True)
-
     def names(*kinds):
         return [f"{kind}{c}" for kind in kinds for c in range(chunks)]
 
-    add("down_grad", names("act"), ["down_grad"], 12.0, (5, 0), 5)(
-        lambda e: (scattered(dot_left(joined(e, "act"), out_grad), 1),)
-    )
-    def feed_grad(e):
-        both = jnp.concatenate([e[f"gb{c}"] for c in range(chunks)], axis=1)
-        part = jnp.einsum("td,ktf->kdf", joined(e, "n2"), both, preferred_element_type=f32)
-        return (scattered(part, 1),)
-
-    add("feed_grad", names("n2", "gb"), ["feed_grad"], 22.0, (5, 1), 9)(feed_grad)
-    add("out_grad", names("gated", "gm"), ["out_proj_grad"], 5.0, (5, 3), 3)(
-        lambda e: (scattered(dot_left(joined(e, "gated"), joined(e, "gm")), 1),)
-    )
-    add("in_grad", names("gp"), ["in_grad"], 10.0, (5, 4), 4)(
-        lambda e: (scattered(dot_left(normed_one, joined(e, "gp")), 0),)
-    )
+    def scattered_sum(name, needs, run, cost, order, dim, lasts):
+        add(f"{name}_part", needs, [f"{name}_part"], cost, (5, order))(run)
+
+        def call(e):
+            return (lax.psum_scatter(e[f"{name}_part"], "seq", scatter_dimension=dim, tiled=True),)
+
+        add(f"call_{name}", [f"{name}_part"], [name], 0.0, (2.6, 9 + order), lasts)(call)
+
+    def down_part(e):
+        return (dot_left(joined(e, "act"), out_grad).astype(bf16),)
+
+    def gate_part(e):
+        return (dot_left(joined(e, "n2"), joined(e, "gg")).astype(bf16),)
+
+    def up_part(e):
+        return (dot_left(joined(e, "n2"), joined(e, "gu")).astype(bf16),)
+
+    def mixer_part(e):
+        return (mixer_products(normed_one, joined(e, "gp"), joined(e, "gm"), joined(e, "gated")),)
+
+    scattered_sum("down_grad", names("act"), down_part, 12.0, 0, 1, 4)
+    scattered_sum("gate_grad", names("n2", "gg"), gate_part, 11.0, 1, 0, 4)
+    scattered_sum("up_grad", names("n2", "gu"), up_part, 11.0, 1.5, 0, 4)
+    scattered_sum("mixer_grad", names("gm", "gated", "gp"), mixer_part, 18.0, 2, 0, 4)
 
     def total(e, kind):
         return sum(e[f"{kind}{c}"] for c in range(chunks))
@@ -578,24 +628,50 @@
             add(f"small{turn + 1}", [f"small{turn}"], [f"small{turn + 1}"], 2.0, (4, 10))(run)
             turn += 1
 
-    slots = plan(steps, sums, line, 30.0)
+    def rows_put(name, needs, first, step):
+        def run(e):
+            block = e[needs[0]].astype(f32 if name == "tokens_grad" else bf16)
+            if len(needs) == 1:
+                return (jnp.pad(block, ((0, count - block.shape[0]), (0, 0))),)
+            return (lax.dynamic_update_slice(e[needs[1]], block, (first, 0)),)
+
+        add(f"{name}_{step}", needs, [f"{name}{step}"], 2.0, (4.6, step))(run)
+
+    for c in range(chunks):
+        so_far = [f"tokens_grad{c - 1}"] if c else []
+        rows_put("tokens_grad", [f"gt{c}"] + so_far, c * rows, c)
+    rows_put("block_out", ["out0"], 0, 0)
+    for c in range(chunks // 2, chunks):
+        step = c - chunks // 2 + 1
+        rows_put("block_out", [f"out{c}", f"block_out{step - 1}"], c * rows, step)
+
+    def widened(name):
+        add(f"{name}_wide", [f"{name}_grad"], [f"{name}_wide"], 2.0, (4.7, 0))(
+            lambda e: (e[f"{name}_grad"].astype(f32),)
+        )
+
+    for name in ("down", "gate", "up"):
+        widened(name)
+
+    def mixer_wide(e):
+        mixer_grad = e["mixer_grad"].astype(f32)
+        return mixer_grad[:, : 3 * inner].reshape(in_weight.shape), mixer_grad[:, 3 * inner :].T
+
+    add("mixer_wide", ["mixer_grad"], ["in_wide", "out_wide"], 3.0, (4.7, 1))(mixer_wide)
+
+    slots = plan(steps, sums, line, 16.0)
     run_slots(slots, sums, env, line, place, half)
-
-    in_grad = env["in_grad"].astype(f32).reshape(in_weight.shape)
-    out_proj_grad = env["out_proj_grad"].astype(f32)
-    gate_grad, up_grad = env["feed_grad"].astype(f32)
-    down_grad = env["down_grad"].astype(f32)
 
     gains = env[f"small{turn}"][:-3].reshape(2, width)
     return (
-        jnp.concatenate([env["out0"]] + [env[f"out{c}"] for c in range(chunks // 2, chunks)], axis=0),
-        jnp.concatenate([env[f"gt{c}"].astype(f32) for c in range(chunks)], axis=0),
-        in_grad,
+        env[f"block_out{chunks - chunks // 2}"],
+        env[f"tokens_grad{chunks - 1}"],
+        env["in_wide"],
         env[f"small{turn}"][-3:],
-        out_proj_grad,
-        gate_grad,
-        up_grad,
-        down_grad,
+        env["out_wide"],
+        env["gate_wide"],
+        env["up_wide"],
+        env["down_wide"],
         gains[0],
         gains[1],
     )
@@ -604,7 +680,7 @@
 def run_slots(slots, sums, env, line, place, half):
     up, down = {}, {}
     last = line - 1
-    fresh, later, busy_until = [], {}, 0
+    fresh, later = [], {}
     awaited = f"head{chunks}"
 
     def chosen(options):
@@ -619,14 +695,12 @@
     def local_parts(slot):
         up_options, down_options = {}, {}
         for one in sums:
-            if one.start is None:
-                continue
             hop = slot - one.start
             if 0 <= hop < last:
                 part = env[one.part]
                 up_options[hop] = part[:half]
                 down_options[last - hop] = part[half:]
-            hop = slot - one.start - line
+            hop = slot - one.back
             if 0 <= hop < last:
                 value = env[one.own] if hop == 0 else None
                 up_options[hop] = down_options[last - hop] = value
@@ -649,16 +723,12 @@
                 send_up = up[slot - 1] if send_up is None else send_up + up[slot - 1]
                 send_down = down[slot - 1] if send_down is None else send_down + down[slot - 1]
         for one in sums:
-            if one.start is not None and slot == one.start + last:
-                part = env[one.part]
-                above = part[:half].astype(f32) + up[slot - 1].astype(f32)
-                below = part[half:].astype(f32) + down[slot - 1].astype(f32)
-                env[one.name + "_sum"] = jnp.where(place == last, above, below)
-            if one.start is not None and slot == one.start + line + last:
-                own, begin = env[one.own], one.start + line
+            if slot == one.back + last:
+                own, begin = env[one.own], one.back
                 top = {last: own} | {last - 1 - j: down[begin + j] for j in range(last)}
                 bottom = {0: own} | {1 + j: up[begin + j] for j in range(last)}
-                env[one.joined] = jnp.concatenate([chosen(top), chosen(bottom)], axis=0)
+                block = jnp.concatenate([chosen(top), chosen(bottom)], axis=0)
+                env[one.joined] = block
         keys = list(fresh) + later.get(slot, [])
         for step in steps:
             keys += [name for name in step.needs if name in env and name not in keys]
@@ -670,15 +740,20 @@
         elif tied:
             tied = lax.optimization_barrier(tied)
         env.update(zip(keys, tied))
+        for one in sums:
+            if slot == one.start + last:
+                part = env[one.part]
+                above = part[:half].astype(f32) + up[slot - 1].astype(f32)
+                below = part[half:].astype(f32) + down[slot - 1].astype(f32)
+                env[one.name + "_sum"] = jnp.where(place == last, above, below)
         fresh = []
         for step in steps:
             env.update(zip(step.gives, step.run(env)))
             if step.lasts:
-                busy_until = max(busy_until, slot + 1) + step.lasts
-                later.setdefault(busy_until, []).extend(step.gives)
+                later.setdefault(step.until, []).extend(step.gives)
             else:
                 fresh += [name for name in step.gives if name != awaited]
-        ready = tuple(mixed(options) for options in local_parts(slot + 1))
+        ready = lax.optimization_barrier(tuple(mixed(o) for o in local_parts(slot + 1)))
 
 
 def solution(mesh):

time: 792 us -> 747 us (0.943)
  waiting for transfers between devices: 253 us -> 171 us
  starting transfers between devices: 185 us -> 203 us
  local copies, waits for them, and re-layouts: 39.9 us -> 53.4 us
  Pallas kernels: 77 us -> 86.8 us
  matrix products: 77.6 us -> 67.9 us
  other arithmetic: 126 us -> 135 us
    ppermute x32 -> x30, waiting for transfers between devices: 138 us -> 91.2 us  [run_slots(): lax.ppermute(send_down, 'tp', [(p, p - 1) for p in down_options])]
    select_n x2 -> x46, other arithmetic: 2.01 us -> 35.6 us  [chosen(): value = jnp.where(place == position, option, value)]
    ppermute x32 -> x30, waiting for transfers between devices: 84.6 us -> 51.8 us  [run_slots(): up[slot] = lax.ppermute(send_up, 'tp', [(p, p + 1) for p in up_options])]
    add x29 -> x16, other arithmetic: 43.5 us -> 11.5 us  [run_slots(): send_down + down[slot - 1]]
    ppermute x32 -> x30, starting transfers between devices: 118 us -> 142 us  [run_slots(): up[slot] = lax.ppermute(send_up, 'tp', [(p, p + 1) for p in up_options])]
    dot_general x1 -> x0, matrix products: 22.4 us -> none  [feed_grad(): jnp.einsum('td,ktf->kdf', joined(e, 'n2'), both, preferred_element_type=f32)]
    select_n x14 -> x0, other arithmetic: 14.5 us -> none  [run_slots(): env[one.name + '_sum'] = jnp.where(place == last, above, below)]
    dot_general x3, matrix products: 24.1 us -> 35.1 us  [dot_left(): lax.dot_general(left, right, (((0,), (0,)), ((), ())), preferred_element_...]
  transfers between devices with their start and end apart: 88 -> 84, of which waited for: 48 -> 40; matrix products, arithmetic and copies ran while one was open for 27% -> 29% of each run, Pallas kernels for 10% -> 12%
where the time goes in v1:
time: 747 us; the launch traced here: 736 us
  starting transfers between devices  203 us (27%)
  waiting for transfers between devices  171 us (23%)
  other arithmetic  135 us (18%)
  Pallas kernels  86.8 us (12%)
  matrix products  67.9 us (9%)
  local copies, waits for them, and re-layouts  53.4 us (7%)
  between operations  18.6 us (2%)
    ppermute x30, starting transfers between devices, run_slots(): up[slot] = lax.ppermute(send_up, 'tp', [(p, p + 1) for p in up_options])  142 us
    ppermute x30, waiting for transfers between devices, run_slots(): lax.ppermute(send_down, 'tp', [(p, p - 1) for p in down_options])  91.2 us
    pallas_call x4, Pallas kernels, feed_forward(): pl.pallas_call(feed_kernel, grid=(hidden // tile,), in_specs=[whole, whol...  75.9 us
    ppermute x30, waiting for transfers between devices, run_slots(): up[slot] = lax.ppermute(send_up, 'tp', [(p, p + 1) for p in up_options])  51.8 us
    ppermute x30, starting transfers between devices, run_slots(): lax.ppermute(send_down, 'tp', [(p, p - 1) for p in down_options])  39.3 us
    unnamed x445, local copies, waits for them, and re-layouts  37.4 us
    select_n x46, other arithmetic, chosen(): value = jnp.where(place == position, option, value)  35.6 us
    dot_general x3, matrix products, dot_left(): lax.dot_general(left, right, (((0,), (0,)), ((), ())), preferred_element_...  35.1 us
  transfers between devices with their start and end apart: 84, of which 40 were waited for; matrix products, arithmetic and copies ran while one was open for 29% of the time, Pallas kernels for 12%

profile of v1, /device:TPU:0, one launch (start us, length us, event | category | flops | bytes accessed | tf_op | source)
XLA Modules:
  0.0 735.6 jit_solution(6694528662363520294)
XLA Ops:
  15.8 3.5 pad_maximum_fusion.1
  36.0 7.6 %collective-permute-done.3.refs_4_ = bf16[256,512]{1,0:T(8,128)(2,1)S(1)} collective-permute-done((bf16[256,512]{1,0:T(8,128)(2,1)S(1)}, bf16[256,512]{1,0:T(8,128)(2,1)S(1)}, u32[]{:S(2)}, u32[]{:S(2)}) %collective-permute-start.3) | collective-permute-done | bytes 262176 | tf_op jit(solution)/shard_map/ppermute | solution.py:131
  48.7 12.7 %all-gather.4.cloned.1.call-done = bf16[2048,1536]{0,1:T(8,128)(2,1)} async-done(((bf16[256,1536]{0,1:T(8,128)(2,1)}), bf16[2048,1536]{0,1:T(8,128)(2,1)}) %all-gather.4.cloned.1.call-update) | async-done | bytes 6291472 | tf_op jit(solution)/shard_map/all_gather | solution.py:392
  61.5 4.9 convolution_convert_fusion.3
  76.7 3.5 collective-permute-start.11
  85.5 6.3 collective-permute-done.11
  92.5 4.4 collective-permute-start.13
  101.3 6.5 collective-permute-done.13
  109.3 8.8 %collective-permute-start.15 = (bf16[128,2048]{1,0:T(8,128)(2,1)S(1)}, bf16[128,2048]{1,0:T(8,128)(2,1)S(1)}, u32[]{:S(2)}, u32[]{:S(2)}) collective-permute-start(bf16[128,2048]{1,0:T(8,128)(2,1)S(1)} %add.550), channel_id=1, source_target_pairs={{2,3},{1,2},{0,1},{6,7},{5,6},{4,5},{10,11},{9,10},{8,9},{14,15},{... | collective-permute-start | bytes 1572872 | tf_op jit(solution)/shard_map/ppermute | solution.py:738
  118.1 4.9 fusion.88
  123.1 3.6 collective-permute-done.16
  130.3 4.4 collective-permute-start.17
  136.0 7.6 %collective-permute-done.17 = bf16[128,2048]{1,0:T(8,128)(2,1)S(1)} collective-permute-done((bf16[128,2048]{1,0:T(8,128)(2,1)S(1)}, bf16[128,2048]{1,0:T(8,128)(2,1)S(1)}, u32[]{:S(2)}, u32[]{:S(2)}) %collective-permute-start.17) | collective-permute-done | bytes 524320 | tf_op jit(solution)/shard_map/ppermute | solution.py:738
  143.8 4.0 collective-permute-done.18
  149.2 4.6 collective-permute-start.19
  154.4 5.8 collective-permute-done.20
  163.3 4.7 collective-permute-start.21
  171.1 3.6 collective-permute-done.21
  174.9 5.1 collective-permute-done.22
  181.4 4.6 collective-permute-start.23
  187.9 3.3 collective-permute-done.24
  195.4 6.2 collective-permute-start.25
  201.7 19.1 %shard_map.187 = (bf16[256,2048]{1,0:T(8,128)(2,1)S(1)}, bf16[256,2048]{1,0:T(8,128)(2,1)S(1)}, bf16[256,2048]{1,0:T(8,128)(2,1)S(1)}, bf16[256,2048]{1,0:T(8,128)(2,1)S(1)}, bf16[256,2048]{1,0:T(8,128)(2,1)S(1)}) custom-call(bf16[256,2048]{1,0:T(8,128)(2,1)S(1)} %pad_maximum_fusion.4.normed, bf16[256,2048]{1,0:T(8,128)(2,1)S(1)} %get-tuple-element.869.grads, ...), custom_call_target="tpu_custom_call" | custom-call | flops 12884901888 | bytes 30408704 | tf_op jit(solution)/shard_map/pallas_call | solution.py:215
  225.9 5.4 collective-permute-start.27
  231.3 18.9 %shard_map.188 = (bf16[256,2048]{1,0:T(8,128)(2,1)S(1)}, bf16[256,2048]{1,0:T(8,128)(2,1)S(1)}, bf16[256,2048]{1,0:T(8,128)(2,1)S(1)}, bf16[256,2048]{1,0:T(8,128)(2,1)S(1)}, bf16[256,2048]{1,0:T(8,128)(2,1)S(1)}) custom-call(bf16[256,2048]{1,0:T(8,128)(2,1)S(1)} %pad_maximum_fusion.5.normed, bf16[256,2048]{1,0:T(8,128)(2,1)S(1)} %copy-done.29, ...), custom_call_target="tpu_custom_call" | custom-call | flops 12884901888 | bytes 30408704 | tf_op jit(solution)/shard_map/pallas_call | solution.py:215
  259.4 4.8 collective-permute-start.29
  264.2 18.9 %shard_map.189 = (bf16[256,2048]{1,0:T(8,128)(2,1)S(1)}, bf16[256,2048]{1,0:T(8,128)(2,1)S(1)}, bf16[256,2048]{1,0:T(8,128)(2,1)S(1)}, bf16[256,2048]{1,0:T(8,128)(2,1)S(1)}, bf16[256,2048]{1,0:T(8,128)(2,1)S(1)}) custom-call(bf16[256,2048]{1,0:T(8,128)(2,1)S(1)} %pad_maximum_fusion.6.normed, bf16[256,2048]{1,0:T(8,128)(2,1)S(1)} %copy-done.28, ...), custom_call_target="tpu_custom_call" | custom-call | flops 12884901888 | bytes 30408704 | tf_op jit(solution)/shard_map/pallas_call | solution.py:215
  283.3 10.4 %collective-permute-done.30 = bf16[128,2048]{1,0:T(8,128)(2,1)S(1)} collective-permute-done((bf16[128,2048]{1,0:T(8,128)(2,1)S(1)}, bf16[128,2048]{1,0:T(8,128)(2,1)S(1)}, u32[]{:S(2)}, u32[]{:S(2)}) %collective-permute-start.30) | collective-permute-done | bytes 524320 | tf_op jit(solution)/shard_map/ppermute | solution.py:739
  294.1 3.4 collective-permute-start.31
  298.8 18.9 %shard_map.190 = (bf16[256,2048]{1,0:T(8,128)(2,1)S(1)}, bf16[256,2048]{1,0:T(8,128)(2,1)S(1)}, bf16[256,2048]{1,0:T(8,128)(2,1)S(1)}, bf16[256,2048]{1,0:T(8,128)(2,1)S(1)}, bf16[256,2048]{1,0:T(8,128)(2,1)S(1)}) custom-call(bf16[256,2048]{1,0:T(8,128)(2,1)S(1)} %pad_maximum_fusion.7.normed, bf16[256,2048]{1,0:T(8,128)(2,1)S(1)} %copy-done.27, ...), custom_call_target="tpu_custom_call" | custom-call | flops 12884901888 | bytes 30408704 | tf_op jit(solution)/shard_map/pallas_call | solution.py:215
  321.0 11.4 %collective-permute-start.33 = (bf16[128,2048]{1,0:T(8,128)(2,1)}, bf16[128,2048]{1,0:T(8,128)(2,1)}, u32[]{:S(2)}, u32[]{:S(2)}) collective-permute-start(bf16[128,2048]{1,0:T(8,128)(2,1)} %add.586), channel_id=1, source_target_pairs={{2,3},{1,2},{0,1},{6,7},{5,6},{4,5},{10,11},{9,10},{8,9},{14,15},{... | collective-permute-start | bytes 1572872 | tf_op jit(solution)/shard_map/ppermute | solution.py:738
  333.9 11.1 %convolution_convert_fusion.2 = bf16[2048,2048]{1,0:T(8,128)(2,1)} fusion(bf16[1024,2048]{1,0:T(8,128)(2,1)S(1)} %copy-done.80, bf16[256,2048]{1,0:T(8,128)(2,1)S(1)} %get-tuple-element.499, bf16[256,2048]{1,0:T(8,128)(2,1)S(1)} %get-tuple-element.498, bf16[256,2048]{1,0:T(8,128)(2,1)S(1)} %copy-done.47, bf16[256,2048]{1,0:T(8,128)(2,1)S(1)} %copy-done.43), kind=kOutput, calls=%fused_computation.7 | convolution fusion | flops 8610906112 | bytes 16777216 | tf_op jit(solution)/shard_map/dot_general | solution.py:26
  354.4 12.4 %collective-permute-done.34 = bf16[128,2048]{1,0:T(8,128)(2,1)} collective-permute-done((bf16[128,2048]{1,0:T(8,128)(2,1)}, bf16[128,2048]{1,0:T(8,128)(2,1)}, u32[]{:S(2)}, u32[]{:S(2)}) %collective-permute-start.34) | collective-permute-done | bytes 524320 | tf_op jit(solution)/shard_map/ppermute | solution.py:739
  376.2 12.8 %convolution_convert_fusion.1 = bf16[2048,2048]{1,0:T(8,128)(2,1)} fusion(bf16[256,2048]{1,0:T(8,128)(2,1)S(1)} %copy-done.25, bf16[256,2048]{1,0:T(8,128)(2,1)S(1)} %copy-done.22, bf16[256,2048]{1,0:T(8,128)(2,1)S(1)} %copy-done.19, bf16[256,2048]{1,0:T(8,128)(2,1)S(1)} %copy-done.16, bf16[256,2048]{1,0:T(8,128)(2,1)} %copy-done.49, ...), kind=kOutput, calls=%fused_computation.6 | convolution fusion | flops 8627683328 | bytes 16777216 | tf_op jit(solution)/shard_map/dot_general | solution.py:26
  389.0 3.5 select_select_fusion.32
  398.0 3.5 fusion.47
  402.8 5.3 collective-permute-start.37
  412.2 11.2 %convolution_convert_fusion = bf16[2048,2048]{1,0:T(8,128)(2,1)} fusion(bf16[256,2048]{1,0:T(8,128)(2,1)S(1)} %copy-done.26, bf16[256,2048]{1,0:T(8,128)(2,1)S(1)} %copy-done.23, bf16[256,2048]{1,0:T(8,128)(2,1)S(1)} %copy-done.20, bf16[256,2048]{1,0:T(8,128)(2,1)S(1)} %copy-done.17, bf16[256,2048]{1,0:T(8,128)(2,1)S(1)} %copy-done.45, ...), kind=kOutput, calls=%fused_computation.5 | convolution fusion | flops 8627683328 | bytes 16777216 | tf_op jit(solution)/shard_map/dot_general | solution.py:26
  432.6 5.7 collective-permute-start.39
  450.6 4.6 collective-permute-start.41
  463.9 6.8 collective-permute-start.43
  480.1 6.2 collective-permute-start.45
  498.8 4.4 collective-permute-start.47
  507.0 5.1 fusion.46
  518.7 4.7 collective-permute-start.50
  525.2 4.8 collective-permute-done.50
  531.0 3.4 collective-permute-done.51
  535.4 4.7 collective-permute-start.52
  555.7 10.5 %shard_map.191 = bf16[2048,2048]{1,0:T(8,128)(2,1)S(1)} custom-call(bf16[1024,2048]{1,0:T(8,128)(2,1)S(1)} %copy-done.4, bf16[1024,1536]{1,0:T(8,128)(2,1)S(1)} %copy-done.13, bf16[1024,2048]{1,0:T(8,128)(2,1)S(1)} %copy-done.5, bf16[1024,512]{1,0:T(8,128)(2,1)S(1)} %pad_maximum_fusion.12.right_last), custom_call_target="tpu_custom_call" | custom-call | flops 524288 | bytes 524288 | tf_op jit(solution)/shard_map/pallas_call | solution.py:254
  566.2 3.2 copy-done.2
  575.3 4.7 collective-permute-start.54
  604.5 3.9 collective-permute-done.58
  620.9 4.3 collective-permute-done.61
  626.6 4.6 collective-permute-start.63
  632.6 5.4 collective-permute-done.65
  639.8 5.0 collective-permute-start.66
  648.1 4.4 pad_convert_fusion
  655.5 4.6 collective-permute-start.69
  665.5 3.9 collective-permute-done.69
  669.8 4.5 collective-permute-start.71
  677.1 3.8 collective-permute-done.71
  680.9 8.5 %collective-permute-done.72 = bf16[128,2048]{1,0:T(8,128)(2,1)S(1)} collective-permute-done((bf16[128,2048]{1,0:T(8,128)(2,1)S(1)}, bf16[128,2048]{1,0:T(8,128)(2,1)S(1)}, u32[]{:S(2)}, u32[]{:S(2)}) %collective-permute-start.72) | collective-permute-done | bytes 524320 | tf_op jit(solution)/shard_map/ppermute | solution.py:739
  693.5 13.7 %collective-permute-done.74 = bf16[128,2048]{1,0:T(8,128)(2,1)S(1)} collective-permute-done((bf16[128,2048]{1,0:T(8,128)(2,1)S(1)}, bf16[128,2048]{1,0:T(8,128)(2,1)S(1)}, u32[]{:S(2)}, u32[]{:S(2)}) %collective-permute-start.74) | collective-permute-done | bytes 524320 | tf_op jit(solution)/shard_map/ppermute | solution.py:739
  712.6 6.2 collective-permute-done.75
  (827 shorter events, 283.8 us)
Async XLA Ops:
  7.2 54.3 %all-gather.4.cloned.1.call-start = ((), (), s32[]{:S(2)}) async-start(), calls=%async_computation.4 | async-start | bytes 7077888 | tf_op jit(solution)/shard_map/all_gather | solution.py:392
  9.6 192.1 %all-gather.6.cloned.1.call-start = ((), (), s32[]{:S(2)}) async-start(), calls=%async_computation.10 | async-start | bytes 28311552 | tf_op jit(solution)/shard_map/all_gather | solution.py:401
  19.5 411.9 %all-reduce.4.cloned.1.call-start = ((), (), s32[]{:S(2)}) async-start(), calls=%async_computation.5 | async-start | bytes 4194304 | tf_op jit(solution)/shard_map/psum | solution.py:493
  20.5 12.5 %collective-permute-start.7 = (bf16[16,2048]{1,0:T(8,128)(2,1)S(1)}, bf16[16,2048]{1,0:T(8,128)(2,1)S(1)}, u32[]{:S(2)}, u32[]{:S(2)}) collective-permute-start(bf16[16,2048]{1,0:T(8,128)(2,1)S(1)} %slice.683), channel_id=1, source_target_pairs={{0,4},{4,8},{8,12},{12,16},{16,20},{20,24},{24,28},{1,5},{5,9},{9,... | collective-permute-start | bytes 196616 | tf_op jit(solution)/shard_map/ppermute | solution.py:40
  23.7 20.7 %collective-permute-start.8 = (f32[1,1]{1,0:T(1,128)}, f32[1,1]{1,0:T(1,128)}, u32[]{:S(2)}, u32[]{:S(2)}) collective-permute-start(f32[1,1]{1,0:T(1,128)} %bitcast.8), channel_id=1, source_target_pairs={{0,4},{4,8},{8,12},{12,16},{16,20},{20,24},{24,28},{1,5},{5,9},{9,... | collective-permute-start | bytes 20 | tf_op jit(solution)/shard_map/ppermute | solution.py:40
  76.7 15.1 %collective-permute-start.11 = (bf16[128,2048]{1,0:T(8,128)(2,1)S(1)}, bf16[128,2048]{1,0:T(8,128)(2,1)S(1)}, u32[]{:S(2)}, u32[]{:S(2)}) collective-permute-start(bf16[128,2048]{1,0:T(8,128)(2,1)S(1)} %get-tuple-element.400), channel_id=1, source_target_pairs={{0,1},{4,5},{8,9},{12,13},{16,17},{20,21},{24,25},{28,29}} | collective-permute-start | bytes 1572872 | tf_op jit(solution)/shard_map/ppermute | solution.py:738
  80.2 11.7 %collective-permute-start.12 = (bf16[128,2048]{1,0:T(8,128)(2,1)S(1)}, bf16[128,2048]{1,0:T(8,128)(2,1)S(1)}, u32[]{:S(2)}, u32[]{:S(2)}) collective-permute-start(bf16[128,2048]{1,0:T(8,128)(2,1)S(1)} %get-tuple-element.402), channel_id=1, source_target_pairs={{3,2},{7,6},{11,10},{15,14},{19,18},{23,22},{27,26},{31,30}} | collective-permute-start | bytes 1572872 | tf_op jit(solution)/shard_map/ppermute | solution.py:739
  92.5 15.3 %collective-permute-start.13 = (bf16[128,2048]{1,0:T(8,128)(2,1)S(1)}, bf16[128,2048]{1,0:T(8,128)(2,1)S(1)}, u32[]{:S(2)}, u32[]{:S(2)}) collective-permute-start(bf16[128,2048]{1,0:T(8,128)(2,1)S(1)} %add.546), channel_id=1, source_target_pairs={{1,2},{0,1},{5,6},{4,5},{9,10},{8,9},{13,14},{12,13},{17,18},{16,1... | collective-permute-start | bytes 1572872 | tf_op jit(solution)/shard_map/ppermute | solution.py:738
  108.0 18.6 %collective-permute-start.16 = (bf16[128,2048]{1,0:T(8,128)(2,1)S(1)}, bf16[128,2048]{1,0:T(8,128)(2,1)S(1)}, u32[]{:S(2)}, u32[]{:S(2)}) collective-permute-start(bf16[128,2048]{1,0:T(8,128)(2,1)S(1)} %add.551), channel_id=1, source_target_pairs={{1,0},{2,1},{3,2},{5,4},{6,5},{7,6},{9,8},{10,9},{11,10},{13,12},{... | collective-permute-start | bytes 1572872 | tf_op jit(solution)/shard_map/ppermute | solution.py:739
  109.3 18.5 %collective-permute-start.15 = (bf16[128,2048]{1,0:T(8,128)(2,1)S(1)}, bf16[128,2048]{1,0:T(8,128)(2,1)S(1)}, u32[]{:S(2)}, u32[]{:S(2)}) collective-permute-start(bf16[128,2048]{1,0:T(8,128)(2,1)S(1)} %add.550), channel_id=1, source_target_pairs={{2,3},{1,2},{0,1},{6,7},{5,6},{4,5},{10,11},{9,10},{8,9},{14,15},{... | collective-permute-start | bytes 1572872 | tf_op jit(solution)/shard_map/ppermute | solution.py:738
  130.3 13.4 %collective-permute-start.17 = (bf16[128,2048]{1,0:T(8,128)(2,1)S(1)}, bf16[128,2048]{1,0:T(8,128)(2,1)S(1)}, u32[]{:S(2)}, u32[]{:S(2)}) collective-permute-start(bf16[128,2048]{1,0:T(8,128)(2,1)S(1)} %add.554), channel_id=1, source_target_pairs={{2,3},{1,2},{0,1},{6,7},{5,6},{4,5},{10,11},{9,10},{8,9},{14,15},{... | collective-permute-start | bytes 1572872 | tf_op jit(solution)/shard_map/ppermute | solution.py:738
  134.7 13.1 %collective-permute-start.18 = (bf16[128,2048]{1,0:T(8,128)(2,1)S(1)}, bf16[128,2048]{1,0:T(8,128)(2,1)S(1)}, u32[]{:S(2)}, u32[]{:S(2)}) collective-permute-start(bf16[128,2048]{1,0:T(8,128)(2,1)S(1)} %add.555), channel_id=1, source_target_pairs={{1,0},{2,1},{3,2},{5,4},{6,5},{7,6},{9,8},{10,9},{11,10},{13,12},{... | collective-permute-start | bytes 1572872 | tf_op jit(solution)/shard_map/ppermute | solution.py:739
  147.9 12.3 %collective-permute-start.20 = (bf16[128,2048]{1,0:T(8,128)(2,1)S(1)}, bf16[128,2048]{1,0:T(8,128)(2,1)S(1)}, u32[]{:S(2)}, u32[]{:S(2)}) collective-permute-start(bf16[128,2048]{1,0:T(8,128)(2,1)S(1)} %add.565), channel_id=1, source_target_pairs={{3,2},{1,0},{2,1},{7,6},{5,4},{6,5},{11,10},{9,8},{10,9},{15,14},{... | collective-permute-start | bytes 1572872 | tf_op jit(solution)/shard_map/ppermute | solution.py:739
  149.2 12.1 %collective-permute-start.19 = (bf16[128,2048]{1,0:T(8,128)(2,1)S(1)}, bf16[128,2048]{1,0:T(8,128)(2,1)S(1)}, u32[]{:S(2)}, u32[]{:S(2)}) collective-permute-start(bf16[128,2048]{1,0:T(8,128)(2,1)S(1)} %add.564), channel_id=1, source_target_pairs={{0,1},{2,3},{1,2},{4,5},{6,7},{5,6},{8,9},{10,11},{9,10},{12,13},{... | collective-permute-start | bytes 1572872 | tf_op jit(solution)/shard_map/ppermute | solution.py:738
  163.3 11.4 %collective-permute-start.21 = (bf16[128,2048]{1,0:T(8,128)(2,1)S(1)}, bf16[128,2048]{1,0:T(8,128)(2,1)S(1)}, u32[]{:S(2)}, u32[]{:S(2)}) collective-permute-start(bf16[128,2048]{1,0:T(8,128)(2,1)S(1)} %add.566), channel_id=1, source_target_pairs={{1,2},{0,1},{2,3},{5,6},{4,5},{6,7},{9,10},{8,9},{10,11},{13,14},{... | collective-permute-start | bytes 1572872 | tf_op jit(solution)/shard_map/ppermute | solution.py:738
  168.0 12.0 %collective-permute-start.22 = (bf16[128,2048]{1,0:T(8,128)(2,1)S(1)}, bf16[128,2048]{1,0:T(8,128)(2,1)S(1)}, u32[]{:S(2)}, u32[]{:S(2)}) collective-permute-start(bf16[128,2048]{1,0:T(8,128)(2,1)S(1)} %add.567), channel_id=1, source_target_pairs={{2,1},{3,2},{1,0},{6,5},{7,6},{5,4},{10,9},{11,10},{9,8},{14,13},{... | collective-permute-start | bytes 1572872 | tf_op jit(solution)/shard_map/ppermute | solution.py:739
  180.1 11.1 %collective-permute-start.24 = (bf16[128,2048]{1,0:T(8,128)(2,1)S(1)}, bf16[128,2048]{1,0:T(8,128)(2,1)S(1)}, u32[]{:S(2)}, u32[]{:S(2)}) collective-permute-start(bf16[128,2048]{1,0:T(8,128)(2,1)S(1)} %add.577), channel_id=1, source_target_pairs={{1,0},{2,1},{3,2},{5,4},{6,5},{7,6},{9,8},{10,9},{11,10},{13,12},{... | collective-permute-start | bytes 1572872 | tf_op jit(solution)/shard_map/ppermute | solution.py:739
  181.4 11.2 %collective-permute-start.23 = (bf16[128,2048]{1,0:T(8,128)(2,1)S(1)}, bf16[128,2048]{1,0:T(8,128)(2,1)S(1)}, u32[]{:S(2)}, u32[]{:S(2)}) collective-permute-start(bf16[128,2048]{1,0:T(8,128)(2,1)S(1)} %add.576), channel_id=1, source_target_pairs={{2,3},{1,2},{0,1},{6,7},{5,6},{4,5},{10,11},{9,10},{8,9},{14,15},{... | collective-permute-start | bytes 1572872 | tf_op jit(solution)/shard_map/ppermute | solution.py:738
  194.1 27.6 %collective-permute-start.26 = (bf16[128,2048]{1,0:T(8,128)(2,1)}, bf16[128,2048]{1,0:T(8,128)(2,1)}, u32[]{:S(2)}, u32[]{:S(2)}) collective-permute-start(bf16[128,2048]{1,0:T(8,128)(2,1)} %get-tuple-element.438), channel_id=1, source_target_pairs={{1,0},{2,1},{3,2},{5,4},{6,5},{7,6},{9,8},{10,9},{11,10},{13,12},{... | collective-permute-start | bytes 1572872 | tf_op jit(solution)/shard_map/ppermute | solution.py:739
  195.4 26.3 %collective-permute-start.25 = (bf16[128,2048]{1,0:T(8,128)(2,1)}, bf16[128,2048]{1,0:T(8,128)(2,1)}, u32[]{:S(2)}, u32[]{:S(2)}) collective-permute-start(bf16[128,2048]{1,0:T(8,128)(2,1)} %get-tuple-element.436), channel_id=1, source_target_pairs={{2,3},{1,2},{0,1},{6,7},{5,6},{4,5},{10,11},{9,10},{8,9},{14,15},{... | collective-permute-start | bytes 1572872 | tf_op jit(solution)/shard_map/ppermute | solution.py:738
  224.6 31.4 %collective-permute-start.28 = (bf16[128,2048]{1,0:T(8,128)(2,1)}, bf16[128,2048]{1,0:T(8,128)(2,1)}, u32[]{:S(2)}, u32[]{:S(2)}) collective-permute-start(bf16[128,2048]{1,0:T(8,128)(2,1)} %get-tuple-element.452), channel_id=1, source_target_pairs={{3,2},{1,0},{2,1},{7,6},{5,4},{6,5},{11,10},{9,8},{10,9},{15,14},{... | collective-permute-start | bytes 1572872 | tf_op jit(solution)/shard_map/ppermute | solution.py:739
  225.9 30.1 %collective-permute-start.27 = (bf16[128,2048]{1,0:T(8,128)(2,1)}, bf16[128,2048]{1,0:T(8,128)(2,1)}, u32[]{:S(2)}, u32[]{:S(2)}) collective-permute-start(bf16[128,2048]{1,0:T(8,128)(2,1)} %get-tuple-element.450), channel_id=1, source_target_pairs={{0,1},{2,3},{1,2},{4,5},{6,7},{5,6},{8,9},{10,11},{9,10},{12,13},{... | collective-permute-start | bytes 1572872 | tf_op jit(solution)/shard_map/ppermute | solution.py:738
  255.9 239.7 %reduce-scatter.5.cloned.1.call-start = ((), (), s32[]{:S(2)}) async-start(), calls=%async_computation.6 | async-start | bytes 9437184 | tf_op jit(solution)/shard_map/reduce_scatter | solution.py:587
  258.1 35.6 %collective-permute-start.30 = (bf16[128,2048]{1,0:T(8,128)(2,1)S(1)}, bf16[128,2048]{1,0:T(8,128)(2,1)S(1)}, u32[]{:S(2)}, u32[]{:S(2)}) collective-permute-start(bf16[128,2048]{1,0:T(8,128)(2,1)S(1)} %get-tuple-element.464), channel_id=1, source_target_pairs={{2,1},{3,2},{1,0},{6,5},{7,6},{5,4},{10,9},{11,10},{9,8},{14,13},{... | collective-permute-start | bytes 1572872 | tf_op jit(solution)/shard_map/ppermute | solution.py:739
  259.4 34.3 %collective-permute-start.29 = (bf16[128,2048]{1,0:T(8,128)(2,1)S(1)}, bf16[128,2048]{1,0:T(8,128)(2,1)S(1)}, u32[]{:S(2)}, u32[]{:S(2)}) collective-permute-start(bf16[128,2048]{1,0:T(8,128)(2,1)S(1)} %get-tuple-element.462), channel_id=1, source_target_pairs={{1,2},{0,1},{2,3},{5,6},{4,5},{6,7},{9,10},{8,9},{10,11},{13,14},{... | collective-permute-start | bytes 1572872 | tf_op jit(solution)/shard_map/ppermute | solution.py:738
  294.1 23.9 %collective-permute-start.31 = (bf16[128,2048]{1,0:T(8,128)(2,1)S(1)}, bf16[128,2048]{1,0:T(8,128)(2,1)S(1)}, u32[]{:S(2)}, u32[]{:S(2)}) collective-permute-start(bf16[128,2048]{1,0:T(8,128)(2,1)S(1)} %get-tuple-element.474), channel_id=1, source_target_pairs={{2,3},{1,2},{0,1},{6,7},{5,6},{4,5},{10,11},{9,10},{8,9},{14,15},{... | collective-permute-start | bytes 1572872 | tf_op jit(solution)/shard_map/ppermute | solution.py:738
  297.5 21.5 %collective-permute-start.32 = (bf16[128,2048]{1,0:T(8,128)(2,1)S(1)}, bf16[128,2048]{1,0:T(8,128)(2,1)S(1)}, u32[]{:S(2)}, u32[]{:S(2)}) collective-permute-start(bf16[128,2048]{1,0:T(8,128)(2,1)S(1)} %get-tuple-element.476), channel_id=1, source_target_pairs={{1,0},{2,1},{3,2},{5,4},{6,5},{7,6},{9,8},{10,9},{11,10},{13,12},{... | collective-permute-start | bytes 1572872 | tf_op jit(solution)/shard_map/ppermute | solution.py:739
  321.0 31.4 %collective-permute-start.33 = (bf16[128,2048]{1,0:T(8,128)(2,1)}, bf16[128,2048]{1,0:T(8,128)(2,1)}, u32[]{:S(2)}, u32[]{:S(2)}) collective-permute-start(bf16[128,2048]{1,0:T(8,128)(2,1)} %add.586), channel_id=1, source_target_pairs={{2,3},{1,2},{0,1},{6,7},{5,6},{4,5},{10,11},{9,10},{8,9},{14,15},{... | collective-permute-start | bytes 1572872 | tf_op jit(solution)/shard_map/ppermute | solution.py:738
  332.4 34.4 %collective-permute-start.34 = (bf16[128,2048]{1,0:T(8,128)(2,1)}, bf16[128,2048]{1,0:T(8,128)(2,1)}, u32[]{:S(2)}, u32[]{:S(2)}) collective-permute-start(bf16[128,2048]{1,0:T(8,128)(2,1)} %add.587), channel_id=1, source_target_pairs={{1,0},{2,1},{3,2},{5,4},{6,5},{7,6},{9,8},{10,9},{11,10},{13,12},{... | collective-permute-start | bytes 1572872 | tf_op jit(solution)/shard_map/ppermute | solution.py:739
  368.8 224.0 %reduce-scatter.7.cloned.1.call-start = ((), (), s32[]{:S(2)}) async-start(), calls=%async_computation.7 | async-start | bytes 9437184 | tf_op jit(solution)/shard_map/reduce_scatter | solution.py:587
  368.9 24.5 %collective-permute-start.35 = (bf16[128,2048]{1,0:T(8,128)(2,1)}, bf16[128,2048]{1,0:T(8,128)(2,1)}, u32[]{:S(2)}, u32[]{:S(2)}) collective-permute-start(bf16[128,2048]{1,0:T(8,128)(2,1)} %add.591), channel_id=1, source_target_pairs={{0,1},{2,3},{1,2},{4,5},{6,7},{5,6},{8,9},{10,11},{9,10},{12,13},{... | collective-permute-start | bytes 1572872 | tf_op jit(solution)/shard_map/ppermute | solution.py:738
  372.0 23.4 %collective-permute-start.36 = (bf16[128,2048]{1,0:T(8,128)(2,1)}, bf16[128,2048]{1,0:T(8,128)(2,1)}, u32[]{:S(2)}, u32[]{:S(2)}) collective-permute-start(bf16[128,2048]{1,0:T(8,128)(2,1)} %add.592), channel_id=1, source_target_pairs={{3,2},{1,0},{2,1},{7,6},{5,4},{6,5},{11,10},{9,8},{10,9},{15,14},{... | collective-permute-start | bytes 1572872 | tf_op jit(solution)/shard_map/ppermute | solution.py:739
  397.4 256.5 %reduce-scatter.9.cloned.1.call-start = ((), (), s32[]{:S(2)}) async-start(), calls=%async_computation.8 | async-start | bytes 9437184 | tf_op jit(solution)/shard_map/reduce_scatter | solution.py:587
  402.8 24.4 %collective-permute-start.37 = (bf16[128,2048]{1,0:T(8,128)(2,1)}, bf16[128,2048]{1,0:T(8,128)(2,1)}, u32[]{:S(2)}, u32[]{:S(2)}) collective-permute-start(bf16[128,2048]{1,0:T(8,128)(2,1)} %add.596), channel_id=1, source_target_pairs={{1,2},{0,1},{2,3},{5,6},{4,5},{6,7},{9,10},{8,9},{10,11},{13,14},{... | collective-permute-start | bytes 1572872 | tf_op jit(solution)/shard_map/ppermute | solution.py:738
  408.2 21.1 %collective-permute-start.38 = (bf16[128,2048]{1,0:T(8,128)(2,1)}, bf16[128,2048]{1,0:T(8,128)(2,1)}, u32[]{:S(2)}, u32[]{:S(2)}) collective-permute-start(bf16[128,2048]{1,0:T(8,128)(2,1)} %add.597), channel_id=1, source_target_pairs={{2,1},{3,2},{1,0},{6,5},{7,6},{5,4},{10,9},{11,10},{9,8},{14,13},{... | collective-permute-start | bytes 1572872 | tf_op jit(solution)/shard_map/ppermute | solution.py:739
  431.3 15.5 %collective-permute-start.40 = (bf16[128,2048]{1,0:T(8,128)(2,1)}, bf16[128,2048]{1,0:T(8,128)(2,1)}, u32[]{:S(2)}, u32[]{:S(2)}) collective-permute-start(bf16[128,2048]{1,0:T(8,128)(2,1)} %add.602), channel_id=1, source_target_pairs={{1,0},{2,1},{3,2},{5,4},{6,5},{7,6},{9,8},{10,9},{11,10},{13,12},{... | collective-permute-start | bytes 1572872 | tf_op jit(solution)/shard_map/ppermute | solution.py:739
  432.6 14.2 %collective-permute-start.39 = (bf16[128,2048]{1,0:T(8,128)(2,1)}, bf16[128,2048]{1,0:T(8,128)(2,1)}, u32[]{:S(2)}, u32[]{:S(2)}) collective-permute-start(bf16[128,2048]{1,0:T(8,128)(2,1)} %add.601), channel_id=1, source_target_pairs={{2,3},{1,2},{0,1},{6,7},{5,6},{4,5},{10,11},{9,10},{8,9},{14,15},{... | collective-permute-start | bytes 1572872 | tf_op jit(solution)/shard_map/ppermute | solution.py:738
  446.7 273.3 %reduce-scatter.11.cloned.1.call-start = ((), (), s32[]{:S(2)}) async-start(), calls=%async_computation.9 | async-start | bytes 9437184 | tf_op jit(solution)/shard_map/reduce_scatter | solution.py:587
  449.0 11.3 %collective-permute-start.42 = (bf16[128,2048]{1,0:T(8,128)(2,1)S(1)}, bf16[128,2048]{1,0:T(8,128)(2,1)S(1)}, u32[]{:S(2)}, u32[]{:S(2)}) collective-permute-start(bf16[128,2048]{1,0:T(8,128)(2,1)S(1)} %get-tuple-element.556), channel_id=1, source_target_pairs={{1,0},{2,1},{3,2},{5,4},{6,5},{7,6},{9,8},{10,9},{11,10},{13,12},{... | collective-permute-start | bytes 1572872 | tf_op jit(solution)/shard_map/ppermute | solution.py:739
  450.6 11.2 %collective-permute-start.41 = (bf16[128,2048]{1,0:T(8,128)(2,1)S(1)}, bf16[128,2048]{1,0:T(8,128)(2,1)S(1)}, u32[]{:S(2)}, u32[]{:S(2)}) collective-permute-start(bf16[128,2048]{1,0:T(8,128)(2,1)S(1)} %get-tuple-element.554), channel_id=1, source_target_pairs={{2,3},{1,2},{0,1},{6,7},{5,6},{4,5},{10,11},{9,10},{8,9},{14,15},{... | collective-permute-start | bytes 1572872 | tf_op jit(solution)/shard_map/ppermute | solution.py:738
  456.3 59.2 %collective-permute-start.49 = (f32[3,512]{1,0:T(4,128)S(1)}, f32[3,512]{1,0:T(4,128)S(1)}, u32[]{:S(2)}, u32[]{:S(2)}) collective-permute-start(f32[3,512]{1,0:T(4,128)S(1)} %pad_maximum_fusion.33), channel_id=1, source_target_pairs={{4,0},{8,4},{12,8},{16,12},{20,16},{24,20},{28,24},{5,1},{9,5},{13... | collective-permute-start | bytes 18440 | tf_op jit(solution)/shard_map/ppermute | solution.py:45
  462.3 15.1 %collective-permute-start.44 = (bf16[128,2048]{1,0:T(8,128)(2,1)S(1)}, bf16[128,2048]{1,0:T(8,128)(2,1)S(1)}, u32[]{:S(2)}, u32[]{:S(2)}) collective-permute-start(bf16[128,2048]{1,0:T(8,128)(2,1)S(1)} %get-tuple-element.573), channel_id=1, source_target_pairs={{1,0},{2,1},{3,2},{5,4},{6,5},{7,6},{9,8},{10,9},{11,10},{13,12},{... | collective-permute-start | bytes 1572872 | tf_op jit(solution)/shard_map/ppermute | solution.py:739
  463.9 14.5 %collective-permute-start.43 = (bf16[128,2048]{1,0:T(8,128)(2,1)S(1)}, bf16[128,2048]{1,0:T(8,128)(2,1)S(1)}, u32[]{:S(2)}, u32[]{:S(2)}) collective-permute-start(bf16[128,2048]{1,0:T(8,128)(2,1)S(1)} %get-tuple-element.571), channel_id=1, source_target_pairs={{2,3},{1,2},{0,1},{6,7},{5,6},{4,5},{10,11},{9,10},{8,9},{14,15},{... | collective-permute-start | bytes 1572872 | tf_op jit(solution)/shard_map/ppermute | solution.py:738
  478.8 13.9 %collective-permute-start.46 = (bf16[128,2048]{1,0:T(8,128)(2,1)S(1)}, bf16[128,2048]{1,0:T(8,128)(2,1)S(1)}, u32[]{:S(2)}, u32[]{:S(2)}) collective-permute-start(bf16[128,2048]{1,0:T(8,128)(2,1)S(1)} %get-tuple-element.589), channel_id=1, source_target_pairs={{3,2},{1,0},{2,1},{7,6},{5,4},{6,5},{11,10},{9,8},{10,9},{15,14},{... | collective-permute-start | bytes 1572872 | tf_op jit(solution)/shard_map/ppermute | solution.py:739
  480.1 13.1 %collective-permute-start.45 = (bf16[128,2048]{1,0:T(8,128)(2,1)S(1)}, bf16[128,2048]{1,0:T(8,128)(2,1)S(1)}, u32[]{:S(2)}, u32[]{:S(2)}) collective-permute-start(bf16[128,2048]{1,0:T(8,128)(2,1)S(1)} %get-tuple-element.587), channel_id=1, source_target_pairs={{0,1},{2,3},{1,2},{4,5},{6,7},{5,6},{8,9},{10,11},{9,10},{12,13},{... | collective-permute-start | bytes 1572872 | tf_op jit(solution)/shard_map/ppermute | solution.py:738
  498.8 16.4 %collective-permute-start.47 = (bf16[128,2048]{1,0:T(8,128)(2,1)S(1)}, bf16[128,2048]{1,0:T(8,128)(2,1)S(1)}, u32[]{:S(2)}, u32[]{:S(2)}) collective-permute-start(bf16[128,2048]{1,0:T(8,128)(2,1)S(1)} %copy-done.182), channel_id=1, source_target_pairs={{1,2},{0,1},{2,3},{5,6},{4,5},{6,7},{9,10},{8,9},{10,11},{13,14},{... | collective-permute-start | bytes 1572872 | tf_op jit(solution)/shard_map/ppermute | solution.py:738
  503.2 12.2 %collective-permute-start.48 = (bf16[128,2048]{1,0:T(8,128)(2,1)S(1)}, bf16[128,2048]{1,0:T(8,128)(2,1)S(1)}, u32[]{:S(2)}, u32[]{:S(2)}) collective-permute-start(bf16[128,2048]{1,0:T(8,128)(2,1)S(1)} %copy-done.181), channel_id=1, source_target_pairs={{2,1},{3,2},{1,0},{6,5},{7,6},{5,4},{10,9},{11,10},{9,8},{14,13},{... | collective-permute-start | bytes 1572872 | tf_op jit(solution)/shard_map/ppermute | solution.py:739
  518.7 11.3 %collective-permute-start.50 = (bf16[128,2048]{1,0:T(8,128)(2,1)S(1)}, bf16[128,2048]{1,0:T(8,128)(2,1)S(1)}, u32[]{:S(2)}, u32[]{:S(2)}) collective-permute-start(bf16[128,2048]{1,0:T(8,128)(2,1)S(1)} %add.626), channel_id=1, source_target_pairs={{2,3},{1,2},{0,1},{6,7},{5,6},{4,5},{10,11},{9,10},{8,9},{14,15},{... | collective-permute-start | bytes 1572872 | tf_op jit(solution)/shard_map/ppermute | solution.py:738
  535.4 34.0 %collective-permute-start.52 = (bf16[128,2048]{1,0:T(8,128)(2,1)}, bf16[128,2048]{1,0:T(8,128)(2,1)}, u32[]{:S(2)}, u32[]{:S(2)}) collective-permute-start(bf16[128,2048]{1,0:T(8,128)(2,1)} %add.631), channel_id=1, source_target_pairs={{2,3},{1,2},{0,1},{6,7},{5,6},{4,5},{10,11},{9,10},{8,9},{14,15},{... | collective-permute-start | bytes 1572872 | tf_op jit(solution)/shard_map/ppermute | solution.py:738
  540.2 30.8 %collective-permute-start.53 = (bf16[128,2048]{1,0:T(8,128)(2,1)}, bf16[128,2048]{1,0:T(8,128)(2,1)}, u32[]{:S(2)}, u32[]{:S(2)}) collective-permute-start(bf16[128,2048]{1,0:T(8,128)(2,1)} %add.632), channel_id=1, source_target_pairs={{1,0},{2,1},{3,2},{5,4},{6,5},{7,6},{9,8},{10,9},{11,10},{13,12},{... | collective-permute-start | bytes 1572872 | tf_op jit(solution)/shard_map/ppermute | solution.py:739
  575.3 11.4 %collective-permute-start.54 = (bf16[128,2048]{1,0:T(8,128)(2,1)S(1)}, bf16[128,2048]{1,0:T(8,128)(2,1)S(1)}, u32[]{:S(2)}, u32[]{:S(2)}) collective-permute-start(bf16[128,2048]{1,0:T(8,128)(2,1)S(1)} %add.637), channel_id=1, source_target_pairs={{2,3},{1,2},{0,1},{6,7},{5,6},{4,5},{10,11},{9,10},{8,9},{14,15},{... | collective-permute-start | bytes 1572872 | tf_op jit(solution)/shard_map/ppermute | solution.py:738
  592.8 11.6 %collective-permute-start.57 = (bf16[128,2048]{1,0:T(8,128)(2,1)}, bf16[128,2048]{1,0:T(8,128)(2,1)S(1)}, u32[]{:S(2)}, u32[]{:S(2)}) collective-permute-start(bf16[128,2048]{1,0:T(8,128)(2,1)} %add.652), channel_id=1, source_target_pairs={{0,1},{2,3},{1,2},{4,5},{6,7},{5,6},{8,9},{10,11},{9,10},{12,13},{... | collective-permute-start | bytes 1572872 | tf_op jit(solution)/shard_map/ppermute | solution.py:738
  595.9 12.6 %collective-permute-start.58 = (bf16[128,2048]{1,0:T(8,128)(2,1)}, bf16[128,2048]{1,0:T(8,128)(2,1)S(1)}, u32[]{:S(2)}, u32[]{:S(2)}) collective-permute-start(bf16[128,2048]{1,0:T(8,128)(2,1)} %add.653), channel_id=1, source_target_pairs={{3,2},{1,0},{2,1},{7,6},{5,4},{6,5},{11,10},{9,8},{10,9},{15,14},{... | collective-permute-start | bytes 1572872 | tf_op jit(solution)/shard_map/ppermute | solution.py:739
  613.2 12.0 %collective-permute-start.61 = (bf16[128,2048]{1,0:T(8,128)(2,1)S(1)}, bf16[128,2048]{1,0:T(8,128)(2,1)S(1)}, u32[]{:S(2)}, u32[]{:S(2)}) collective-permute-start(bf16[128,2048]{1,0:T(8,128)(2,1)S(1)} %add.660), channel_id=1, source_target_pairs={{2,1},{3,2},{1,0},{6,5},{7,6},{5,4},{10,9},{11,10},{9,8},{14,13},{... | collective-permute-start | bytes 1572872 | tf_op jit(solution)/shard_map/ppermute | solution.py:739
  625.3 12.7 %collective-permute-start.64 = (bf16[128,2048]{1,0:T(8,128)(2,1)S(1)}, bf16[128,2048]{1,0:T(8,128)(2,1)S(1)}, u32[]{:S(2)}, u32[]{:S(2)}) collective-permute-start(bf16[128,2048]{1,0:T(8,128)(2,1)S(1)} %add.667), channel_id=1, source_target_pairs={{1,0},{2,1},{3,2},{5,4},{6,5},{7,6},{9,8},{10,9},{11,10},{13,12},{... | collective-permute-start | bytes 1572872 | tf_op jit(solution)/shard_map/ppermute | solution.py:739
  626.6 11.4 %collective-permute-start.63 = (bf16[128,2048]{1,0:T(8,128)(2,1)S(1)}, bf16[128,2048]{1,0:T(8,128)(2,1)S(1)}, u32[]{:S(2)}, u32[]{:S(2)}) collective-permute-start(bf16[128,2048]{1,0:T(8,128)(2,1)S(1)} %add.666), channel_id=1, source_target_pairs={{2,3},{1,2},{0,1},{6,7},{5,6},{4,5},{10,11},{9,10},{8,9},{14,15},{... | collective-permute-start | bytes 1572872 | tf_op jit(solution)/shard_map/ppermute | solution.py:738
  638.5 14.1 %collective-permute-start.67 = (bf16[128,2048]{1,0:T(8,128)(2,1)S(1)}, bf16[128,2048]{1,0:T(8,128)(2,1)S(1)}, u32[]{:S(2)}, u32[]{:S(2)}) collective-permute-start(bf16[128,2048]{1,0:T(8,128)(2,1)S(1)} %get-tuple-element.708), channel_id=1, source_target_pairs={{1,0},{2,1},{3,2},{5,4},{6,5},{7,6},{9,8},{10,9},{11,10},{13,12},{... | collective-permute-start | bytes 1572872 | tf_op jit(solution)/shard_map/ppermute | solution.py:739
  639.8 12.8 %collective-permute-start.66 = (bf16[128,2048]{1,0:T(8,128)(2,1)S(1)}, bf16[128,2048]{1,0:T(8,128)(2,1)S(1)}, u32[]{:S(2)}, u32[]{:S(2)}) collective-permute-start(bf16[128,2048]{1,0:T(8,128)(2,1)S(1)} %get-tuple-element.706), channel_id=1, source_target_pairs={{2,3},{1,2},{0,1},{6,7},{5,6},{4,5},{10,11},{9,10},{8,9},{14,15},{... | collective-permute-start | bytes 1572872 | tf_op jit(solution)/shard_map/ppermute | solution.py:738
  654.0 11.5 %collective-permute-start.70 = (bf16[128,2048]{1,0:T(8,128)(2,1)}, bf16[128,2048]{1,0:T(8,128)(2,1)S(1)}, u32[]{:S(2)}, u32[]{:S(2)}) collective-permute-start(bf16[128,2048]{1,0:T(8,128)(2,1)} %get-tuple-element.714), channel_id=1, source_target_pairs={{1,0},{2,1},{3,2},{5,4},{6,5},{7,6},{9,8},{10,9},{11,10},{13,12},{... | collective-permute-start | bytes 1572872 | tf_op jit(solution)/shard_map/ppermute | solution.py:739
  655.5 13.8 %collective-permute-start.69 = (bf16[128,2048]{1,0:T(8,128)(2,1)}, bf16[128,2048]{1,0:T(8,128)(2,1)S(1)}, u32[]{:S(2)}, u32[]{:S(2)}) collective-permute-start(bf16[128,2048]{1,0:T(8,128)(2,1)} %get-tuple-element.712), channel_id=1, source_target_pairs={{2,3},{1,2},{0,1},{6,7},{5,6},{4,5},{10,11},{9,10},{8,9},{14,15},{... | collective-permute-start | bytes 1572872 | tf_op jit(solution)/shard_map/ppermute | solution.py:738
  669.8 11.1 %collective-permute-start.71 = (bf16[128,2048]{1,0:T(8,128)(2,1)S(1)}, bf16[128,2048]{1,0:T(8,128)(2,1)S(1)}, u32[]{:S(2)}, u32[]{:S(2)}) collective-permute-start(bf16[128,2048]{1,0:T(8,128)(2,1)S(1)} %get-tuple-element.718), channel_id=1, source_target_pairs={{2,3},{1,2},{0,1},{6,7},{5,6},{4,5},{10,11},{9,10},{8,9},{14,15},{... | collective-permute-start | bytes 1572872 | tf_op jit(solution)/shard_map/ppermute | solution.py:738
  674.3 15.2 %collective-permute-start.72 = (bf16[128,2048]{1,0:T(8,128)(2,1)S(1)}, bf16[128,2048]{1,0:T(8,128)(2,1)S(1)}, u32[]{:S(2)}, u32[]{:S(2)}) collective-permute-start(bf16[128,2048]{1,0:T(8,128)(2,1)S(1)} %get-tuple-element.719), channel_id=1, source_target_pairs={{1,0},{2,1},{3,2},{5,4},{6,5},{7,6},{9,8},{10,9},{11,10},{13,12},{... | collective-permute-start | bytes 1572872 | tf_op jit(solution)/shard_map/ppermute | solution.py:739
  690.7 16.6 %collective-permute-start.74 = (bf16[128,2048]{1,0:T(8,128)(2,1)S(1)}, bf16[128,2048]{1,0:T(8,128)(2,1)S(1)}, u32[]{:S(2)}, u32[]{:S(2)}) collective-permute-start(bf16[128,2048]{1,0:T(8,128)(2,1)S(1)} %collective-permute-done.72), channel_id=1, source_target_pairs={{1,0},{2,1},{5,4},{6,5},{9,8},{10,9},{13,12},{14,13},{17,16},{18,1... | collective-permute-start | bytes 1572872 | tf_op jit(solution)/shard_map/ppermute | solution.py:739
  707.6 11.2 %collective-permute-start.75 = (bf16[128,2048]{1,0:T(8,128)(2,1)S(1)}, bf16[128,2048]{1,0:T(8,128)(2,1)S(1)}, u32[]{:S(2)}, u32[]{:S(2)}) collective-permute-start(bf16[128,2048]{1,0:T(8,128)(2,1)S(1)} %collective-permute-done.74), channel_id=1, source_target_pairs={{1,0},{5,4},{9,8},{13,12},{17,16},{21,20},{25,24},{29,28}} | collective-permute-start | bytes 1572872 | tf_op jit(solution)/shard_map/ppermute | solution.py:739
  (240 other events, 2285.6 us)
Sparse Core Ops, SparseCore 0:
  10.5 50.9 all-gather.3
  63.9 125.7 all-gather.5
  256.0 108.8 all-reduce.3
  368.9 75.5 reduce-scatter.4
  448.3 71.2 reduce-scatter.6
  523.4 71.2 reduce-scatter.8
  598.1 71.6 reduce-scatter.10

commit v2 on v1

--- a/solution.py
+++ b/solution.py
@@ -538,16 +538,22 @@
                 axis=1,
             )
             grad_normed = dot_right(grad_projected, in_full).astype(bf16)
-            value = tokens_of(c).astype(f32)
-            gain_sum = jnp.sum(grad_normed.astype(f32) * (value * rms_scale(value)), axis=0)
-            return grad_projected, grad_normed, gain_sum
+            return grad_projected, grad_normed
 
         needs = [f"gm{c}", f"proj{c}", f"longer{c}", f"conv{c}"]
         gives = [f"gc{c}", f"go{c}", f"tap{c}", f"head{c}"]
         gives += [f"head{chunks}"] if c == 0 else []
         add(f"backA{c}", needs, gives, 5.0, (2, c))(run_a)
         needs = [f"gc{c}", f"go{c}", f"proj{c}", f"head{c + 1}"]
-        add(f"backB{c}", needs, [f"gp{c}", f"gn1{c}", f"g1{c}"], 9.0, (3, c))(run_b)
+        add(f"backB{c}", needs, [f"gp{c}", f"gn1{c}"], 8.0, (3, c))(run_b)
+
+        def run_gain(e):
+            value = tokens_of(c).astype(f32)
+            scaled = value * rms_scale(value)
+            return (jnp.sum(e[f"gn1{c}"].astype(f32) * scaled, axis=0),)
+
+        needs = [f"gn1{c}", f"gn1{chunks - 1}", f"four{(c + 1) // 2}_sum"]
+        add(f"gain{c}", needs, [f"g1{c}"], 2.0, (3.5, c))(run_gain)
 
     def fourth(c):
         def run(e):
@@ -603,7 +609,7 @@
     scattered_sum("down_grad", names("act"), down_part, 12.0, 0, 1, 4)
     scattered_sum("gate_grad", names("n2", "gg"), gate_part, 11.0, 1, 0, 4)
     scattered_sum("up_grad", names("n2", "gu"), up_part, 11.0, 1.5, 0, 4)
-    scattered_sum("mixer_grad", names("gm", "gated", "gp"), mixer_part, 18.0, 2, 0, 4)
+    scattered_sum("mixer_grad", names("gm", "gated", "gp"), mixer_part, 18.0, 2, 0, 3)
 
     def total(e, kind):
         return sum(e[f"{kind}{c}"] for c in range(chunks))
@@ -628,25 +634,25 @@
             add(f"small{turn + 1}", [f"small{turn}"], [f"small{turn + 1}"], 2.0, (4, 10))(run)
             turn += 1
 
-    def rows_put(name, needs, first, step):
+    def rows_put(name, needs, first, step, after=()):
         def run(e):
             block = e[needs[0]].astype(f32 if name == "tokens_grad" else bf16)
             if len(needs) == 1:
                 return (jnp.pad(block, ((0, count - block.shape[0]), (0, 0))),)
             return (lax.dynamic_update_slice(e[needs[1]], block, (first, 0)),)
 
-        add(f"{name}_{step}", needs, [f"{name}{step}"], 2.0, (4.6, step))(run)
+        add(f"{name}_{step}", needs + list(after), [f"{name}{step}"], 2.0, (4.6, step))(run)
 
     for c in range(chunks):
         so_far = [f"tokens_grad{c - 1}"] if c else []
         rows_put("tokens_grad", [f"gt{c}"] + so_far, c * rows, c)
-    rows_put("block_out", ["out0"], 0, 0)
+    rows_put("block_out", ["out0"], 0, 0, ["small0"])
     for c in range(chunks // 2, chunks):
         step = c - chunks // 2 + 1
         rows_put("block_out", [f"out{c}", f"block_out{step - 1}"], c * rows, step)
 
     def widened(name):
-        add(f"{name}_wide", [f"{name}_grad"], [f"{name}_wide"], 2.0, (4.7, 0))(
+        add(f"{name}_wide", [f"{name}_grad", "small0"], [f"{name}_wide"], 2.0, (4.7, 0))(
             lambda e: (e[f"{name}_grad"].astype(f32),)
         )
 
@@ -657,7 +663,7 @@
         mixer_grad = e["mixer_grad"].astype(f32)
         return mixer_grad[:, : 3 * inner].reshape(in_weight.shape), mixer_grad[:, 3 * inner :].T
 
-    add("mixer_wide", ["mixer_grad"], ["in_wide", "out_wide"], 3.0, (4.7, 1))(mixer_wide)
+    add("mixer_wide", ["mixer_grad"], ["in_wide", "out_wide"], 3.0, (4.5, 1))(mixer_wide)
 
     slots = plan(steps, sums, line, 16.0)
     run_slots(slots, sums, env, line, place, half)

time: 747 us -> 751 us (level)
  waiting for transfers between devices: 171 us -> 147 us
  other arithmetic: 135 us -> 157 us
  starting transfers between devices: 203 us -> 213 us
    ppermute x30, waiting for transfers between devices: 91.2 us -> 66.2 us  [run_slots(): lax.ppermute(send_down, 'tp', [(p, p - 1) for p in down_options])]
    unnamed x445 -> x461, local copies, waits for them, and re-layouts: 37.4 us -> 29.2 us
  transfers between devices with their start and end apart: 84 -> 84, of which waited for: 40 -> 38; matrix products, arithmetic and copies ran while one was open for 29% -> 32% of each run, Pallas kernels for 12% -> 12%
where the time goes in v2:
time: 751 us; the launch traced here: 736 us
  starting transfers between devices  213 us (28%)
  other arithmetic  157 us (21%)
  waiting for transfers between devices  147 us (20%)
  Pallas kernels  86.8 us (12%)
  matrix products  68.3 us (9%)
  local copies, waits for them, and re-layouts  46.3 us (6%)
  between operations  18.7 us (2%)
    ppermute x30, starting transfers between devices, run_slots(): up[slot] = lax.ppermute(send_up, 'tp', [(p, p + 1) for p in up_options])  147 us
    pallas_call x4, Pallas kernels, feed_forward(): pl.pallas_call(feed_kernel, grid=(hidden // tile,), in_specs=[whole, whol...  75.9 us
    ppermute x30, waiting for transfers between devices, run_slots(): lax.ppermute(send_down, 'tp', [(p, p - 1) for p in down_options])  66.2 us
    ppermute x30, waiting for transfers between devices, run_slots(): up[slot] = lax.ppermute(send_up, 'tp', [(p, p + 1) for p in up_options])  45.5 us
    ppermute x30, starting transfers between devices, run_slots(): lax.ppermute(send_down, 'tp', [(p, p - 1) for p in down_options])  39.1 us
    select_n x46, other arithmetic, chosen(): value = jnp.where(place == position, option, value)  39 us
    dot_general x3, matrix products, dot_left(): lax.dot_general(left, right, (((0,), (0,)), ((), ())), preferred_element_...  35.1 us
    unnamed x461, local copies, waits for them, and re-layouts  29.2 us
  transfers between devices with their start and end apart: 84, of which 38 were waited for; matrix products, arithmetic and copies ran while one was open for 32% of the time, Pallas kernels for 12%

profile of v2, /device:TPU:0, one launch (start us, length us, event | category | flops | bytes accessed | tf_op | source)
XLA Modules:
  0.0 736.5 jit_solution(3729229570347144921)
XLA Ops:
  15.8 3.5 pad_maximum_fusion.1
  36.1 7.6 %collective-permute-done.3.refs_4_ = bf16[256,512]{1,0:T(8,128)(2,1)S(1)} collective-permute-done((bf16[256,512]{1,0:T(8,128)(2,1)S(1)}, bf16[256,512]{1,0:T(8,128)(2,1)S(1)}, u32[]{:S(2)}, u32[]{:S(2)}) %collective-permute-start.3) | collective-permute-done | bytes 262176 | tf_op jit(solution)/shard_map/ppermute | solution.py:131
  48.9 12.6 %all-gather.4.cloned.1.call-done = bf16[2048,1536]{0,1:T(8,128)(2,1)} async-done(((bf16[256,1536]{0,1:T(8,128)(2,1)}), bf16[2048,1536]{0,1:T(8,128)(2,1)}) %all-gather.4.cloned.1.call-update) | async-done | bytes 6291472 | tf_op jit(solution)/shard_map/all_gather | solution.py:392
  61.5 4.9 convolution_convert_fusion.3
  76.6 3.5 collective-permute-start.11
  85.5 6.2 collective-permute-done.11
  92.4 4.4 collective-permute-start.13
  101.2 6.5 collective-permute-done.13
  109.3 8.8 %collective-permute-start.15 = (bf16[128,2048]{1,0:T(8,128)(2,1)S(1)}, bf16[128,2048]{1,0:T(8,128)(2,1)S(1)}, u32[]{:S(2)}, u32[]{:S(2)}) collective-permute-start(bf16[128,2048]{1,0:T(8,128)(2,1)S(1)} %add.550), channel_id=1, source_target_pairs={{2,3},{1,2},{0,1},{6,7},{5,6},{4,5},{10,11},{9,10},{8,9},{14,15},{... | collective-permute-start | bytes 1572872 | tf_op jit(solution)/shard_map/ppermute | solution.py:744
  118.1 4.4 fusion.88
  122.5 4.1 collective-permute-done.16
  130.2 4.4 collective-permute-start.17
  135.9 7.6 %collective-permute-done.17 = bf16[128,2048]{1,0:T(8,128)(2,1)S(1)} collective-permute-done((bf16[128,2048]{1,0:T(8,128)(2,1)S(1)}, bf16[128,2048]{1,0:T(8,128)(2,1)S(1)}, u32[]{:S(2)}, u32[]{:S(2)}) %collective-permute-start.17) | collective-permute-done | bytes 524320 | tf_op jit(solution)/shard_map/ppermute | solution.py:744
  143.7 4.0 collective-permute-done.18
  149.1 4.6 collective-permute-start.19
  154.3 5.8 collective-permute-done.20
  163.2 4.7 collective-permute-start.21
  171.0 3.6 collective-permute-done.21
  174.8 5.1 collective-permute-done.22
  181.3 4.6 collective-permute-start.23
  187.8 3.3 collective-permute-done.24
  195.3 6.2 collective-permute-start.25
  201.6 19.1 %shard_map.187 = (bf16[256,2048]{1,0:T(8,128)(2,1)S(1)}, bf16[256,2048]{1,0:T(8,128)(2,1)S(1)}, bf16[256,2048]{1,0:T(8,128)(2,1)S(1)}, bf16[256,2048]{1,0:T(8,128)(2,1)S(1)}, bf16[256,2048]{1,0:T(8,128)(2,1)S(1)}) custom-call(bf16[256,2048]{1,0:T(8,128)(2,1)S(1)} %pad_maximum_fusion.4.normed, bf16[256,2048]{1,0:T(8,128)(2,1)S(1)} %get-tuple-element.889.grads, ...), custom_call_target="tpu_custom_call" | custom-call | flops 12884901888 | bytes 30408704 | tf_op jit(solution)/shard_map/pallas_call | solution.py:215
  225.7 5.4 collective-permute-start.27
  231.1 18.9 %shard_map.188 = (bf16[256,2048]{1,0:T(8,128)(2,1)S(1)}, bf16[256,2048]{1,0:T(8,128)(2,1)S(1)}, bf16[256,2048]{1,0:T(8,128)(2,1)S(1)}, bf16[256,2048]{1,0:T(8,128)(2,1)S(1)}, bf16[256,2048]{1,0:T(8,128)(2,1)S(1)}) custom-call(bf16[256,2048]{1,0:T(8,128)(2,1)S(1)} %pad_maximum_fusion.5.normed, bf16[256,2048]{1,0:T(8,128)(2,1)S(1)} %copy-done.27, ...), custom_call_target="tpu_custom_call" | custom-call | flops 12884901888 | bytes 30408704 | tf_op jit(solution)/shard_map/pallas_call | solution.py:215
  259.2 4.8 collective-permute-start.29
  264.0 18.9 %shard_map.189 = (bf16[256,2048]{1,0:T(8,128)(2,1)S(1)}, bf16[256,2048]{1,0:T(8,128)(2,1)S(1)}, bf16[256,2048]{1,0:T(8,128)(2,1)S(1)}, bf16[256,2048]{1,0:T(8,128)(2,1)S(1)}, bf16[256,2048]{1,0:T(8,128)(2,1)S(1)}) custom-call(bf16[256,2048]{1,0:T(8,128)(2,1)S(1)} %pad_maximum_fusion.6.normed, bf16[256,2048]{1,0:T(8,128)(2,1)S(1)} %copy-done.26, ...), custom_call_target="tpu_custom_call" | custom-call | flops 12884901888 | bytes 30408704 | tf_op jit(solution)/shard_map/pallas_call | solution.py:215
  283.1 10.4 %collective-permute-done.30 = bf16[128,2048]{1,0:T(8,128)(2,1)S(1)} collective-permute-done((bf16[128,2048]{1,0:T(8,128)(2,1)S(1)}, bf16[128,2048]{1,0:T(8,128)(2,1)S(1)}, u32[]{:S(2)}, u32[]{:S(2)}) %collective-permute-start.30) | collective-permute-done | bytes 524320 | tf_op jit(solution)/shard_map/ppermute | solution.py:745
  293.9 3.4 collective-permute-start.31
  298.6 18.9 %shard_map.190 = (bf16[256,2048]{1,0:T(8,128)(2,1)S(1)}, bf16[256,2048]{1,0:T(8,128)(2,1)S(1)}, bf16[256,2048]{1,0:T(8,128)(2,1)S(1)}, bf16[256,2048]{1,0:T(8,128)(2,1)S(1)}, bf16[256,2048]{1,0:T(8,128)(2,1)S(1)}) custom-call(bf16[256,2048]{1,0:T(8,128)(2,1)S(1)} %pad_maximum_fusion.7.normed, bf16[256,2048]{1,0:T(8,128)(2,1)S(1)} %copy-done.25, ...), custom_call_target="tpu_custom_call" | custom-call | flops 12884901888 | bytes 30408704 | tf_op jit(solution)/shard_map/pallas_call | solution.py:215
  320.8 11.5 %collective-permute-start.33 = (bf16[128,2048]{1,0:T(8,128)(2,1)}, bf16[128,2048]{1,0:T(8,128)(2,1)}, u32[]{:S(2)}, u32[]{:S(2)}) collective-permute-start(bf16[128,2048]{1,0:T(8,128)(2,1)} %add.586), channel_id=1, source_target_pairs={{2,3},{1,2},{0,1},{6,7},{5,6},{4,5},{10,11},{9,10},{8,9},{14,15},{... | collective-permute-start | bytes 1572872 | tf_op jit(solution)/shard_map/ppermute | solution.py:744
  333.8 11.2 %convolution_convert_fusion.2 = bf16[2048,2048]{1,0:T(8,128)(2,1)} fusion(bf16[1024,2048]{1,0:T(8,128)(2,1)S(1)} %copy-done.77, bf16[256,2048]{1,0:T(8,128)(2,1)S(1)} %get-tuple-element.509, bf16[256,2048]{1,0:T(8,128)(2,1)S(1)} %get-tuple-element.508, bf16[256,2048]{1,0:T(8,128)(2,1)S(1)} %copy-done.45, bf16[256,2048]{1,0:T(8,128)(2,1)S(1)} %copy-done.43), kind=kOutput, calls=%fused_computation.7 | convolution fusion | flops 8610906112 | bytes 16777216 | tf_op jit(solution)/shard_map/dot_general | solution.py:26
  354.2 12.4 %collective-permute-done.34 = bf16[128,2048]{1,0:T(8,128)(2,1)} collective-permute-done((bf16[128,2048]{1,0:T(8,128)(2,1)}, bf16[128,2048]{1,0:T(8,128)(2,1)}, u32[]{:S(2)}, u32[]{:S(2)}) %collective-permute-start.34) | collective-permute-done | bytes 524320 | tf_op jit(solution)/shard_map/ppermute | solution.py:745
  375.9 12.8 %convolution_convert_fusion.1 = bf16[2048,2048]{1,0:T(8,128)(2,1)} fusion(bf16[256,2048]{1,0:T(8,128)(2,1)S(1)} %copy-done.23, bf16[256,2048]{1,0:T(8,128)(2,1)S(1)} %copy-done.20, bf16[256,2048]{1,0:T(8,128)(2,1)S(1)} %copy-done.17, bf16[256,2048]{1,0:T(8,128)(2,1)S(1)} %copy-done.14, bf16[256,2048]{1,0:T(8,128)(2,1)} %copy-done.47, ...), kind=kOutput, calls=%fused_computation.6 | convolution fusion | flops 8627683328 | bytes 16777216 | tf_op jit(solution)/shard_map/dot_general | solution.py:26
  388.7 3.6 select_select_fusion.32
  397.8 3.5 fusion.47
  402.6 5.4 collective-permute-start.37
  412.0 11.2 %convolution_convert_fusion = bf16[2048,2048]{1,0:T(8,128)(2,1)} fusion(bf16[256,2048]{1,0:T(8,128)(2,1)S(1)} %copy-done.24, bf16[256,2048]{1,0:T(8,128)(2,1)S(1)} %copy-done.21, bf16[256,2048]{1,0:T(8,128)(2,1)S(1)} %copy-done.18, bf16[256,2048]{1,0:T(8,128)(2,1)S(1)} %copy-done.15, bf16[256,2048]{1,0:T(8,128)(2,1)S(1)} %copy-done.41, ...), kind=kOutput, calls=%fused_computation.5 | convolution fusion | flops 8627683328 | bytes 16777216 | tf_op jit(solution)/shard_map/dot_general | solution.py:26
  432.6 5.7 collective-permute-start.39
  448.3 5.1 collective-permute-start.41
  462.1 6.8 collective-permute-start.43
  478.6 6.1 collective-permute-start.45
  497.4 4.4 collective-permute-start.47
  503.8 5.8 convolution_convert_fusion.9
  515.7 4.1 collective-permute-start.50
  521.6 4.8 collective-permute-done.50
  534.1 4.5 collective-permute-start.52
  544.7 10.5 %shard_map.191 = bf16[2048,2048]{1,0:T(8,128)(2,1)S(1)} custom-call(bf16[1024,2048]{1,0:T(8,128)(2,1)S(1)} %copy-done.4, bf16[1024,1536]{1,0:T(8,128)(2,1)S(1)} %pad_maximum_fusion.2.right, bf16[1024,2048]{1,0:T(8,128)(2,1)S(1)} %pad_maximum_fusion.left_last, bf16[1024,512]{1,0:T(8,128)(2,1)S(1)} %pad_maximum_fusion.12.right_last), custom_call_target="tpu_custom_call" | custom-call | flops 524288 | bytes 524288 | tf_op jit(solution)/shard_map/pallas_call | solution.py:254
  555.2 3.2 copy-done.2
  568.3 5.5 collective-permute-start.54
  587.1 3.8 collective-permute-start.56
  594.4 3.5 collective-permute-done.56
  598.9 3.3 collective-permute-done.57
  627.4 4.6 collective-permute-start.60
  633.9 3.3 collective-permute-done.61
  640.4 6.1 collective-permute-start.63
  649.0 4.4 pad_convert_fusion
  657.2 5.8 collective-permute-start.66
  669.4 3.2 collective-permute-done.66
  673.0 4.5 collective-permute-start.69
  678.9 3.1 collective-permute-start.71
  683.6 8.7 %collective-permute-done.71 = f32[8,512]{1,0:T(8,128)S(1)} collective-permute-done((f32[8,512]{1,0:T(8,128)S(1)}, f32[8,512]{1,0:T(8,128)S(1)}, u32[]{:S(2)}, u32[]{:S(2)}) %collective-permute-start.71) | collective-permute-done | bytes 16416 | tf_op jit(solution)/shard_map/ppermute | solution.py:54
  695.5 6.4 collective-permute-start.74
  703.5 5.2 collective-permute-done.74
  (847 shorter events, 293.4 us)
Async XLA Ops:
  7.2 54.3 %all-gather.4.cloned.1.call-start = ((), (), s32[]{:S(2)}) async-start(), calls=%async_computation.4 | async-start | bytes 7077888 | tf_op jit(solution)/shard_map/all_gather | solution.py:392
  9.6 191.9 %all-gather.6.cloned.1.call-start = ((), (), s32[]{:S(2)}) async-start(), calls=%async_computation.10 | async-start | bytes 28311552 | tf_op jit(solution)/shard_map/all_gather | solution.py:401
  19.5 411.8 %all-reduce.4.cloned.1.call-start = ((), (), s32[]{:S(2)}) async-start(), calls=%async_computation.5 | async-start | bytes 4194304 | tf_op jit(solution)/shard_map/psum | solution.py:493
  20.5 12.5 %collective-permute-start.7 = (bf16[16,2048]{1,0:T(8,128)(2,1)S(1)}, bf16[16,2048]{1,0:T(8,128)(2,1)S(1)}, u32[]{:S(2)}, u32[]{:S(2)}) collective-permute-start(bf16[16,2048]{1,0:T(8,128)(2,1)S(1)} %slice.703), channel_id=1, source_target_pairs={{0,4},{4,8},{8,12},{12,16},{16,20},{20,24},{24,28},{1,5},{5,9},{9,... | collective-permute-start | bytes 196616 | tf_op jit(solution)/shard_map/ppermute | solution.py:40
  23.7 20.9 %collective-permute-start.8 = (f32[1,1]{1,0:T(1,128)}, f32[1,1]{1,0:T(1,128)}, u32[]{:S(2)}, u32[]{:S(2)}) collective-permute-start(f32[1,1]{1,0:T(1,128)} %bitcast.8), channel_id=1, source_target_pairs={{0,4},{4,8},{8,12},{12,16},{16,20},{20,24},{24,28},{1,5},{5,9},{9,... | collective-permute-start | bytes 20 | tf_op jit(solution)/shard_map/ppermute | solution.py:40
  76.6 15.1 %collective-permute-start.11 = (bf16[128,2048]{1,0:T(8,128)(2,1)S(1)}, bf16[128,2048]{1,0:T(8,128)(2,1)S(1)}, u32[]{:S(2)}, u32[]{:S(2)}) collective-permute-start(bf16[128,2048]{1,0:T(8,128)(2,1)S(1)} %get-tuple-element.410), channel_id=1, source_target_pairs={{0,1},{4,5},{8,9},{12,13},{16,17},{20,21},{24,25},{28,29}} | collective-permute-start | bytes 1572872 | tf_op jit(solution)/shard_map/ppermute | solution.py:744
  80.1 11.7 %collective-permute-start.12 = (bf16[128,2048]{1,0:T(8,128)(2,1)S(1)}, bf16[128,2048]{1,0:T(8,128)(2,1)S(1)}, u32[]{:S(2)}, u32[]{:S(2)}) collective-permute-start(bf16[128,2048]{1,0:T(8,128)(2,1)S(1)} %get-tuple-element.412), channel_id=1, source_target_pairs={{3,2},{7,6},{11,10},{15,14},{19,18},{23,22},{27,26},{31,30}} | collective-permute-start | bytes 1572872 | tf_op jit(solution)/shard_map/ppermute | solution.py:745
  92.4 15.3 %collective-permute-start.13 = (bf16[128,2048]{1,0:T(8,128)(2,1)S(1)}, bf16[128,2048]{1,0:T(8,128)(2,1)S(1)}, u32[]{:S(2)}, u32[]{:S(2)}) collective-permute-start(bf16[128,2048]{1,0:T(8,128)(2,1)S(1)} %add.546), channel_id=1, source_target_pairs={{1,2},{0,1},{5,6},{4,5},{9,10},{8,9},{13,14},{12,13},{17,18},{16,1... | collective-permute-start | bytes 1572872 | tf_op jit(solution)/shard_map/ppermute | solution.py:744
  108.0 18.6 %collective-permute-start.16 = (bf16[128,2048]{1,0:T(8,128)(2,1)S(1)}, bf16[128,2048]{1,0:T(8,128)(2,1)S(1)}, u32[]{:S(2)}, u32[]{:S(2)}) collective-permute-start(bf16[128,2048]{1,0:T(8,128)(2,1)S(1)} %add.551), channel_id=1, source_target_pairs={{1,0},{2,1},{3,2},{5,4},{6,5},{7,6},{9,8},{10,9},{11,10},{13,12},{... | collective-permute-start | bytes 1572872 | tf_op jit(solution)/shard_map/ppermute | solution.py:745
  109.3 18.5 %collective-permute-start.15 = (bf16[128,2048]{1,0:T(8,128)(2,1)S(1)}, bf16[128,2048]{1,0:T(8,128)(2,1)S(1)}, u32[]{:S(2)}, u32[]{:S(2)}) collective-permute-start(bf16[128,2048]{1,0:T(8,128)(2,1)S(1)} %add.550), channel_id=1, source_target_pairs={{2,3},{1,2},{0,1},{6,7},{5,6},{4,5},{10,11},{9,10},{8,9},{14,15},{... | collective-permute-start | bytes 1572872 | tf_op jit(solution)/shard_map/ppermute | solution.py:744
  130.2 13.4 %collective-permute-start.17 = (bf16[128,2048]{1,0:T(8,128)(2,1)S(1)}, bf16[128,2048]{1,0:T(8,128)(2,1)S(1)}, u32[]{:S(2)}, u32[]{:S(2)}) collective-permute-start(bf16[128,2048]{1,0:T(8,128)(2,1)S(1)} %add.554), channel_id=1, source_target_pairs={{2,3},{1,2},{0,1},{6,7},{5,6},{4,5},{10,11},{9,10},{8,9},{14,15},{... | collective-permute-start | bytes 1572872 | tf_op jit(solution)/shard_map/ppermute | solution.py:744
  134.6 13.1 %collective-permute-start.18 = (bf16[128,2048]{1,0:T(8,128)(2,1)S(1)}, bf16[128,2048]{1,0:T(8,128)(2,1)S(1)}, u32[]{:S(2)}, u32[]{:S(2)}) collective-permute-start(bf16[128,2048]{1,0:T(8,128)(2,1)S(1)} %add.555), channel_id=1, source_target_pairs={{1,0},{2,1},{3,2},{5,4},{6,5},{7,6},{9,8},{10,9},{11,10},{13,12},{... | collective-permute-start | bytes 1572872 | tf_op jit(solution)/shard_map/ppermute | solution.py:745
  147.8 12.3 %collective-permute-start.20 = (bf16[128,2048]{1,0:T(8,128)(2,1)S(1)}, bf16[128,2048]{1,0:T(8,128)(2,1)S(1)}, u32[]{:S(2)}, u32[]{:S(2)}) collective-permute-start(bf16[128,2048]{1,0:T(8,128)(2,1)S(1)} %add.565), channel_id=1, source_target_pairs={{3,2},{1,0},{2,1},{7,6},{5,4},{6,5},{11,10},{9,8},{10,9},{15,14},{... | collective-permute-start | bytes 1572872 | tf_op jit(solution)/shard_map/ppermute | solution.py:745
  149.1 12.1 %collective-permute-start.19 = (bf16[128,2048]{1,0:T(8,128)(2,1)S(1)}, bf16[128,2048]{1,0:T(8,128)(2,1)S(1)}, u32[]{:S(2)}, u32[]{:S(2)}) collective-permute-start(bf16[128,2048]{1,0:T(8,128)(2,1)S(1)} %add.564), channel_id=1, source_target_pairs={{0,1},{2,3},{1,2},{4,5},{6,7},{5,6},{8,9},{10,11},{9,10},{12,13},{... | collective-permute-start | bytes 1572872 | tf_op jit(solution)/shard_map/ppermute | solution.py:744
  163.2 11.4 %collective-permute-start.21 = (bf16[128,2048]{1,0:T(8,128)(2,1)S(1)}, bf16[128,2048]{1,0:T(8,128)(2,1)S(1)}, u32[]{:S(2)}, u32[]{:S(2)}) collective-permute-start(bf16[128,2048]{1,0:T(8,128)(2,1)S(1)} %add.566), channel_id=1, source_target_pairs={{1,2},{0,1},{2,3},{5,6},{4,5},{6,7},{9,10},{8,9},{10,11},{13,14},{... | collective-permute-start | bytes 1572872 | tf_op jit(solution)/shard_map/ppermute | solution.py:744
  167.9 12.0 %collective-permute-start.22 = (bf16[128,2048]{1,0:T(8,128)(2,1)S(1)}, bf16[128,2048]{1,0:T(8,128)(2,1)S(1)}, u32[]{:S(2)}, u32[]{:S(2)}) collective-permute-start(bf16[128,2048]{1,0:T(8,128)(2,1)S(1)} %add.567), channel_id=1, source_target_pairs={{2,1},{3,2},{1,0},{6,5},{7,6},{5,4},{10,9},{11,10},{9,8},{14,13},{... | collective-permute-start | bytes 1572872 | tf_op jit(solution)/shard_map/ppermute | solution.py:745
  181.3 11.2 %collective-permute-start.23 = (bf16[128,2048]{1,0:T(8,128)(2,1)S(1)}, bf16[128,2048]{1,0:T(8,128)(2,1)S(1)}, u32[]{:S(2)}, u32[]{:S(2)}) collective-permute-start(bf16[128,2048]{1,0:T(8,128)(2,1)S(1)} %add.576), channel_id=1, source_target_pairs={{2,3},{1,2},{0,1},{6,7},{5,6},{4,5},{10,11},{9,10},{8,9},{14,15},{... | collective-permute-start | bytes 1572872 | tf_op jit(solution)/shard_map/ppermute | solution.py:744
  194.0 27.6 %collective-permute-start.26 = (bf16[128,2048]{1,0:T(8,128)(2,1)}, bf16[128,2048]{1,0:T(8,128)(2,1)}, u32[]{:S(2)}, u32[]{:S(2)}) collective-permute-start(bf16[128,2048]{1,0:T(8,128)(2,1)} %get-tuple-element.448), channel_id=1, source_target_pairs={{1,0},{2,1},{3,2},{5,4},{6,5},{7,6},{9,8},{10,9},{11,10},{13,12},{... | collective-permute-start | bytes 1572872 | tf_op jit(solution)/shard_map/ppermute | solution.py:745
  195.3 26.4 %collective-permute-start.25 = (bf16[128,2048]{1,0:T(8,128)(2,1)}, bf16[128,2048]{1,0:T(8,128)(2,1)}, u32[]{:S(2)}, u32[]{:S(2)}) collective-permute-start(bf16[128,2048]{1,0:T(8,128)(2,1)} %get-tuple-element.446), channel_id=1, source_target_pairs={{2,3},{1,2},{0,1},{6,7},{5,6},{4,5},{10,11},{9,10},{8,9},{14,15},{... | collective-permute-start | bytes 1572872 | tf_op jit(solution)/shard_map/ppermute | solution.py:744
  224.4 31.3 %collective-permute-start.28 = (bf16[128,2048]{1,0:T(8,128)(2,1)}, bf16[128,2048]{1,0:T(8,128)(2,1)}, u32[]{:S(2)}, u32[]{:S(2)}) collective-permute-start(bf16[128,2048]{1,0:T(8,128)(2,1)} %get-tuple-element.462), channel_id=1, source_target_pairs={{3,2},{1,0},{2,1},{7,6},{5,4},{6,5},{11,10},{9,8},{10,9},{15,14},{... | collective-permute-start | bytes 1572872 | tf_op jit(solution)/shard_map/ppermute | solution.py:745
  225.7 30.0 %collective-permute-start.27 = (bf16[128,2048]{1,0:T(8,128)(2,1)}, bf16[128,2048]{1,0:T(8,128)(2,1)}, u32[]{:S(2)}, u32[]{:S(2)}) collective-permute-start(bf16[128,2048]{1,0:T(8,128)(2,1)} %get-tuple-element.460), channel_id=1, source_target_pairs={{0,1},{2,3},{1,2},{4,5},{6,7},{5,6},{8,9},{10,11},{9,10},{12,13},{... | collective-permute-start | bytes 1572872 | tf_op jit(solution)/shard_map/ppermute | solution.py:744
  255.7 238.6 %reduce-scatter.5.cloned.1.call-start = ((), (), s32[]{:S(2)}) async-start(), calls=%async_computation.6 | async-start | bytes 9437184 | tf_op jit(solution)/shard_map/reduce_scatter | solution.py:593
  257.9 35.6 %collective-permute-start.30 = (bf16[128,2048]{1,0:T(8,128)(2,1)S(1)}, bf16[128,2048]{1,0:T(8,128)(2,1)S(1)}, u32[]{:S(2)}, u32[]{:S(2)}) collective-permute-start(bf16[128,2048]{1,0:T(8,128)(2,1)S(1)} %get-tuple-element.474), channel_id=1, source_target_pairs={{2,1},{3,2},{1,0},{6,5},{7,6},{5,4},{10,9},{11,10},{9,8},{14,13},{... | collective-permute-start | bytes 1572872 | tf_op jit(solution)/shard_map/ppermute | solution.py:745
  259.2 34.3 %collective-permute-start.29 = (bf16[128,2048]{1,0:T(8,128)(2,1)S(1)}, bf16[128,2048]{1,0:T(8,128)(2,1)S(1)}, u32[]{:S(2)}, u32[]{:S(2)}) collective-permute-start(bf16[128,2048]{1,0:T(8,128)(2,1)S(1)} %get-tuple-element.472), channel_id=1, source_target_pairs={{1,2},{0,1},{2,3},{5,6},{4,5},{6,7},{9,10},{8,9},{10,11},{13,14},{... | collective-permute-start | bytes 1572872 | tf_op jit(solution)/shard_map/ppermute | solution.py:744
  293.9 23.9 %collective-permute-start.31 = (bf16[128,2048]{1,0:T(8,128)(2,1)S(1)}, bf16[128,2048]{1,0:T(8,128)(2,1)S(1)}, u32[]{:S(2)}, u32[]{:S(2)}) collective-permute-start(bf16[128,2048]{1,0:T(8,128)(2,1)S(1)} %get-tuple-element.484), channel_id=1, source_target_pairs={{2,3},{1,2},{0,1},{6,7},{5,6},{4,5},{10,11},{9,10},{8,9},{14,15},{... | collective-permute-start | bytes 1572872 | tf_op jit(solution)/shard_map/ppermute | solution.py:744
  297.3 21.4 %collective-permute-start.32 = (bf16[128,2048]{1,0:T(8,128)(2,1)S(1)}, bf16[128,2048]{1,0:T(8,128)(2,1)S(1)}, u32[]{:S(2)}, u32[]{:S(2)}) collective-permute-start(bf16[128,2048]{1,0:T(8,128)(2,1)S(1)} %get-tuple-element.486), channel_id=1, source_target_pairs={{1,0},{2,1},{3,2},{5,4},{6,5},{7,6},{9,8},{10,9},{11,10},{13,12},{... | collective-permute-start | bytes 1572872 | tf_op jit(solution)/shard_map/ppermute | solution.py:745
  320.8 31.5 %collective-permute-start.33 = (bf16[128,2048]{1,0:T(8,128)(2,1)}, bf16[128,2048]{1,0:T(8,128)(2,1)}, u32[]{:S(2)}, u32[]{:S(2)}) collective-permute-start(bf16[128,2048]{1,0:T(8,128)(2,1)} %add.586), channel_id=1, source_target_pairs={{2,3},{1,2},{0,1},{6,7},{5,6},{4,5},{10,11},{9,10},{8,9},{14,15},{... | collective-permute-start | bytes 1572872 | tf_op jit(solution)/shard_map/ppermute | solution.py:744
  332.3 34.4 %collective-permute-start.34 = (bf16[128,2048]{1,0:T(8,128)(2,1)}, bf16[128,2048]{1,0:T(8,128)(2,1)}, u32[]{:S(2)}, u32[]{:S(2)}) collective-permute-start(bf16[128,2048]{1,0:T(8,128)(2,1)} %add.587), channel_id=1, source_target_pairs={{1,0},{2,1},{3,2},{5,4},{6,5},{7,6},{9,8},{10,9},{11,10},{13,12},{... | collective-permute-start | bytes 1572872 | tf_op jit(solution)/shard_map/ppermute | solution.py:745
  368.7 218.4 %reduce-scatter.7.cloned.1.call-start = ((), (), s32[]{:S(2)}) async-start(), calls=%async_computation.7 | async-start | bytes 9437184 | tf_op jit(solution)/shard_map/reduce_scatter | solution.py:593
  368.8 24.4 %collective-permute-start.35 = (bf16[128,2048]{1,0:T(8,128)(2,1)}, bf16[128,2048]{1,0:T(8,128)(2,1)}, u32[]{:S(2)}, u32[]{:S(2)}) collective-permute-start(bf16[128,2048]{1,0:T(8,128)(2,1)} %add.591), channel_id=1, source_target_pairs={{0,1},{2,3},{1,2},{4,5},{6,7},{5,6},{8,9},{10,11},{9,10},{12,13},{... | collective-permute-start | bytes 1572872 | tf_op jit(solution)/shard_map/ppermute | solution.py:744
  371.8 23.5 %collective-permute-start.36 = (bf16[128,2048]{1,0:T(8,128)(2,1)}, bf16[128,2048]{1,0:T(8,128)(2,1)}, u32[]{:S(2)}, u32[]{:S(2)}) collective-permute-start(bf16[128,2048]{1,0:T(8,128)(2,1)} %add.592), channel_id=1, source_target_pairs={{3,2},{1,0},{2,1},{7,6},{5,4},{6,5},{11,10},{9,8},{10,9},{15,14},{... | collective-permute-start | bytes 1572872 | tf_op jit(solution)/shard_map/ppermute | solution.py:745
  397.2 258.6 %reduce-scatter.9.cloned.1.call-start = ((), (), s32[]{:S(2)}) async-start(), calls=%async_computation.8 | async-start | bytes 9437184 | tf_op jit(solution)/shard_map/reduce_scatter | solution.py:593
  402.6 24.5 %collective-permute-start.37 = (bf16[128,2048]{1,0:T(8,128)(2,1)}, bf16[128,2048]{1,0:T(8,128)(2,1)}, u32[]{:S(2)}, u32[]{:S(2)}) collective-permute-start(bf16[128,2048]{1,0:T(8,128)(2,1)} %add.596), channel_id=1, source_target_pairs={{1,2},{0,1},{2,3},{5,6},{4,5},{6,7},{9,10},{8,9},{10,11},{13,14},{... | collective-permute-start | bytes 1572872 | tf_op jit(solution)/shard_map/ppermute | solution.py:744
  408.0 21.2 %collective-permute-start.38 = (bf16[128,2048]{1,0:T(8,128)(2,1)}, bf16[128,2048]{1,0:T(8,128)(2,1)}, u32[]{:S(2)}, u32[]{:S(2)}) collective-permute-start(bf16[128,2048]{1,0:T(8,128)(2,1)} %add.597), channel_id=1, source_target_pairs={{2,1},{3,2},{1,0},{6,5},{7,6},{5,4},{10,9},{11,10},{9,8},{14,13},{... | collective-permute-start | bytes 1572872 | tf_op jit(solution)/shard_map/ppermute | solution.py:745
  431.3 12.8 %collective-permute-start.40 = (bf16[128,2048]{1,0:T(8,128)(2,1)}, bf16[128,2048]{1,0:T(8,128)(2,1)}, u32[]{:S(2)}, u32[]{:S(2)}) collective-permute-start(bf16[128,2048]{1,0:T(8,128)(2,1)} %add.602), channel_id=1, source_target_pairs={{1,0},{2,1},{3,2},{5,4},{6,5},{7,6},{9,8},{10,9},{11,10},{13,12},{... | collective-permute-start | bytes 1572872 | tf_op jit(solution)/shard_map/ppermute | solution.py:745
  432.6 11.9 %collective-permute-start.39 = (bf16[128,2048]{1,0:T(8,128)(2,1)}, bf16[128,2048]{1,0:T(8,128)(2,1)}, u32[]{:S(2)}, u32[]{:S(2)}) collective-permute-start(bf16[128,2048]{1,0:T(8,128)(2,1)} %add.601), channel_id=1, source_target_pairs={{2,3},{1,2},{0,1},{6,7},{5,6},{4,5},{10,11},{9,10},{8,9},{14,15},{... | collective-permute-start | bytes 1572872 | tf_op jit(solution)/shard_map/ppermute | solution.py:744
  444.0 268.5 %reduce-scatter.11.cloned.1.call-start = ((), (), s32[]{:S(2)}) async-start(), calls=%async_computation.9 | async-start | bytes 9437184 | tf_op jit(solution)/shard_map/reduce_scatter | solution.py:593
  446.8 11.9 %collective-permute-start.42 = (bf16[128,2048]{1,0:T(8,128)(2,1)S(1)}, bf16[128,2048]{1,0:T(8,128)(2,1)S(1)}, u32[]{:S(2)}, u32[]{:S(2)}) collective-permute-start(bf16[128,2048]{1,0:T(8,128)(2,1)S(1)} %get-tuple-element.565), channel_id=1, source_target_pairs={{1,0},{2,1},{3,2},{5,4},{6,5},{7,6},{9,8},{10,9},{11,10},{13,12},{... | collective-permute-start | bytes 1572872 | tf_op jit(solution)/shard_map/ppermute | solution.py:745
  448.3 11.8 %collective-permute-start.41 = (bf16[128,2048]{1,0:T(8,128)(2,1)S(1)}, bf16[128,2048]{1,0:T(8,128)(2,1)S(1)}, u32[]{:S(2)}, u32[]{:S(2)}) collective-permute-start(bf16[128,2048]{1,0:T(8,128)(2,1)S(1)} %get-tuple-element.563), channel_id=1, source_target_pairs={{2,3},{1,2},{0,1},{6,7},{5,6},{4,5},{10,11},{9,10},{8,9},{14,15},{... | collective-permute-start | bytes 1572872 | tf_op jit(solution)/shard_map/ppermute | solution.py:744
  454.5 58.5 %collective-permute-start.49 = (f32[3,512]{1,0:T(4,128)S(1)}, f32[3,512]{1,0:T(4,128)S(1)}, u32[]{:S(2)}, u32[]{:S(2)}) collective-permute-start(f32[3,512]{1,0:T(4,128)S(1)} %pad_maximum_fusion.33), channel_id=1, source_target_pairs={{4,0},{8,4},{12,8},{16,12},{20,16},{24,20},{28,24},{5,1},{9,5},{13... | collective-permute-start | bytes 18440 | tf_op jit(solution)/shard_map/ppermute | solution.py:45
  460.6 14.9 %collective-permute-start.44 = (bf16[128,2048]{1,0:T(8,128)(2,1)S(1)}, bf16[128,2048]{1,0:T(8,128)(2,1)S(1)}, u32[]{:S(2)}, u32[]{:S(2)}) collective-permute-start(bf16[128,2048]{1,0:T(8,128)(2,1)S(1)} %get-tuple-element.582), channel_id=1, source_target_pairs={{1,0},{2,1},{3,2},{5,4},{6,5},{7,6},{9,8},{10,9},{11,10},{13,12},{... | collective-permute-start | bytes 1572872 | tf_op jit(solution)/shard_map/ppermute | solution.py:745
  462.1 14.8 %collective-permute-start.43 = (bf16[128,2048]{1,0:T(8,128)(2,1)S(1)}, bf16[128,2048]{1,0:T(8,128)(2,1)S(1)}, u32[]{:S(2)}, u32[]{:S(2)}) collective-permute-start(bf16[128,2048]{1,0:T(8,128)(2,1)S(1)} %get-tuple-element.580), channel_id=1, source_target_pairs={{2,3},{1,2},{0,1},{6,7},{5,6},{4,5},{10,11},{9,10},{8,9},{14,15},{... | collective-permute-start | bytes 1572872 | tf_op jit(solution)/shard_map/ppermute | solution.py:744
  477.3 14.7 %collective-permute-start.46 = (bf16[128,2048]{1,0:T(8,128)(2,1)S(1)}, bf16[128,2048]{1,0:T(8,128)(2,1)S(1)}, u32[]{:S(2)}, u32[]{:S(2)}) collective-permute-start(bf16[128,2048]{1,0:T(8,128)(2,1)S(1)} %get-tuple-element.598), channel_id=1, source_target_pairs={{3,2},{1,0},{2,1},{7,6},{5,4},{6,5},{11,10},{9,8},{10,9},{15,14},{... | collective-permute-start | bytes 1572872 | tf_op jit(solution)/shard_map/ppermute | solution.py:745
  478.6 13.4 %collective-permute-start.45 = (bf16[128,2048]{1,0:T(8,128)(2,1)S(1)}, bf16[128,2048]{1,0:T(8,128)(2,1)S(1)}, u32[]{:S(2)}, u32[]{:S(2)}) collective-permute-start(bf16[128,2048]{1,0:T(8,128)(2,1)S(1)} %get-tuple-element.596), channel_id=1, source_target_pairs={{0,1},{2,3},{1,2},{4,5},{6,7},{5,6},{8,9},{10,11},{9,10},{12,13},{... | collective-permute-start | bytes 1572872 | tf_op jit(solution)/shard_map/ppermute | solution.py:744
  497.4 12.4 %collective-permute-start.47 = (bf16[128,2048]{1,0:T(8,128)(2,1)S(1)}, bf16[128,2048]{1,0:T(8,128)(2,1)S(1)}, u32[]{:S(2)}, u32[]{:S(2)}) collective-permute-start(bf16[128,2048]{1,0:T(8,128)(2,1)S(1)} %copy-done.191), channel_id=1, source_target_pairs={{1,2},{0,1},{2,3},{5,6},{4,5},{6,7},{9,10},{8,9},{10,11},{13,14},{... | collective-permute-start | bytes 1572872 | tf_op jit(solution)/shard_map/ppermute | solution.py:744
  534.1 28.8 %collective-permute-start.52 = (bf16[128,2048]{1,0:T(8,128)(2,1)}, bf16[128,2048]{1,0:T(8,128)(2,1)}, u32[]{:S(2)}, u32[]{:S(2)}) collective-permute-start(bf16[128,2048]{1,0:T(8,128)(2,1)} %add.628), channel_id=1, source_target_pairs={{2,3},{1,2},{0,1},{6,7},{5,6},{4,5},{10,11},{9,10},{8,9},{14,15},{... | collective-permute-start | bytes 1572872 | tf_op jit(solution)/shard_map/ppermute | solution.py:744
  538.7 26.5 %collective-permute-start.53 = (bf16[128,2048]{1,0:T(8,128)(2,1)}, bf16[128,2048]{1,0:T(8,128)(2,1)}, u32[]{:S(2)}, u32[]{:S(2)}) collective-permute-start(bf16[128,2048]{1,0:T(8,128)(2,1)} %add.629), channel_id=1, source_target_pairs={{1,0},{2,1},{3,2},{5,4},{6,5},{7,6},{9,8},{10,9},{11,10},{13,12},{... | collective-permute-start | bytes 1572872 | tf_op jit(solution)/shard_map/ppermute | solution.py:745
  568.3 14.1 %collective-permute-start.54 = (bf16[128,2048]{1,0:T(8,128)(2,1)}, bf16[128,2048]{1,0:T(8,128)(2,1)}, u32[]{:S(2)}, u32[]{:S(2)}) collective-permute-start(bf16[128,2048]{1,0:T(8,128)(2,1)} %add.633), channel_id=1, source_target_pairs={{2,3},{1,2},{0,1},{6,7},{5,6},{4,5},{10,11},{9,10},{8,9},{14,15},{... | collective-permute-start | bytes 1572872 | tf_op jit(solution)/shard_map/ppermute | solution.py:744
  573.7 11.4 %collective-permute-start.55 = (bf16[128,2048]{1,0:T(8,128)(2,1)}, bf16[128,2048]{1,0:T(8,128)(2,1)}, u32[]{:S(2)}, u32[]{:S(2)}) collective-permute-start(bf16[128,2048]{1,0:T(8,128)(2,1)} %add.634), channel_id=1, source_target_pairs={{1,0},{2,1},{3,2},{5,4},{6,5},{7,6},{9,8},{10,9},{11,10},{13,12},{... | collective-permute-start | bytes 1572872 | tf_op jit(solution)/shard_map/ppermute | solution.py:745
  590.9 11.3 %collective-permute-start.57 = (bf16[128,2048]{1,0:T(8,128)(2,1)}, bf16[128,2048]{1,0:T(8,128)(2,1)S(1)}, u32[]{:S(2)}, u32[]{:S(2)}) collective-permute-start(bf16[128,2048]{1,0:T(8,128)(2,1)} %add.641), channel_id=1, source_target_pairs={{3,2},{1,0},{2,1},{7,6},{5,4},{6,5},{11,10},{9,8},{10,9},{15,14},{... | collective-permute-start | bytes 1572872 | tf_op jit(solution)/shard_map/ppermute | solution.py:745
  609.4 11.6 %collective-permute-start.58 = (bf16[128,2048]{1,0:T(8,128)(2,1)}, bf16[128,2048]{1,0:T(8,128)(2,1)}, u32[]{:S(2)}, u32[]{:S(2)}) collective-permute-start(bf16[128,2048]{1,0:T(8,128)(2,1)} %add.648), channel_id=1, source_target_pairs={{1,2},{0,1},{2,3},{5,6},{4,5},{6,7},{9,10},{8,9},{10,11},{13,14},{... | collective-permute-start | bytes 1572872 | tf_op jit(solution)/shard_map/ppermute | solution.py:744
  611.8 13.2 %collective-permute-start.59 = (bf16[128,2048]{1,0:T(8,128)(2,1)}, bf16[128,2048]{1,0:T(8,128)(2,1)}, u32[]{:S(2)}, u32[]{:S(2)}) collective-permute-start(bf16[128,2048]{1,0:T(8,128)(2,1)} %add.649), channel_id=1, source_target_pairs={{2,1},{3,2},{1,0},{6,5},{7,6},{5,4},{10,9},{11,10},{9,8},{14,13},{... | collective-permute-start | bytes 1572872 | tf_op jit(solution)/shard_map/ppermute | solution.py:745
  627.4 11.2 %collective-permute-start.60 = (bf16[128,2048]{1,0:T(8,128)(2,1)S(1)}, bf16[128,2048]{1,0:T(8,128)(2,1)S(1)}, u32[]{:S(2)}, u32[]{:S(2)}) collective-permute-start(bf16[128,2048]{1,0:T(8,128)(2,1)S(1)} %add.655), channel_id=1, source_target_pairs={{2,3},{1,2},{0,1},{6,7},{5,6},{4,5},{10,11},{9,10},{8,9},{14,15},{... | collective-permute-start | bytes 1572872 | tf_op jit(solution)/shard_map/ppermute | solution.py:744
  639.1 14.3 %collective-permute-start.64 = (bf16[128,2048]{1,0:T(8,128)(2,1)S(1)}, bf16[128,2048]{1,0:T(8,128)(2,1)S(1)}, u32[]{:S(2)}, u32[]{:S(2)}) collective-permute-start(bf16[128,2048]{1,0:T(8,128)(2,1)S(1)} %get-tuple-element.723), channel_id=1, source_target_pairs={{1,0},{2,1},{3,2},{5,4},{6,5},{7,6},{9,8},{10,9},{11,10},{13,12},{... | collective-permute-start | bytes 1572872 | tf_op jit(solution)/shard_map/ppermute | solution.py:745
  640.4 13.0 %collective-permute-start.63 = (bf16[128,2048]{1,0:T(8,128)(2,1)S(1)}, bf16[128,2048]{1,0:T(8,128)(2,1)S(1)}, u32[]{:S(2)}, u32[]{:S(2)}) collective-permute-start(bf16[128,2048]{1,0:T(8,128)(2,1)S(1)} %get-tuple-element.721), channel_id=1, source_target_pairs={{2,3},{1,2},{0,1},{6,7},{5,6},{4,5},{10,11},{9,10},{8,9},{14,15},{... | collective-permute-start | bytes 1572872 | tf_op jit(solution)/shard_map/ppermute | solution.py:744
  655.8 13.5 %collective-permute-start.67 = (bf16[128,2048]{1,0:T(8,128)(2,1)}, bf16[128,2048]{1,0:T(8,128)(2,1)S(1)}, u32[]{:S(2)}, u32[]{:S(2)}) collective-permute-start(bf16[128,2048]{1,0:T(8,128)(2,1)} %get-tuple-element.729), channel_id=1, source_target_pairs={{1,0},{2,1},{3,2},{5,4},{6,5},{7,6},{9,8},{10,9},{11,10},{13,12},{... | collective-permute-start | bytes 1572872 | tf_op jit(solution)/shard_map/ppermute | solution.py:745
  657.2 15.3 %collective-permute-start.66 = (bf16[128,2048]{1,0:T(8,128)(2,1)}, bf16[128,2048]{1,0:T(8,128)(2,1)S(1)}, u32[]{:S(2)}, u32[]{:S(2)}) collective-permute-start(bf16[128,2048]{1,0:T(8,128)(2,1)} %get-tuple-element.727), channel_id=1, source_target_pairs={{2,3},{1,2},{0,1},{6,7},{5,6},{4,5},{10,11},{9,10},{8,9},{14,15},{... | collective-permute-start | bytes 1572872 | tf_op jit(solution)/shard_map/ppermute | solution.py:744
  673.0 19.2 %collective-permute-start.69 = (bf16[128,2048]{1,0:T(8,128)(2,1)S(1)}, bf16[128,2048]{1,0:T(8,128)(2,1)S(1)}, u32[]{:S(2)}, u32[]{:S(2)}) collective-permute-start(bf16[128,2048]{1,0:T(8,128)(2,1)S(1)} %get-tuple-element.734), channel_id=1, source_target_pairs={{2,3},{1,2},{0,1},{6,7},{5,6},{4,5},{10,11},{9,10},{8,9},{14,15},{... | collective-permute-start | bytes 1572872 | tf_op jit(solution)/shard_map/ppermute | solution.py:744
  677.6 14.7 %collective-permute-start.70 = (bf16[128,2048]{1,0:T(8,128)(2,1)S(1)}, bf16[128,2048]{1,0:T(8,128)(2,1)S(1)}, u32[]{:S(2)}, u32[]{:S(2)}) collective-permute-start(bf16[128,2048]{1,0:T(8,128)(2,1)S(1)} %get-tuple-element.735), channel_id=1, source_target_pairs={{1,0},{2,1},{3,2},{5,4},{6,5},{7,6},{9,8},{10,9},{11,10},{13,12},{... | collective-permute-start | bytes 1572872 | tf_op jit(solution)/shard_map/ppermute | solution.py:745
  678.9 13.3 %collective-permute-start.71 = (f32[8,512]{1,0:T(8,128)S(1)}, f32[8,512]{1,0:T(8,128)S(1)}, u32[]{:S(2)}, u32[]{:S(2)}) collective-permute-start(f32[8,512]{1,0:T(8,128)S(1)} %slice.873), channel_id=1, source_target_pairs={{0,1},{1,0},{2,3},{3,2},{4,5},{5,4},{6,7},{7,6},{8,9},{9,8},{10,11... | collective-permute-start | bytes 49160 | tf_op jit(solution)/shard_map/ppermute | solution.py:54
  692.6 16.2 %collective-permute-start.72 = (bf16[128,2048]{1,0:T(8,128)(2,1)S(1)}, bf16[128,2048]{1,0:T(8,128)(2,1)}, u32[]{:S(2)}, u32[]{:S(2)}) collective-permute-start(bf16[128,2048]{1,0:T(8,128)(2,1)S(1)} %collective-permute-done.69), channel_id=1, source_target_pairs={{2,3},{1,2},{6,7},{5,6},{10,11},{9,10},{14,15},{13,14},{18,19},{17... | collective-permute-start | bytes 1572872 | tf_op jit(solution)/shard_map/ppermute | solution.py:744
  694.2 15.7 %collective-permute-start.73 = (bf16[128,2048]{1,0:T(8,128)(2,1)S(1)}, bf16[128,2048]{1,0:T(8,128)(2,1)}, u32[]{:S(2)}, u32[]{:S(2)}) collective-permute-start(bf16[128,2048]{1,0:T(8,128)(2,1)S(1)} %collective-permute-done.70), channel_id=1, source_target_pairs={{1,0},{2,1},{5,4},{6,5},{9,8},{10,9},{13,12},{14,13},{17,16},{18,1... | collective-permute-start | bytes 1572872 | tf_op jit(solution)/shard_map/ppermute | solution.py:745
  695.5 13.2 %collective-permute-start.74 = (f32[8,512]{1,0:T(8,128)S(1)}, f32[8,512]{1,0:T(8,128)S(1)}, u32[]{:S(2)}, u32[]{:S(2)}) collective-permute-start(f32[8,512]{1,0:T(8,128)S(1)} %slice.875), channel_id=1, source_target_pairs={{0,2},{1,3},{2,0},{3,1},{4,6},{5,7},{6,4},{7,5},{8,10},{9,11},{10,... | collective-permute-start | bytes 49160 | tf_op jit(solution)/shard_map/ppermute | solution.py:54
  712.4 11.5 %collective-permute-start.75 = (bf16[128,2048]{1,0:T(8,128)(2,1)}, bf16[128,2048]{1,0:T(8,128)(2,1)}, u32[]{:S(2)}, u32[]{:S(2)}) collective-permute-start(bf16[128,2048]{1,0:T(8,128)(2,1)} %collective-permute-done.73), channel_id=1, source_target_pairs={{1,0},{5,4},{9,8},{13,12},{17,16},{21,20},{25,24},{29,28}} | collective-permute-start | bytes 1572872 | tf_op jit(solution)/shard_map/ppermute | solution.py:745
  (248 other events, 2367.7 us)
Sparse Core Ops, SparseCore 0:
  10.5 51.0 all-gather.3
  64.0 125.7 all-gather.5
  255.8 108.9 all-reduce.3
  368.8 75.3 reduce-scatter.4
  448.1 71.2 reduce-scatter.6
  523.1 71.2 reduce-scatter.8
  597.9 72.3 reduce-scatter.10
